TPU v7x, 512 devices: a whole 4x8x8 slice. The times are simulated.
512 devices in a mesh: ta: 128 (over y_hi, x, z), gz: 4 (over y_lo, core).
Axes of the slice: x: 4, y: 8 (y_hi: 4, y_lo: 2; y = y_hi * 2 + y_lo), z: 8, core: 2. Of those that a mesh axis runs over, the one named last changes fastest.
Arguments:
- source: bfloat16 [128, 8, 4, 4, 64, 128], P('ta', 'gz'), may hold values from -6 to 6
- self_codes: bfloat16 [128, 8, 4, 4, 64, 64], P('ta', 'gz'), may hold values from -6 to 6
- hop_codes: bfloat16 [128, 8, 4, 4, 64, 256], P('ta', 'gz'), may hold values from -6 to 6
- link_scales: bfloat16 [128, 8, 4, 4, 5], P('ta', 'gz'), may hold values from 0.019897461 to 0.079589844
- restrict_map: int32 [128, 8, 4, 4], P('ta', 'gz'), may hold values from 0 to 15
- restrictor: bfloat16 [128, 8, 4, 4, 64, 64], P('ta', 'gz'), may hold values from -0.75 to 0.75
Outputs:
- smoothed: bfloat16 [128, 8, 4, 4, 64, 128], P('ta', 'gz')
- coarse: float32 [128, 16, 64, 128], P('ta', 'gz')
All inputs are finite; a program needn't handle non-finite values.
Results may differ from a plain program's by a relative error of at most 0.0041.
Values may be sent and summed in bfloat16 or wider, within the bound.
No kernel may reach another device: no remote copies, remote signals or barrier semaphores. Data moves between devices by JAX's collectives and lax.ppermute only.
A program may use at most 64 MiB of HBM per device.

v0:
```python
import jax
import jax.numpy as jnp
from jax import lax
from jax.sharding import PartitionSpec as P

ITERS = 3
AGG_DEV = 4


OMEGA = 0.5


def shifted(block, axis, distance):
    devices = range(lax.axis_size(axis))
    route = [((i - distance) % len(devices), i) for i in devices]
    return lax.ppermute(block, axis, route)


def local_mult(codes, vector):
    return jnp.einsum("tzxyab,tzxybr->tzxyar", codes, vector, preferred_element_type=jnp.float32)


def local_mult_transposed(codes, vector):
    return jnp.einsum("tzxyab,tzxyar->tzxybr", codes, vector, preferred_element_type=jnp.float32)


def shards(source, self_codes, hop_codes, link_scales, restrict_map, restrictor):
    degrees = source.shape[4]
    blocks = [
        hop_codes[..., direction * degrees : (direction + 1) * degrees] for direction in range(4)
    ]
    scales = link_scales.astype(jnp.float32)
    factors = [scales[..., direction][..., None, None] for direction in range(5)]
    source_float = source.astype(jnp.float32)
    estimate = source_float
    vector_field = source
    for iteration in range(ITERS):
        result = vector_field.astype(jnp.float32) + factors[0] * local_mult(
            self_codes, vector_field
        )
        arrived = shifted(vector_field, "ta", -1)
        t_next = jnp.concatenate([vector_field[1:], arrived], axis=0)
        z_arrived = shifted(vector_field[:, :1], "gz", -1)
        z_next = jnp.concatenate([vector_field[:, 1:], z_arrived], axis=1)
        neighbours = [jnp.roll(vector_field, -1, 2), jnp.roll(vector_field, -1, 3), z_next, t_next]
        for operate_direction in range(4):
            result = result + factors[operate_direction + 1] * local_mult(
                blocks[operate_direction], neighbours[operate_direction]
            )
        for operate_direction in range(2):
            behind_term = (
                factors[operate_direction + 1]
                * local_mult_transposed(blocks[operate_direction], vector_field)
            ).astype(jnp.bfloat16)
            result = result + jnp.roll(behind_term, 1, axis=2 + operate_direction).astype(
                jnp.float32
            )
        z_terms = (factors[3] * local_mult_transposed(blocks[2], vector_field)).astype(jnp.bfloat16)
        z_from = shifted(z_terms[:, -1:], "gz", 1)
        result = result + jnp.concatenate([z_from, z_terms[:, :-1]], axis=1).astype(jnp.float32)
        t_terms = (factors[4] * local_mult_transposed(blocks[3], vector_field)).astype(jnp.bfloat16)
        t_from = shifted(t_terms, "ta", 1)
        t_incoming = jnp.concatenate([t_from, t_terms[:-1]], axis=0)
        applied = result + t_incoming.astype(jnp.float32)
        estimate = estimate + OMEGA * (source_float - applied)
        vector_field = estimate.astype(jnp.bfloat16)
    coarse_width = restrictor.shape[4]
    right_cols = source.shape[5]
    site_count = source.shape[0] * source.shape[1] * source.shape[2] * source.shape[3]
    projected = jnp.einsum(
        "tzxyca,tzxyar->tzxycr", restrictor, vector_field, preferred_element_type=jnp.float32
    )
    flattened = projected.reshape(site_count, coarse_width * right_cols)
    groups = AGG_DEV * lax.axis_size("gz")
    labels = restrict_map.reshape(site_count)
    onehot = (labels[None, :] == jnp.arange(groups, dtype=jnp.int32)[:, None]).astype(jnp.float32)
    partial_sums = jnp.dot(onehot, flattened, precision=lax.Precision.HIGHEST)
    summed = lax.psum(partial_sums, "gz")
    owned = lax.dynamic_slice_in_dim(summed, lax.axis_index("gz") * AGG_DEV, AGG_DEV, 0)
    return (vector_field, owned.reshape(1, AGG_DEV, coarse_width, right_cols))


def solution(mesh):
    placed = (
        P("ta", "gz", None, None, None, None),
        P("ta", "gz", None, None, None, None),
        P("ta", "gz", None, None, None, None),
        P("ta", "gz", None, None, None),
        P("ta", "gz", None, None),
        P("ta", "gz", None, None, None, None),
    )
    return jax.shard_map(
        shards,
        mesh=mesh,
        in_specs=placed,
        out_specs=(P("ta", "gz", None, None, None, None), P("ta", "gz", None, None)),
        check_vma=False,
    )
```

profile of v0, /device:TPU:1, one launch (start us, length us, event | category | flops | bytes accessed | tf_op | source)
XLA Modules:
  0.0 201.6 jit_solution(1051310907819398375)
XLA Ops:
  7.2 17.5 %collective-permute-start.1 = (bf16[1,2,4,4,64,128]{5,4,3,2,1,0:T(8,128)(2,1)}, bf16[1,2,4,4,64,128]{5,4,3,2,1,0:T(8,128)(2,1)}, u32[]{:S(2)}, u32[]{:S(2)}) collective-permute-start(bf16[1,2,4,4,64,128]{5,4,3,2,1,0:T(8,128)(2,1)} %param.6), channel_id=1, source_target_pairs={{4,0},{8,4},{12,8},{16,12},{20,16},{24,20},{28,24},{32,28},{36,32}... | collective-permute-start | bytes 1572872 | tf_op jit(solution)/shard_map/ppermute | solution.py:16
  24.8 0.7 convert_element_type.228
  25.5 0.2 slice_reduce_fusion.1
  25.7 1.6 fusion.66
  27.4 0.8 fusion.176
  28.1 3.1 %collective-permute-start.2 = (bf16[1,1,4,4,64,128]{5,4,3,2,1,0:T(8,128)(2,1)}, bf16[1,1,4,4,64,128]{5,4,3,2,1,0:T(8,128)(2,1)}, u32[]{:S(2)}, u32[]{:S(2)}) collective-permute-start(bf16[1,1,4,4,64,128]{5,4,3,2,1,0:T(8,128)(2,1)} %get-tuple-element.15), channel_id=1, source_target_pairs={{3,0},{0,1},{1,2},{2,3},{7,4},{4,5},{5,6},{6,7},{11,8},{8,9},{9,10... | collective-permute-start | bytes 786440 | tf_op jit(solution)/shard_map/ppermute | solution.py:16
  31.3 1.4 fusion.65
  32.7 1.9 collective-permute-start.3
  34.6 0.9 fusion.177
  35.5 1.9 collective-permute-start
  37.5 0.3 convert_add_fusion.1
  37.8 0.4 fusion.11
  38.1 0.4 fusion.68
  38.5 0.7 copy-done.4
  39.3 0.3 fusion.16
  39.6 0.6 fusion.67
  40.2 0.8 copy-done.6
  41.0 0.7 copy-done.12
  41.8 5.1 %collective-permute-done.1 = bf16[1,2,4,4,64,128]{5,4,3,2,1,0:T(8,128)(2,1)} collective-permute-done((bf16[1,2,4,4,64,128]{5,4,3,2,1,0:T(8,128)(2,1)}, bf16[1,2,4,4,64,128]{5,4,3,2,1,0:T(8,128)(2,1)}, u32[]{:S(2)}, u32[]{:S(2)}) %collective-permute-start.1) | collective-permute-done | bytes 524320 | tf_op jit(solution)/shard_map/ppermute | solution.py:16
  46.9 1.4 fusion.13
  48.3 5.4 %collective-permute-done = bf16[1,1,4,4,64,128]{5,4,3,2,1,0:T(8,128)(2,1)} collective-permute-done((bf16[1,1,4,4,64,128]{5,4,3,2,1,0:T(8,128)(2,1)}, bf16[1,1,4,4,64,128]{5,4,3,2,1,0:T(8,128)(2,1)}, u32[]{:S(2)}, u32[]{:S(2)}) %collective-permute-start) | collective-permute-done | bytes 262176 | tf_op jit(solution)/shard_map/ppermute | solution.py:16
  53.7 12.5 %collective-permute-done.3 = bf16[1,2,4,4,64,128]{5,4,3,2,1,0:T(8,128)(2,1)} collective-permute-done((bf16[1,2,4,4,64,128]{5,4,3,2,1,0:T(8,128)(2,1)}, bf16[1,2,4,4,64,128]{5,4,3,2,1,0:T(8,128)(2,1)}, u32[]{:S(2)}, u32[]{:S(2)}) %collective-permute-start.3) | collective-permute-done | bytes 524320 | tf_op jit(solution)/shard_map/ppermute | solution.py:16
  66.2 1.9 fusion.178
  68.2 1.9 collective-permute-start.5
  70.2 0.4 fusion.62
  70.5 0.6 fusion.61
  71.2 0.4 fusion.64
  71.5 0.8 copy-done.7
  72.4 2.1 %collective-permute-start.6 = (bf16[1,1,4,4,64,128]{5,4,3,2,1,0:T(8,128)(2,1)S(1)}, bf16[1,1,4,4,64,128]{5,4,3,2,1,0:T(8,128)(2,1)S(1)}, u32[]{:S(2)}, u32[]{:S(2)}) collective-permute-start(bf16[1,1,4,4,64,128]{5,4,3,2,1,0:T(8,128)(2,1)S(1)} %get-tuple-element.11), channel_id=1, source_target_pairs={{3,0},{0,1},{1,2},{2,3},{7,4},{4,5},{5,6},{6,7},{11,8},{8,9},{9,10... | collective-permute-start | bytes 786440 | tf_op jit(solution)/shard_map/ppermute | solution.py:16
  74.5 3.6 %collective-permute-start.7 = (bf16[1,2,4,4,64,128]{5,4,3,2,1,0:T(8,128)(2,1)S(1)}, bf16[1,2,4,4,64,128]{5,4,3,2,1,0:T(8,128)(2,1)S(1)}, u32[]{:S(2)}, u32[]{:S(2)}) collective-permute-start(bf16[1,2,4,4,64,128]{5,4,3,2,1,0:T(8,128)(2,1)S(1)} %fusion.61), channel_id=1, source_target_pairs={{508,0},{0,4},{4,8},{8,12},{12,16},{16,20},{20,24},{24,28},{28,32}... | collective-permute-start | bytes 1572872 | tf_op jit(solution)/shard_map/ppermute | solution.py:16
  78.1 2.8 %collective-permute-start.4 = (bf16[1,1,4,4,64,128]{5,4,3,2,1,0:T(8,128)(2,1)S(1)}, bf16[1,1,4,4,64,128]{5,4,3,2,1,0:T(8,128)(2,1)S(1)}, u32[]{:S(2)}, u32[]{:S(2)}) collective-permute-start(bf16[1,1,4,4,64,128]{5,4,3,2,1,0:T(8,128)(2,1)S(1)} %get-tuple-element.14), channel_id=1, source_target_pairs={{1,0},{2,1},{3,2},{0,3},{5,4},{6,5},{7,6},{4,7},{9,8},{10,9},{11,1... | collective-permute-start | bytes 786440 | tf_op jit(solution)/shard_map/ppermute | solution.py:16
  81.0 0.4 fusion.7
  81.3 0.3 fusion.9
  81.7 0.3 fusion.25
  82.0 0.6 fusion.63
  82.7 0.8 copy-done.8
  83.5 9.1 %collective-permute-done.5 = bf16[1,2,4,4,64,128]{5,4,3,2,1,0:T(8,128)(2,1)S(1)} collective-permute-done((bf16[1,2,4,4,64,128]{5,4,3,2,1,0:T(8,128)(2,1)S(1)}, bf16[1,2,4,4,64,128]{5,4,3,2,1,0:T(8,128)(2,1)S(1)}, u32[]{:S(2)}, u32[]{:S(2)}) %collective-permute-start.5) | collective-permute-done | bytes 524320 | tf_op jit(solution)/shard_map/ppermute | solution.py:16
  92.6 0.3 fusion.5
  93.0 10.9 %collective-permute-done.7 = bf16[1,2,4,4,64,128]{5,4,3,2,1,0:T(8,128)(2,1)S(1)} collective-permute-done((bf16[1,2,4,4,64,128]{5,4,3,2,1,0:T(8,128)(2,1)S(1)}, bf16[1,2,4,4,64,128]{5,4,3,2,1,0:T(8,128)(2,1)S(1)}, u32[]{:S(2)}, u32[]{:S(2)}) %collective-permute-start.7) | collective-permute-done | bytes 524320 | tf_op jit(solution)/shard_map/ppermute | solution.py:16
  103.9 0.7 fusion.179
  104.7 1.9 collective-permute-start.9
  106.7 0.4 fusion.58
  107.0 0.6 fusion.57
  107.7 0.4 fusion.60
  108.1 0.7 copy-done.3
  108.9 7.5 %collective-permute-start.10 = (bf16[1,1,4,4,64,128]{5,4,3,2,1,0:T(8,128)(2,1)S(1)}, bf16[1,1,4,4,64,128]{5,4,3,2,1,0:T(8,128)(2,1)S(1)}, u32[]{:S(2)}, u32[]{:S(2)}) collective-permute-start(bf16[1,1,4,4,64,128]{5,4,3,2,1,0:T(8,128)(2,1)S(1)} %get-tuple-element.7), channel_id=1, source_target_pairs={{3,0},{0,1},{1,2},{2,3},{7,4},{4,5},{5,6},{6,7},{11,8},{8,9},{9,10... | collective-permute-start | bytes 786440 | tf_op jit(solution)/shard_map/ppermute | solution.py:16
  116.4 3.6 %collective-permute-start.11 = (bf16[1,2,4,4,64,128]{5,4,3,2,1,0:T(8,128)(2,1)S(1)}, bf16[1,2,4,4,64,128]{5,4,3,2,1,0:T(8,128)(2,1)S(1)}, u32[]{:S(2)}, u32[]{:S(2)}) collective-permute-start(bf16[1,2,4,4,64,128]{5,4,3,2,1,0:T(8,128)(2,1)S(1)} %fusion.57), channel_id=1, source_target_pairs={{508,0},{0,4},{4,8},{8,12},{12,16},{16,20},{20,24},{24,28},{28,32}... | collective-permute-start | bytes 1572872 | tf_op jit(solution)/shard_map/ppermute | solution.py:16
  120.0 2.1 %collective-permute-start.8 = (bf16[1,1,4,4,64,128]{5,4,3,2,1,0:T(8,128)(2,1)S(1)}, bf16[1,1,4,4,64,128]{5,4,3,2,1,0:T(8,128)(2,1)S(1)}, u32[]{:S(2)}, u32[]{:S(2)}) collective-permute-start(bf16[1,1,4,4,64,128]{5,4,3,2,1,0:T(8,128)(2,1)S(1)} %get-tuple-element.10), channel_id=1, source_target_pairs={{1,0},{2,1},{3,2},{0,3},{5,4},{6,5},{7,6},{4,7},{9,8},{10,9},{11,1... | collective-permute-start | bytes 786440 | tf_op jit(solution)/shard_map/ppermute | solution.py:16
  122.1 0.4 fusion.2
  122.5 0.3 fusion.4
  122.8 0.4 fusion.35
  123.2 0.6 fusion.59
  123.9 0.8 copy-done.5
  124.7 0.4 fusion
  125.0 11.4 %collective-permute-done.8 = bf16[1,1,4,4,64,128]{5,4,3,2,1,0:T(8,128)(2,1)S(1)} collective-permute-done((bf16[1,1,4,4,64,128]{5,4,3,2,1,0:T(8,128)(2,1)S(1)}, bf16[1,1,4,4,64,128]{5,4,3,2,1,0:T(8,128)(2,1)S(1)}, u32[]{:S(2)}, u32[]{:S(2)}) %collective-permute-start.8) | collective-permute-done | bytes 262176 | tf_op jit(solution)/shard_map/ppermute | solution.py:16
  136.5 11.5 %collective-permute-done.11 = bf16[1,2,4,4,64,128]{5,4,3,2,1,0:T(8,128)(2,1)S(1)} collective-permute-done((bf16[1,2,4,4,64,128]{5,4,3,2,1,0:T(8,128)(2,1)S(1)}, bf16[1,2,4,4,64,128]{5,4,3,2,1,0:T(8,128)(2,1)S(1)}, u32[]{:S(2)}, u32[]{:S(2)}) %collective-permute-start.11) | collective-permute-done | bytes 524320 | tf_op jit(solution)/shard_map/ppermute | solution.py:16
  148.1 0.7 fusion.44
  148.8 0.3 copy-done.11
  149.1 0.3 fusion.90
  149.4 0.5 copy-done.9
  149.9 1.9 fusion.69
  151.8 41.3 %all-reduce.2.cloned.1.call-done = f32[16,8192]{1,0:T(8,128)} async-done(((f32[16,8192]{1,0:T(8,128)}), f32[16,8192]{1,0:T(8,128)}) %all-reduce.2.cloned.1.call-update) | async-done | bytes 524304 | tf_op jit(solution)/shard_map/psum | solution.py:78
  193.2 1.0 dynamic-slice_bitcast_fusion
  194.1 0.7 copy.51
  (65 shorter events, 0.6 us)
Async XLA Ops:
  7.2 30.3 %copy-start = (bf16[1,2,4,4,64,64]{5,4,3,2,1,0:T(8,128)(2,1)S(1)}, bf16[1,2,4,4,64,64]{5,4,3,2,1,0:T(8,128)(2,1)}, u32[]{:S(2)}) copy-start(bf16[1,2,4,4,64,64]{5,4,3,2,1,0:T(8,128)(2,1)} %param.7) | copy-start | bytes 786436
  7.2 186.0 %all-reduce.2.cloned.1.call-start = ((), (), s32[]{:S(2)}) async-start(), calls=%async_computation | async-start | bytes 1048576 | tf_op jit(solution)/shard_map/psum | solution.py:78
  7.2 39.7 %collective-permute-start.1 = (bf16[1,2,4,4,64,128]{5,4,3,2,1,0:T(8,128)(2,1)}, bf16[1,2,4,4,64,128]{5,4,3,2,1,0:T(8,128)(2,1)}, u32[]{:S(2)}, u32[]{:S(2)}) collective-permute-start(bf16[1,2,4,4,64,128]{5,4,3,2,1,0:T(8,128)(2,1)} %param.6), channel_id=1, source_target_pairs={{4,0},{8,4},{12,8},{16,12},{20,16},{24,20},{28,24},{32,28},{36,32}... | collective-permute-start | bytes 1572872 | tf_op jit(solution)/shard_map/ppermute | solution.py:16
  25.7 5.6 %copy-start.1 = (bf16[1,2,4,4,64,256]{5,4,3,2,1,0:T(8,128)(2,1)S(1)}, bf16[1,2,4,4,64,256]{5,4,3,2,1,0:T(8,128)(2,1)}, u32[]{:S(2)}) copy-start(bf16[1,2,4,4,64,256]{5,4,3,2,1,0:T(8,128)(2,1)} %param.8) | copy-start | bytes 3145732
  27.3 3.9 %copy-start.2 = (bf16[1,2,4,4,64,128]{5,4,3,2,1,0:T(8,128)(2,1)S(1)}, bf16[1,2,4,4,64,128]{5,4,3,2,1,0:T(8,128)(2,1)}, u32[]{:S(2)}) copy-start(bf16[1,2,4,4,64,128]{5,4,3,2,1,0:T(8,128)(2,1)} %param.6) | copy-start | bytes 1572868
  28.1 20.2 %collective-permute-start.2 = (bf16[1,1,4,4,64,128]{5,4,3,2,1,0:T(8,128)(2,1)}, bf16[1,1,4,4,64,128]{5,4,3,2,1,0:T(8,128)(2,1)}, u32[]{:S(2)}, u32[]{:S(2)}) collective-permute-start(bf16[1,1,4,4,64,128]{5,4,3,2,1,0:T(8,128)(2,1)} %get-tuple-element.15), channel_id=1, source_target_pairs={{3,0},{0,1},{1,2},{2,3},{7,4},{4,5},{5,6},{6,7},{11,8},{8,9},{9,10... | collective-permute-start | bytes 786440 | tf_op jit(solution)/shard_map/ppermute | solution.py:16
  32.7 33.5 %collective-permute-start.3 = (bf16[1,2,4,4,64,128]{5,4,3,2,1,0:T(8,128)(2,1)}, bf16[1,2,4,4,64,128]{5,4,3,2,1,0:T(8,128)(2,1)}, u32[]{:S(2)}, u32[]{:S(2)}) collective-permute-start(bf16[1,2,4,4,64,128]{5,4,3,2,1,0:T(8,128)(2,1)} %fusion.65), channel_id=1, source_target_pairs={{508,0},{0,4},{4,8},{8,12},{12,16},{16,20},{20,24},{24,28},{28,32}... | collective-permute-start | bytes 1572872 | tf_op jit(solution)/shard_map/ppermute | solution.py:16
  35.5 18.3 %collective-permute-start = (bf16[1,1,4,4,64,128]{5,4,3,2,1,0:T(8,128)(2,1)}, bf16[1,1,4,4,64,128]{5,4,3,2,1,0:T(8,128)(2,1)}, u32[]{:S(2)}, u32[]{:S(2)}) collective-permute-start(bf16[1,1,4,4,64,128]{5,4,3,2,1,0:T(8,128)(2,1)} %get-tuple-element.18), channel_id=1, source_target_pairs={{1,0},{2,1},{3,2},{0,3},{5,4},{6,5},{7,6},{4,7},{9,8},{10,9},{11,1... | collective-permute-start | bytes 786440 | tf_op jit(solution)/shard_map/ppermute | solution.py:16
  38.5 0.8 copy-start.4
  40.2 0.8 copy-start.6
  41.0 0.7 copy-start.12
  41.8 24.4 %slice-start.2 = ((bf16[1,2,4,4,64,128]{5,4,3,2,1,0:T(8,128)(2,1)}), bf16[1,2,3,4,64,128]{5,4,3,2,1,0:T(8,128)(2,1)S(1)}, s32[]{:S(2)}) async-start(bf16[1,2,4,4,64,128]{5,4,3,2,1,0:T(8,128)(2,1)} %copy-done.4), calls=%async_computation.3 | async-start | bytes 786432 | tf_op jit(solution)/shard_map/jit(_roll_static)/slice | solution.py:55
  41.8 24.4 %slice-start.3 = ((bf16[1,2,4,4,64,128]{5,4,3,2,1,0:T(8,128)(2,1)}), bf16[1,2,1,4,64,128]{5,4,3,2,1,0:T(8,128)(2,1)S(1)}, s32[]{:S(2)}) async-start(bf16[1,2,4,4,64,128]{5,4,3,2,1,0:T(8,128)(2,1)} %copy-done.4), calls=%async_computation.4 | async-start | bytes 262144 | tf_op jit(solution)/shard_map/jit(_roll_static)/slice | solution.py:55
  41.8 24.4 %slice-start.6 = ((bf16[1,2,4,4,64,128]{5,4,3,2,1,0:T(8,128)(2,1)}), bf16[1,2,4,3,64,128]{5,4,3,2,1,0:T(8,128)(2,1)S(1)}, s32[]{:S(2)}) async-start(bf16[1,2,4,4,64,128]{5,4,3,2,1,0:T(8,128)(2,1)} %copy-done.6), calls=%async_computation.7 | async-start | bytes 786432 | tf_op jit(solution)/shard_map/jit(_roll_static)/slice | solution.py:55
  41.8 24.4 %slice-start.7 = ((bf16[1,2,4,4,64,128]{5,4,3,2,1,0:T(8,128)(2,1)}), bf16[1,2,4,1,64,128]{5,4,3,2,1,0:T(8,128)(2,1)S(1)}, s32[]{:S(2)}) async-start(bf16[1,2,4,4,64,128]{5,4,3,2,1,0:T(8,128)(2,1)} %copy-done.6), calls=%async_computation.8 | async-start | bytes 262144 | tf_op jit(solution)/shard_map/jit(_roll_static)/slice | solution.py:55
  41.8 24.4 %copy-start.10 = (bf16[1,1,4,4,64,128]{5,4,3,2,1,0:T(8,128)(2,1)S(1)}, bf16[1,1,4,4,64,128]{5,4,3,2,1,0:T(8,128)(2,1)}, u32[]{:S(2)}) copy-start(bf16[1,1,4,4,64,128]{5,4,3,2,1,0:T(8,128)(2,1)} %get-tuple-element.17) | copy-start | bytes 786436
  68.2 24.4 %collective-permute-start.5 = (bf16[1,2,4,4,64,128]{5,4,3,2,1,0:T(8,128)(2,1)S(1)}, bf16[1,2,4,4,64,128]{5,4,3,2,1,0:T(8,128)(2,1)S(1)}, u32[]{:S(2)}, u32[]{:S(2)}) collective-permute-start(bf16[1,2,4,4,64,128]{5,4,3,2,1,0:T(8,128)(2,1)S(1)} %get-tuple-element.19), channel_id=1, source_target_pairs={{4,0},{8,4},{12,8},{16,12},{20,16},{24,20},{28,24},{32,28},{36,32}... | collective-permute-start | bytes 1572872 | tf_op jit(solution)/shard_map/ppermute | solution.py:16
  71.5 0.8 copy-start.7
  72.4 20.5 %collective-permute-start.6 = (bf16[1,1,4,4,64,128]{5,4,3,2,1,0:T(8,128)(2,1)S(1)}, bf16[1,1,4,4,64,128]{5,4,3,2,1,0:T(8,128)(2,1)S(1)}, u32[]{:S(2)}, u32[]{:S(2)}) collective-permute-start(bf16[1,1,4,4,64,128]{5,4,3,2,1,0:T(8,128)(2,1)S(1)} %get-tuple-element.11), channel_id=1, source_target_pairs={{3,0},{0,1},{1,2},{2,3},{7,4},{4,5},{5,6},{6,7},{11,8},{8,9},{9,10... | collective-permute-start | bytes 786440 | tf_op jit(solution)/shard_map/ppermute | solution.py:16
  74.5 29.4 %collective-permute-start.7 = (bf16[1,2,4,4,64,128]{5,4,3,2,1,0:T(8,128)(2,1)S(1)}, bf16[1,2,4,4,64,128]{5,4,3,2,1,0:T(8,128)(2,1)S(1)}, u32[]{:S(2)}, u32[]{:S(2)}) collective-permute-start(bf16[1,2,4,4,64,128]{5,4,3,2,1,0:T(8,128)(2,1)S(1)} %fusion.61), channel_id=1, source_target_pairs={{508,0},{0,4},{4,8},{8,12},{12,16},{16,20},{20,24},{24,28},{28,32}... | collective-permute-start | bytes 1572872 | tf_op jit(solution)/shard_map/ppermute | solution.py:16
  78.1 14.8 %collective-permute-start.4 = (bf16[1,1,4,4,64,128]{5,4,3,2,1,0:T(8,128)(2,1)S(1)}, bf16[1,1,4,4,64,128]{5,4,3,2,1,0:T(8,128)(2,1)S(1)}, u32[]{:S(2)}, u32[]{:S(2)}) collective-permute-start(bf16[1,1,4,4,64,128]{5,4,3,2,1,0:T(8,128)(2,1)S(1)} %get-tuple-element.14), channel_id=1, source_target_pairs={{1,0},{2,1},{3,2},{0,3},{5,4},{6,5},{7,6},{4,7},{9,8},{10,9},{11,1... | collective-permute-start | bytes 786440 | tf_op jit(solution)/shard_map/ppermute | solution.py:16
  82.6 0.8 copy-start.8
  83.4 20.5 %slice-start.8 = ((bf16[1,2,4,4,64,128]{5,4,3,2,1,0:T(8,128)(2,1)}), bf16[1,2,3,4,64,128]{5,4,3,2,1,0:T(8,128)(2,1)S(1)}, s32[]{:S(2)}) async-start(bf16[1,2,4,4,64,128]{5,4,3,2,1,0:T(8,128)(2,1)} %copy-done.7), calls=%async_computation.9 | async-start | bytes 786432 | tf_op jit(solution)/shard_map/jit(_roll_static)/slice | solution.py:55
  83.4 20.5 %slice-start.9 = ((bf16[1,2,4,4,64,128]{5,4,3,2,1,0:T(8,128)(2,1)}), bf16[1,2,1,4,64,128]{5,4,3,2,1,0:T(8,128)(2,1)S(1)}, s32[]{:S(2)}) async-start(bf16[1,2,4,4,64,128]{5,4,3,2,1,0:T(8,128)(2,1)} %copy-done.7), calls=%async_computation.10 | async-start | bytes 262144 | tf_op jit(solution)/shard_map/jit(_roll_static)/slice | solution.py:55
  83.4 20.5 %slice-start.10 = ((bf16[1,2,4,4,64,128]{5,4,3,2,1,0:T(8,128)(2,1)}), bf16[1,2,4,3,64,128]{5,4,3,2,1,0:T(8,128)(2,1)S(1)}, s32[]{:S(2)}) async-start(bf16[1,2,4,4,64,128]{5,4,3,2,1,0:T(8,128)(2,1)} %copy-done.8), calls=%async_computation.11 | async-start | bytes 786432 | tf_op jit(solution)/shard_map/jit(_roll_static)/slice | solution.py:55
  83.5 20.5 %slice-start.11 = ((bf16[1,2,4,4,64,128]{5,4,3,2,1,0:T(8,128)(2,1)}), bf16[1,2,4,1,64,128]{5,4,3,2,1,0:T(8,128)(2,1)S(1)}, s32[]{:S(2)}) async-start(bf16[1,2,4,4,64,128]{5,4,3,2,1,0:T(8,128)(2,1)} %copy-done.8), calls=%async_computation.12 | async-start | bytes 262144 | tf_op jit(solution)/shard_map/jit(_roll_static)/slice | solution.py:55
  104.7 19.9 %collective-permute-start.9 = (bf16[1,2,4,4,64,128]{5,4,3,2,1,0:T(8,128)(2,1)S(1)}, bf16[1,2,4,4,64,128]{5,4,3,2,1,0:T(8,128)(2,1)S(1)}, u32[]{:S(2)}, u32[]{:S(2)}) collective-permute-start(bf16[1,2,4,4,64,128]{5,4,3,2,1,0:T(8,128)(2,1)S(1)} %get-tuple-element.21), channel_id=1, source_target_pairs={{4,0},{8,4},{12,8},{16,12},{20,16},{24,20},{28,24},{32,28},{36,32}... | collective-permute-start | bytes 1572872 | tf_op jit(solution)/shard_map/ppermute | solution.py:16
  108.0 0.8 copy-start.3
  108.9 16.2 %collective-permute-start.10 = (bf16[1,1,4,4,64,128]{5,4,3,2,1,0:T(8,128)(2,1)S(1)}, bf16[1,1,4,4,64,128]{5,4,3,2,1,0:T(8,128)(2,1)S(1)}, u32[]{:S(2)}, u32[]{:S(2)}) collective-permute-start(bf16[1,1,4,4,64,128]{5,4,3,2,1,0:T(8,128)(2,1)S(1)} %get-tuple-element.7), channel_id=1, source_target_pairs={{3,0},{0,1},{1,2},{2,3},{7,4},{4,5},{5,6},{6,7},{11,8},{8,9},{9,10... | collective-permute-start | bytes 786440 | tf_op jit(solution)/shard_map/ppermute | solution.py:16
  116.4 31.7 %collective-permute-start.11 = (bf16[1,2,4,4,64,128]{5,4,3,2,1,0:T(8,128)(2,1)S(1)}, bf16[1,2,4,4,64,128]{5,4,3,2,1,0:T(8,128)(2,1)S(1)}, u32[]{:S(2)}, u32[]{:S(2)}) collective-permute-start(bf16[1,2,4,4,64,128]{5,4,3,2,1,0:T(8,128)(2,1)S(1)} %fusion.57), channel_id=1, source_target_pairs={{508,0},{0,4},{4,8},{8,12},{12,16},{16,20},{20,24},{24,28},{28,32}... | collective-permute-start | bytes 1572872 | tf_op jit(solution)/shard_map/ppermute | solution.py:16
  120.0 16.5 %collective-permute-start.8 = (bf16[1,1,4,4,64,128]{5,4,3,2,1,0:T(8,128)(2,1)S(1)}, bf16[1,1,4,4,64,128]{5,4,3,2,1,0:T(8,128)(2,1)S(1)}, u32[]{:S(2)}, u32[]{:S(2)}) collective-permute-start(bf16[1,1,4,4,64,128]{5,4,3,2,1,0:T(8,128)(2,1)S(1)} %get-tuple-element.10), channel_id=1, source_target_pairs={{1,0},{2,1},{3,2},{0,3},{5,4},{6,5},{7,6},{4,7},{9,8},{10,9},{11,1... | collective-permute-start | bytes 786440 | tf_op jit(solution)/shard_map/ppermute | solution.py:16
  123.9 0.8 copy-start.5
  124.6 23.4 %slice-start = ((bf16[1,2,4,4,64,128]{5,4,3,2,1,0:T(8,128)(2,1)}), bf16[1,2,3,4,64,128]{5,4,3,2,1,0:T(8,128)(2,1)S(1)}, s32[]{:S(2)}) async-start(bf16[1,2,4,4,64,128]{5,4,3,2,1,0:T(8,128)(2,1)} %copy-done.3), calls=%async_computation.1 | async-start | bytes 786432 | tf_op jit(solution)/shard_map/jit(_roll_static)/slice | solution.py:55
  124.6 23.4 %slice-start.1 = ((bf16[1,2,4,4,64,128]{5,4,3,2,1,0:T(8,128)(2,1)}), bf16[1,2,1,4,64,128]{5,4,3,2,1,0:T(8,128)(2,1)S(1)}, s32[]{:S(2)}) async-start(bf16[1,2,4,4,64,128]{5,4,3,2,1,0:T(8,128)(2,1)} %copy-done.3), calls=%async_computation.2 | async-start | bytes 262144 | tf_op jit(solution)/shard_map/jit(_roll_static)/slice | solution.py:55
  124.6 23.4 %slice-start.4 = ((bf16[1,2,4,4,64,128]{5,4,3,2,1,0:T(8,128)(2,1)}), bf16[1,2,4,3,64,128]{5,4,3,2,1,0:T(8,128)(2,1)S(1)}, s32[]{:S(2)}) async-start(bf16[1,2,4,4,64,128]{5,4,3,2,1,0:T(8,128)(2,1)} %copy-done.5), calls=%async_computation.5 | async-start | bytes 786432 | tf_op jit(solution)/shard_map/jit(_roll_static)/slice | solution.py:55
  124.6 23.4 %slice-start.5 = ((bf16[1,2,4,4,64,128]{5,4,3,2,1,0:T(8,128)(2,1)}), bf16[1,2,4,1,64,128]{5,4,3,2,1,0:T(8,128)(2,1)S(1)}, s32[]{:S(2)}) async-start(bf16[1,2,4,4,64,128]{5,4,3,2,1,0:T(8,128)(2,1)} %copy-done.5), calls=%async_computation.6 | async-start | bytes 262144 | tf_op jit(solution)/shard_map/jit(_roll_static)/slice | solution.py:55
  148.1 1.0 copy-start.11
  149.1 0.8 copy-start.9
Sparse Core Ops, SparseCore 0:
  151.9 41.1 all-reduce.1
where the time goes:
time: 202 us
  waiting for transfers between devices  107 us (53%)
  starting transfers between devices  50.1 us (25%)
  matrix products  18.6 us (9%)
  between operations  14.7 us (7%)
  local copies, waits for them, and re-layouts  10.1 us (5%)
    ppermute x12, waiting for transfers between devices, shifted(): return lax.ppermute(block, axis, route)  66.1 us
    ppermute x12, starting transfers between devices, shifted(): return lax.ppermute(block, axis, route)  50.1 us
    psum x1, waiting for transfers between devices, shards(): summed = lax.psum(partial_sums, 'gz')  41.3 us
    dot_general x15, matrix products, local_mult(): jnp.einsum('tzxyab,tzxybr->tzxyar', codes, vector, preferred_element_type...  8.42 us
    dot_general x12, matrix products, local_mult_transposed(): jnp.einsum('tzxyab,tzxyar->tzxybr', codes, vector, preferred_element_type...  8.03 us
    unnamed x28, local copies, waits for them, and re-layouts  7.74 us
  transfers between devices with their start and end apart: 13, of which 8 were waited for; matrix products, arithmetic and copies ran while one was open for 8% of the time, Pallas kernels for 0%

commit v1 on v0

v1 whole, which is shorter than its diff:
```python
import functools

import jax
import jax.numpy as jnp
from jax import lax
from jax.experimental import pallas as pl
from jax.experimental.pallas import tpu as pltpu
from jax.sharding import PartitionSpec as P

ITERS = 3
OMEGA = 0.5
F32 = jnp.float32
BF16 = jnp.bfloat16
VMEM = pl.BlockSpec(memory_space=pltpu.VMEM)
SMEM = pl.BlockSpec(memory_space=pltpu.SMEM)
PARAMS = pltpu.CompilerParams(vmem_limit_bytes=12 * 1024 * 1024)


def shifted(block, axis, distance):
    n = lax.axis_size(axis)
    return lax.ppermute(block, axis, [((i - distance) % n, i) for i in range(n)])


def dot(a, b):
    return jnp.dot(a, b, preferred_element_type=F32)


def dot_t(a, b):
    return lax.dot_general(a, b, (((0,), (0,)), ((), ())), preferred_element_type=F32)


def first_terms(scales, vector, hops, t_terms, z_terms):
    sites, degrees = vector.shape[:2]
    last = sites - z_terms.shape[0]
    for s in range(sites):
        p = vector[s]
        t_terms[s] = (scales[5 * s + 4] * dot_t(hops[s, :, 3 * degrees :], p)).astype(BF16)
        if s >= last:
            z_terms[s - last] = (scales[5 * s + 3] * dot_t(hops[s, :, 2 * degrees : 3 * degrees], p)).astype(BF16)


def local_terms(shape, scales, estimate, source, vector, selfs, hops, z_next, z_back, partial):
    zs, xs, ys, d = shape

    def at(z, x, y):
        return (z * xs + x % xs) * ys + y % ys

    def fwd(m, s, p):
        return scales[5 * s + m + 1] * dot(hops[s, :, m * d : (m + 1) * d], p)

    def bwd(m, s):
        return scales[5 * s + m + 1] * dot_t(hops[s, :, m * d : (m + 1) * d], vector[s])

    for z in range(zs):
        for x in range(xs):
            for y in range(ys):
                s = at(z, x, y)
                p = vector[s]
                total = p.astype(F32) + scales[5 * s] * dot(selfs[s], p)
                total += fwd(0, s, vector[at(z, x + 1, y)])
                total += fwd(1, s, vector[at(z, x, y + 1)])
                total += fwd(2, s, vector[at(z + 1, x, y)] if z + 1 < zs else z_next[at(0, x, y)])
                total += bwd(0, at(z, x - 1, y))
                total += bwd(1, at(z, x, y - 1))
                total += bwd(2, at(z - 1, x, y)) if z else z_back[at(0, x, y)].astype(F32)
                partial[s] = estimate[s].astype(F32) + OMEGA * (source[s].astype(F32) - total)


def finish(sites, scales, partial, t_next, t_back, hops, s, d):
    total = scales[5 * s + 4] * dot(hops[s, :, 3 * d :], t_next[s]) + t_back[s].astype(F32)
    return partial[s] - OMEGA * total


def sweep_end(scales, partial, t_next, t_back, hops, estimate, vector, t_terms, z_terms):
    sites, d = vector.shape[:2]
    last = sites - z_terms.shape[0]
    for s in range(sites):
        e = finish(sites, scales, partial, t_next, t_back, hops, s, d)
        p = e.astype(BF16)
        estimate[s] = e
        vector[s] = p
        t_terms[s] = (scales[5 * s + 4] * dot_t(hops[s, :, 3 * d :], p)).astype(BF16)
        if s >= last:
            z_terms[s - last] = (scales[5 * s + 3] * dot_t(hops[s, :, 2 * d : 3 * d], p)).astype(BF16)


def last_end(peers, scales, labels, place, partial, t_next, t_back, hops, restrictor, vector, own, *rest):
    away, sums = rest[:-1], rest[-1]
    sites, d = vector.shape[:2]
    keep = own.shape[0]
    sums[...] = jnp.zeros_like(sums)
    for s in range(sites):
        p = finish(sites, scales, partial, t_next, t_back, hops, s, d).astype(BF16)
        vector[s] = p
        sums[labels[s]] += dot(restrictor[s], p)
    me = place[0]
    own[...] = sums[pl.ds(me * keep, keep)]
    for j, out in enumerate(away, 1):
        out[...] = sums[pl.ds((me ^ j) * keep, keep)].astype(BF16)


def shards(source, self_codes, hop_codes, link_scales, restrict_map, restrictor):
    ts, zs, xs, ys, d, cols = source.shape
    assert ts == 1
    sites, edge = zs * xs * ys, xs * ys
    b = source.reshape(sites, d, cols)
    selfs = self_codes.reshape(sites, d, d)
    hops = hop_codes.reshape(sites, d, 4 * d)
    restricts = restrictor.reshape(sites, -1, d)
    scales = link_scales.astype(F32).reshape(sites * 5)
    labels = restrict_map.reshape(sites)
    field = jax.ShapeDtypeStruct((sites, d, cols), BF16)
    wide = jax.ShapeDtypeStruct((sites, d, cols), F32)
    slab = jax.ShapeDtypeStruct((edge, d, cols), BF16)

    t_terms, z_terms = pl.pallas_call(
        first_terms,
        out_shape=(field, slab),
        in_specs=[SMEM, VMEM, VMEM],
        out_specs=(VMEM, VMEM),
        compiler_params=PARAMS,
    )(scales, b, hops)
    vector, estimate = b, b
    for sweep in range(ITERS):
        t_back = shifted(t_terms, "ta", 1)
        t_next = shifted(vector, "ta", -1)
        z_next = shifted(vector[:edge], "gz", -1)
        z_back = shifted(z_terms, "gz", 1)
        partial = pl.pallas_call(
            functools.partial(local_terms, (zs, xs, ys, d)),
            out_shape=wide,
            in_specs=[SMEM] + [VMEM] * 7,
            out_specs=VMEM,
            compiler_params=PARAMS,
        )(scales, estimate, b, vector, selfs, hops, z_next, z_back)
        if sweep + 1 < ITERS:
            estimate, vector, t_terms, z_terms = pl.pallas_call(
                sweep_end,
                out_shape=(wide, field, field, slab),
                in_specs=[SMEM] + [VMEM] * 3 + [VMEM],
                out_specs=(VMEM,) * 4,
                compiler_params=PARAMS,
            )(scales, partial, t_next, t_back, hops)
    peers = lax.axis_size("gz")
    keep = 16 // peers
    coarse_d = restricts.shape[1]
    own_shape = jax.ShapeDtypeStruct((keep, coarse_d, cols), F32)
    away_shape = jax.ShapeDtypeStruct((keep, coarse_d, cols), BF16)
    place = lax.axis_index("gz").reshape(1).astype(jnp.int32)
    smoothed, own, *away = pl.pallas_call(
        functools.partial(last_end, peers),
        out_shape=(field, own_shape) + (away_shape,) * (peers - 1),
        in_specs=[SMEM] * 3 + [VMEM] * 3 + [VMEM, VMEM],
        out_specs=(VMEM,) * (peers + 1),
        scratch_shapes=[pltpu.VMEM((keep * peers, coarse_d, cols), F32)],
        compiler_params=PARAMS,
    )(scales, labels, place, partial, t_next, t_back, hops, restricts)
    came = [
        lax.ppermute(part, "gz", [(i, i ^ j) for i in range(peers)]) for j, part in enumerate(away, 1)
    ]
    coarse = own
    for part in came:
        coarse = coarse + part.astype(F32)
    return smoothed.reshape(source.shape), coarse.reshape(1, keep, coarse_d, cols)


def solution(mesh):
    site = P("ta", "gz", None, None, None, None)
    return jax.shard_map(
        shards,
        mesh=mesh,
        in_specs=(site, site, site, P("ta", "gz", None, None, None), P("ta", "gz", None, None), site),
        out_specs=(site, P("ta", "gz", None, None)),
        check_vma=False,
    )
```

time: 202 us -> 158 us (0.78)
  waiting for transfers between devices: 107 us -> 66.1 us
  Pallas kernels: 0 us -> 20.7 us
  matrix products: 18.6 us -> 0 us
  between operations: 14.7 us -> 0.9 us
  starting transfers between devices: 50.1 us -> 62.9 us
  local copies, waits for them, and re-layouts: 10.1 us -> 6.16 us
    psum x1 -> x0, waiting for transfers between devices: 41.3 us -> none  [shards(): summed = lax.psum(partial_sums, 'gz')]
    pallas_call x0 -> x7, Pallas kernels: none -> 20.7 us  [the longest x3 9.12 us: shards(): pl.pallas_call(functools.partial(local_terms, (zs, xs, ys, d)), out_shape...]
    dot_general x29 -> x0, matrix products: 18.6 us -> none  [the longest x15 8.42 us: local_mult(): jnp.einsum('tzxyab,tzxybr->tzxyar', codes, vector, preferred_element_type...]
    ppermute x12 -> x15, starting transfers between devices: 50.1 us -> 62.9 us  [the longest x12 53.8 us: shifted(): lax.ppermute(block, axis, [((i - distance) % n, i) for i in range(n)])]
    unnamed x28 -> x18, local copies, waits for them, and re-layouts: 7.74 us -> 4.52 us
    ppermute x12 -> x15, waiting for transfers between devices: 66.1 us -> 66.1 us  [the longest x12 64 us: shifted(): lax.ppermute(block, axis, [((i - distance) % n, i) for i in range(n)])]
  transfers between devices with their start and end apart: 13 -> 15, of which waited for: 8 -> 7; matrix products, arithmetic and copies ran while one was open for 8% -> 1% of each run, Pallas kernels for 0% -> 6%
where the time goes in v1:
time: 158 us; the launch traced here: 157 us
  waiting for transfers between devices  66.1 us (42%)
  starting transfers between devices  62.9 us (40%)
  Pallas kernels  20.7 us (13%)
  local copies, waits for them, and re-layouts  6.16 us (4%)
    ppermute x12, waiting for transfers between devices, shifted(): lax.ppermute(block, axis, [((i - distance) % n, i) for i in range(n)])  64 us
    ppermute x12, starting transfers between devices, shifted(): lax.ppermute(block, axis, [((i - distance) % n, i) for i in range(n)])  53.8 us
    pallas_call x3, Pallas kernels, shards(): pl.pallas_call(functools.partial(local_terms, (zs, xs, ys, d)), out_shape...  9.12 us
    ppermute x3, starting transfers between devices, shards(): lax.ppermute(part, 'gz', [(i, i ^ j) for i in range(peers)])  9.1 us
    pallas_call x2, Pallas kernels, shards(): pl.pallas_call(sweep_end, out_shape=(wide, field, field, slab), in_specs=...  7.6 us
    unnamed x18, local copies, waits for them, and re-layouts  4.52 us
  transfers between devices with their start and end apart: 15, of which 7 were waited for; matrix products, arithmetic and copies ran while one was open for 1% of the time, Pallas kernels for 6%

profile of v1, /device:TPU:1, one launch (start us, length us, event | category | flops | bytes accessed | tf_op | source)
XLA Modules:
  0.0 157.5 jit_solution(7965168982935144102)
XLA Ops:
  0.6 0.8 reshape.45.scales
  1.4 0.0 copy-start
  1.4 1.2 copy-done
  2.7 0.0 copy-start.2
  2.7 1.0 copy-done.2
  3.7 1.6 %shard_map.77 = (bf16[32,64,128]{2,1,0:T(8,128)(2,1)S(1)}, bf16[16,64,128]{2,1,0:T(8,128)(2,1)S(1)}) custom-call(f32[160]{0:T(256)S(1)} %reshape.45.scales, bf16[32,64,128]{2,1,0:T(8,128)(2,1)S(1)} %bitcast.16, bf16[32,64,256]{2,1,0:T(8,128)(2,1)S(1)} %bitcast.9), custom_call_target="tpu_custom_call" | custom-call | tf_op jit(solution)/shard_map/pallas_call | solution.py:116
  5.3 0.0 copy-start.4
  5.3 5.0 %collective-permute-start.3 = (bf16[32,64,128]{2,1,0:T(8,128)(2,1)S(1)}, bf16[32,64,128]{2,1,0:T(8,128)(2,1)S(1)}, u32[]{:S(2)}, u32[]{:S(2)}) collective-permute-start(bf16[32,64,128]{2,1,0:T(8,128)(2,1)S(1)} %get-tuple-element.18), channel_id=1, source_target_pairs={{508,0},{0,4},{4,8},{8,12},{12,16},{16,20},{20,24},{24,28},{28,32}... | collective-permute-start | bytes 1572872 | tf_op jit(solution)/shard_map/ppermute | solution.py:21
  10.3 14.5 %collective-permute-start.2 = (bf16[32,64,128]{2,1,0:T(8,128)(2,1)S(1)}, bf16[32,64,128]{2,1,0:T(8,128)(2,1)S(1)}, u32[]{:S(2)}, u32[]{:S(2)}) collective-permute-start(bf16[32,64,128]{2,1,0:T(8,128)(2,1)S(1)} %bitcast.17), channel_id=1, source_target_pairs={{4,0},{8,4},{12,8},{16,12},{20,16},{24,20},{28,24},{32,28},{36,32}... | collective-permute-start | bytes 1572872 | tf_op jit(solution)/shard_map/ppermute | solution.py:21
  24.8 3.1 %collective-permute-start.1 = (bf16[16,64,128]{2,1,0:T(8,128)(2,1)S(1)}, bf16[16,64,128]{2,1,0:T(8,128)(2,1)S(1)}, u32[]{:S(2)}, u32[]{:S(2)}) collective-permute-start(bf16[16,64,128]{2,1,0:T(8,128)(2,1)S(1)} %get-tuple-element.17), channel_id=1, source_target_pairs={{3,0},{0,1},{1,2},{2,3},{7,4},{4,5},{5,6},{6,7},{11,8},{8,9},{9,10... | collective-permute-start | bytes 786440 | tf_op jit(solution)/shard_map/ppermute | solution.py:21
  28.0 1.9 %collective-permute-start = (bf16[16,64,128]{2,1,0:T(8,128)(2,1)S(1)}, bf16[16,64,128]{2,1,0:T(8,128)(2,1)S(1)}, u32[]{:S(2)}, u32[]{:S(2)}) collective-permute-start(bf16[16,64,128]{2,1,0:T(8,128)(2,1)S(1)} %bitcast.27), channel_id=1, source_target_pairs={{1,0},{2,1},{3,2},{0,3},{5,4},{6,5},{7,6},{4,7},{9,8},{10,9},{11,1... | collective-permute-start | bytes 786440 | tf_op jit(solution)/shard_map/ppermute | solution.py:21
  29.9 1.3 collective-permute-done.1.z_back
  31.2 21.9 %collective-permute-done.z_next = bf16[16,64,128]{2,1,0:T(8,128)(2,1)S(1)} collective-permute-done((bf16[16,64,128]{2,1,0:T(8,128)(2,1)S(1)}, bf16[16,64,128]{2,1,0:T(8,128)(2,1)S(1)}, u32[]{:S(2)}, u32[]{:S(2)}) %collective-permute-start) | collective-permute-done | bytes 262176 | tf_op jit(solution)/shard_map/ppermute | solution.py:21
  53.2 0.0 copy-done.4
  53.2 0.0 copy-start.1
  53.2 2.9 %shard_map.78.partial = f32[32,64,128]{2,1,0:T(8,128)S(1)} custom-call(f32[160]{0:T(256)S(1)} %reshape.45.scales, bf16[32,64,128]{2,1,0:T(8,128)(2,1)S(1)} %bitcast.18, bf16[32,64,128]{2,1,0:T(8,128)(2,1)S(1)} %bitcast.19, bf16[32,64,128]{2,1,0:T(8,128)(2,1)S(1)} %bitcast.20, bf16[32,64,64]{2,1,0:T(8,128)(2,1)S(1)} %bitcast.23, ...), custom_call_target="tpu_custom_call" | custom-call | tf_op jit(solution)/shard_map/pallas_call | solution.py:129
  56.1 0.0 collective-permute-done.3.t_back
  56.1 0.0 collective-permute-done.2.t_next
  56.1 0.0 copy-done.1
  56.1 3.3 %shard_map.79 = (f32[32,64,128]{2,1,0:T(8,128)S(1)}, bf16[32,64,128]{2,1,0:T(8,128)(2,1)S(1)}, bf16[32,64,128]{2,1,0:T(8,128)(2,1)S(1)}, bf16[16,64,128]{2,1,0:T(8,128)(2,1)S(1)}) custom-call(f32[160]{0:T(256)S(1)} %reshape.45.scales, f32[32,64,128]{2,1,0:T(8,128)S(1)} %shard_map.78.partial, bf16[32,64,128]{2,1,0:T(8,128)(2,1)S(1)} %collective-permute-done.2.t_next, ...), custom_call_target="tpu_custom_call" | custom-call | tf_op jit(solution)/shard_map/pallas_call | solution.py:137
  59.4 1.9 %collective-permute-start.6 = (bf16[32,64,128]{2,1,0:T(8,128)(2,1)S(1)}, bf16[32,64,128]{2,1,0:T(8,128)(2,1)S(1)}, u32[]{:S(2)}, u32[]{:S(2)}) collective-permute-start(bf16[32,64,128]{2,1,0:T(8,128)(2,1)S(1)} %get-tuple-element.20.vector), channel_id=1, source_target_pairs={{4,0},{8,4},{12,8},{16,12},{20,16},{24,20},{28,24},{32,28},{36,32}... | collective-permute-start | bytes 1572872 | tf_op jit(solution)/shard_map/ppermute | solution.py:21
  61.4 3.4 %collective-permute-start.7 = (bf16[32,64,128]{2,1,0:T(8,128)(2,1)S(1)}, bf16[32,64,128]{2,1,0:T(8,128)(2,1)S(1)}, u32[]{:S(2)}, u32[]{:S(2)}) collective-permute-start(bf16[32,64,128]{2,1,0:T(8,128)(2,1)S(1)} %get-tuple-element.22), channel_id=1, source_target_pairs={{508,0},{0,4},{4,8},{8,12},{12,16},{16,20},{20,24},{24,28},{28,32}... | collective-permute-start | bytes 1572872 | tf_op jit(solution)/shard_map/ppermute | solution.py:21
  64.8 2.1 %collective-permute-start.4 = (bf16[16,64,128]{2,1,0:T(8,128)(2,1)S(1)}, bf16[16,64,128]{2,1,0:T(8,128)(2,1)S(1)}, u32[]{:S(2)}, u32[]{:S(2)}) collective-permute-start(bf16[16,64,128]{2,1,0:T(8,128)(2,1)S(1)} %slice.14), channel_id=1, source_target_pairs={{1,0},{2,1},{3,2},{0,3},{5,4},{6,5},{7,6},{4,7},{9,8},{10,9},{11,1... | collective-permute-start | bytes 786440 | tf_op jit(solution)/shard_map/ppermute | solution.py:21
  66.8 3.5 %collective-permute-start.5 = (bf16[16,64,128]{2,1,0:T(8,128)(2,1)S(1)}, bf16[16,64,128]{2,1,0:T(8,128)(2,1)S(1)}, u32[]{:S(2)}, u32[]{:S(2)}) collective-permute-start(bf16[16,64,128]{2,1,0:T(8,128)(2,1)S(1)} %get-tuple-element.21), channel_id=1, source_target_pairs={{3,0},{0,1},{1,2},{2,3},{7,4},{4,5},{5,6},{6,7},{11,8},{8,9},{9,10... | collective-permute-start | bytes 786440 | tf_op jit(solution)/shard_map/ppermute | solution.py:21
  70.3 20.8 %collective-permute-done.4.z_next = bf16[16,64,128]{2,1,0:T(8,128)(2,1)S(1)} collective-permute-done((bf16[16,64,128]{2,1,0:T(8,128)(2,1)S(1)}, bf16[16,64,128]{2,1,0:T(8,128)(2,1)S(1)}, u32[]{:S(2)}, u32[]{:S(2)}) %collective-permute-start.4) | collective-permute-done | bytes 262176 | tf_op jit(solution)/shard_map/ppermute | solution.py:21
  91.1 0.0 collective-permute-done.5.z_back
  91.1 2.9 %shard_map.80.partial = f32[32,64,128]{2,1,0:T(8,128)S(1)} custom-call(f32[160]{0:T(256)S(1)} %reshape.45.scales, f32[32,64,128]{2,1,0:T(8,128)S(1)} %get-tuple-element.19.estimate, bf16[32,64,128]{2,1,0:T(8,128)(2,1)S(1)} %bitcast.21, bf16[32,64,128]{2,1,0:T(8,128)(2,1)S(1)} %get-tuple-element.20.vector, bf16[32,64,64]{2,1,0:T(8,128)(2,1)S(1)} %bitcast.24, ...), custom_call_target="tpu_custom_call" | custom-call | tf_op jit(solution)/shard_map/pallas_call | solution.py:129
  94.0 0.0 collective-permute-done.6.t_next
  94.0 0.4 collective-permute-done.7.t_back
  94.4 4.3 %shard_map.81 = (f32[32,64,128]{2,1,0:T(8,128)S(1)}, bf16[32,64,128]{2,1,0:T(8,128)(2,1)S(1)}, bf16[32,64,128]{2,1,0:T(8,128)(2,1)}, bf16[16,64,128]{2,1,0:T(8,128)(2,1)}) custom-call(f32[160]{0:T(256)S(1)} %reshape.45.scales, f32[32,64,128]{2,1,0:T(8,128)S(1)} %shard_map.80.partial, bf16[32,64,128]{2,1,0:T(8,128)(2,1)S(1)} %collective-permute-done.6.t_next, ...), custom_call_target="tpu_custom_call" | custom-call | tf_op jit(solution)/shard_map/pallas_call | solution.py:137
  98.7 0.0 copy-start.5
  98.7 1.0 copy-done.5
  99.7 0.0 copy-start.3
  99.7 9.8 %collective-permute-start.10 = (bf16[32,64,128]{2,1,0:T(8,128)(2,1)S(1)}, bf16[32,64,128]{2,1,0:T(8,128)(2,1)S(1)}, u32[]{:S(2)}, u32[]{:S(2)}) collective-permute-start(bf16[32,64,128]{2,1,0:T(8,128)(2,1)S(1)} %get-tuple-element.24.vector), channel_id=1, source_target_pairs={{4,0},{8,4},{12,8},{16,12},{20,16},{24,20},{28,24},{32,28},{36,32}... | collective-permute-start | bytes 1572872 | tf_op jit(solution)/shard_map/ppermute | solution.py:21
  109.6 1.9 %collective-permute-start.11 = (bf16[32,64,128]{2,1,0:T(8,128)(2,1)}, bf16[32,64,128]{2,1,0:T(8,128)(2,1)}, u32[]{:S(2)}, u32[]{:S(2)}) collective-permute-start(bf16[32,64,128]{2,1,0:T(8,128)(2,1)} %get-tuple-element.26), channel_id=1, source_target_pairs={{508,0},{0,4},{4,8},{8,12},{12,16},{16,20},{20,24},{24,28},{28,32}... | collective-permute-start | bytes 1572872 | tf_op jit(solution)/shard_map/ppermute | solution.py:21
  111.5 0.7 slice.15
  112.2 0.0 copy-start.8
  112.2 2.8 %collective-permute-start.8 = (bf16[16,64,128]{2,1,0:T(8,128)(2,1)}, bf16[16,64,128]{2,1,0:T(8,128)(2,1)S(1)}, u32[]{:S(2)}, u32[]{:S(2)}) collective-permute-start(bf16[16,64,128]{2,1,0:T(8,128)(2,1)} %slice.15), channel_id=1, source_target_pairs={{1,0},{2,1},{3,2},{0,3},{5,4},{6,5},{7,6},{4,7},{9,8},{10,9},{11,1... | collective-permute-start | bytes 786440 | tf_op jit(solution)/shard_map/ppermute | solution.py:21
  115.0 3.9 %collective-permute-start.9 = (bf16[16,64,128]{2,1,0:T(8,128)(2,1)}, bf16[16,64,128]{2,1,0:T(8,128)(2,1)}, u32[]{:S(2)}, u32[]{:S(2)}) collective-permute-start(bf16[16,64,128]{2,1,0:T(8,128)(2,1)} %get-tuple-element.25), channel_id=1, source_target_pairs={{3,0},{0,1},{1,2},{2,3},{7,4},{4,5},{5,6},{6,7},{11,8},{8,9},{9,10... | collective-permute-start | bytes 786440 | tf_op jit(solution)/shard_map/ppermute | solution.py:21
  118.9 0.0 copy-done.8
  118.9 0.1 reshape.36.labels
  119.0 19.5 %collective-permute-done.8.z_next = bf16[16,64,128]{2,1,0:T(8,128)(2,1)S(1)} collective-permute-done((bf16[16,64,128]{2,1,0:T(8,128)(2,1)}, bf16[16,64,128]{2,1,0:T(8,128)(2,1)S(1)}, u32[]{:S(2)}, u32[]{:S(2)}) %collective-permute-start.8) | collective-permute-done | bytes 262176 | tf_op jit(solution)/shard_map/ppermute | solution.py:21
  138.5 0.0 collective-permute-done.9.z_back
  138.5 0.0 copy-done.3
  138.5 0.0 copy-start.6
  138.5 1.2 copy-done.6
  139.8 0.0 copy-start.7
  139.8 3.3 %shard_map.82.partial = f32[32,64,128]{2,1,0:T(8,128)S(1)} custom-call(f32[160]{0:T(256)S(1)} %reshape.45.scales, f32[32,64,128]{2,1,0:T(8,128)S(1)} %copy-done.6, bf16[32,64,128]{2,1,0:T(8,128)(2,1)S(1)} %bitcast.22, bf16[32,64,128]{2,1,0:T(8,128)(2,1)S(1)} %get-tuple-element.24.vector, bf16[32,64,64]{2,1,0:T(8,128)(2,1)S(1)} %bitcast.25, ...), custom_call_target="tpu_custom_call" | custom-call | tf_op jit(solution)/shard_map/pallas_call | solution.py:129
  143.1 0.0 collective-permute-done.10.t_next
  143.1 0.0 collective-permute-done.11.t_back
  143.1 0.0 copy-done.7
  143.2 2.4 %shard_map.83 = (bf16[32,64,128]{2,1,0:T(8,128)(2,1)}, f32[4,64,128]{2,1,0:T(8,128)S(1)}, bf16[4,64,128]{2,1,0:T(8,128)(2,1)S(1)}, bf16[4,64,128]{2,1,0:T(8,128)(2,1)S(1)}, bf16[4,64,128]{2,1,0:T(8,128)(2,1)S(1)}) custom-call(f32[160]{0:T(256)S(1)} %reshape.45.scales, s32[32]{0:T(128)S(1)} %reshape.36.labels, s32[1]{0:T(128)} %bitcast.place, ...), custom_call_target="tpu_custom_call" | custom-call | tf_op jit(solution)/shard_map/pallas_call | solution.py:150
  145.5 3.6 %collective-permute-start.12 = (bf16[4,64,128]{2,1,0:T(8,128)(2,1)S(1)}, bf16[4,64,128]{2,1,0:T(8,128)(2,1)S(1)}, u32[]{:S(2)}, u32[]{:S(2)}) collective-permute-start(bf16[4,64,128]{2,1,0:T(8,128)(2,1)S(1)} %get-tuple-element.29), channel_id=1, source_target_pairs={{0,1},{1,0},{2,3},{3,2},{4,5},{5,4},{6,7},{7,6},{8,9},{9,8},{10,11... | collective-permute-start | bytes 196616 | tf_op jit(solution)/shard_map/ppermute | solution.py:159
  149.2 1.9 %collective-permute-start.13 = (bf16[4,64,128]{2,1,0:T(8,128)(2,1)S(1)}, bf16[4,64,128]{2,1,0:T(8,128)(2,1)S(1)}, u32[]{:S(2)}, u32[]{:S(2)}) collective-permute-start(bf16[4,64,128]{2,1,0:T(8,128)(2,1)S(1)} %get-tuple-element.30), channel_id=1, source_target_pairs={{0,2},{1,3},{2,0},{3,1},{4,6},{5,7},{6,4},{7,5},{8,10},{9,11},{10,... | collective-permute-start | bytes 196616 | tf_op jit(solution)/shard_map/ppermute | solution.py:159
  151.1 3.5 %collective-permute-start.14 = (bf16[4,64,128]{2,1,0:T(8,128)(2,1)S(1)}, bf16[4,64,128]{2,1,0:T(8,128)(2,1)S(1)}, u32[]{:S(2)}, u32[]{:S(2)}) collective-permute-start(bf16[4,64,128]{2,1,0:T(8,128)(2,1)S(1)} %get-tuple-element.31), channel_id=1, source_target_pairs={{0,3},{1,2},{2,1},{3,0},{4,7},{5,6},{6,5},{7,4},{8,11},{9,10},{10,... | collective-permute-start | bytes 196616 | tf_op jit(solution)/shard_map/ppermute | solution.py:159
  154.6 0.0 collective-permute-done.12
  154.7 0.1 collective-permute-done.13
  154.8 2.0 %collective-permute-done.14 = bf16[4,64,128]{2,1,0:T(8,128)(2,1)S(1)} collective-permute-done((bf16[4,64,128]{2,1,0:T(8,128)(2,1)S(1)}, bf16[4,64,128]{2,1,0:T(8,128)(2,1)S(1)}, u32[]{:S(2)}, u32[]{:S(2)}) %collective-permute-start.14) | collective-permute-done | bytes 65568 | tf_op jit(solution)/shard_map/ppermute | solution.py:159
  156.8 0.7 add_bitcast_fusion
  (2 shorter events, 0.0 us)
Async XLA Ops:
  1.4 1.2 copy-start
  2.7 1.0 copy-start.2
  5.3 47.9 %copy-start.4 = (bf16[1,2,4,4,64,64]{5,4,3,2,1,0:T(8,128)(2,1)S(1)}, bf16[1,2,4,4,64,64]{5,4,3,2,1,0:T(8,128)(2,1)}, u32[]{:S(2)}) copy-start(bf16[1,2,4,4,64,64]{5,4,3,2,1,0:T(8,128)(2,1)} %param.7) | copy-start | bytes 786436
  5.3 50.7 %collective-permute-start.3 = (bf16[32,64,128]{2,1,0:T(8,128)(2,1)S(1)}, bf16[32,64,128]{2,1,0:T(8,128)(2,1)S(1)}, u32[]{:S(2)}, u32[]{:S(2)}) collective-permute-start(bf16[32,64,128]{2,1,0:T(8,128)(2,1)S(1)} %get-tuple-element.18), channel_id=1, source_target_pairs={{508,0},{0,4},{4,8},{8,12},{12,16},{16,20},{20,24},{24,28},{28,32}... | collective-permute-start | bytes 1572872 | tf_op jit(solution)/shard_map/ppermute | solution.py:21
  10.3 45.8 %collective-permute-start.2 = (bf16[32,64,128]{2,1,0:T(8,128)(2,1)S(1)}, bf16[32,64,128]{2,1,0:T(8,128)(2,1)S(1)}, u32[]{:S(2)}, u32[]{:S(2)}) collective-permute-start(bf16[32,64,128]{2,1,0:T(8,128)(2,1)S(1)} %bitcast.17), channel_id=1, source_target_pairs={{4,0},{8,4},{12,8},{16,12},{20,16},{24,20},{28,24},{32,28},{36,32}... | collective-permute-start | bytes 1572872 | tf_op jit(solution)/shard_map/ppermute | solution.py:21
  24.8 6.4 %collective-permute-start.1 = (bf16[16,64,128]{2,1,0:T(8,128)(2,1)S(1)}, bf16[16,64,128]{2,1,0:T(8,128)(2,1)S(1)}, u32[]{:S(2)}, u32[]{:S(2)}) collective-permute-start(bf16[16,64,128]{2,1,0:T(8,128)(2,1)S(1)} %get-tuple-element.17), channel_id=1, source_target_pairs={{3,0},{0,1},{1,2},{2,3},{7,4},{4,5},{5,6},{6,7},{11,8},{8,9},{9,10... | collective-permute-start | bytes 786440 | tf_op jit(solution)/shard_map/ppermute | solution.py:21
  28.0 25.2 %collective-permute-start = (bf16[16,64,128]{2,1,0:T(8,128)(2,1)S(1)}, bf16[16,64,128]{2,1,0:T(8,128)(2,1)S(1)}, u32[]{:S(2)}, u32[]{:S(2)}) collective-permute-start(bf16[16,64,128]{2,1,0:T(8,128)(2,1)S(1)} %bitcast.27), channel_id=1, source_target_pairs={{1,0},{2,1},{3,2},{0,3},{5,4},{6,5},{7,6},{4,7},{9,8},{10,9},{11,1... | collective-permute-start | bytes 786440 | tf_op jit(solution)/shard_map/ppermute | solution.py:21
  53.2 2.9 %copy-start.1 = (bf16[1,2,4,4,64,256]{5,4,3,2,1,0:T(8,128)(2,1)S(1)}, bf16[1,2,4,4,64,256]{5,4,3,2,1,0:T(8,128)(2,1)}, u32[]{:S(2)}) copy-start(bf16[1,2,4,4,64,256]{5,4,3,2,1,0:T(8,128)(2,1)} %param.8) | copy-start | bytes 3145732
  59.4 34.6 %collective-permute-start.6 = (bf16[32,64,128]{2,1,0:T(8,128)(2,1)S(1)}, bf16[32,64,128]{2,1,0:T(8,128)(2,1)S(1)}, u32[]{:S(2)}, u32[]{:S(2)}) collective-permute-start(bf16[32,64,128]{2,1,0:T(8,128)(2,1)S(1)} %get-tuple-element.20.vector), channel_id=1, source_target_pairs={{4,0},{8,4},{12,8},{16,12},{20,16},{24,20},{28,24},{32,28},{36,32}... | collective-permute-start | bytes 1572872 | tf_op jit(solution)/shard_map/ppermute | solution.py:21
  61.4 33.1 %collective-permute-start.7 = (bf16[32,64,128]{2,1,0:T(8,128)(2,1)S(1)}, bf16[32,64,128]{2,1,0:T(8,128)(2,1)S(1)}, u32[]{:S(2)}, u32[]{:S(2)}) collective-permute-start(bf16[32,64,128]{2,1,0:T(8,128)(2,1)S(1)} %get-tuple-element.22), channel_id=1, source_target_pairs={{508,0},{0,4},{4,8},{8,12},{12,16},{16,20},{20,24},{24,28},{28,32}... | collective-permute-start | bytes 1572872 | tf_op jit(solution)/shard_map/ppermute | solution.py:21
  64.8 26.3 %collective-permute-start.4 = (bf16[16,64,128]{2,1,0:T(8,128)(2,1)S(1)}, bf16[16,64,128]{2,1,0:T(8,128)(2,1)S(1)}, u32[]{:S(2)}, u32[]{:S(2)}) collective-permute-start(bf16[16,64,128]{2,1,0:T(8,128)(2,1)S(1)} %slice.14), channel_id=1, source_target_pairs={{1,0},{2,1},{3,2},{0,3},{5,4},{6,5},{7,6},{4,7},{9,8},{10,9},{11,1... | collective-permute-start | bytes 786440 | tf_op jit(solution)/shard_map/ppermute | solution.py:21
  66.8 24.3 %collective-permute-start.5 = (bf16[16,64,128]{2,1,0:T(8,128)(2,1)S(1)}, bf16[16,64,128]{2,1,0:T(8,128)(2,1)S(1)}, u32[]{:S(2)}, u32[]{:S(2)}) collective-permute-start(bf16[16,64,128]{2,1,0:T(8,128)(2,1)S(1)} %get-tuple-element.21), channel_id=1, source_target_pairs={{3,0},{0,1},{1,2},{2,3},{7,4},{4,5},{5,6},{6,7},{11,8},{8,9},{9,10... | collective-permute-start | bytes 786440 | tf_op jit(solution)/shard_map/ppermute | solution.py:21
  98.7 1.0 copy-start.5
  99.7 38.8 %copy-start.3 = (bf16[1,2,4,4,64,128]{5,4,3,2,1,0:T(8,128)(2,1)S(1)}, bf16[1,2,4,4,64,128]{5,4,3,2,1,0:T(8,128)(2,1)}, u32[]{:S(2)}) copy-start(bf16[1,2,4,4,64,128]{5,4,3,2,1,0:T(8,128)(2,1)} %param.6) | copy-start | bytes 1572868
  99.7 43.4 %collective-permute-start.10 = (bf16[32,64,128]{2,1,0:T(8,128)(2,1)S(1)}, bf16[32,64,128]{2,1,0:T(8,128)(2,1)S(1)}, u32[]{:S(2)}, u32[]{:S(2)}) collective-permute-start(bf16[32,64,128]{2,1,0:T(8,128)(2,1)S(1)} %get-tuple-element.24.vector), channel_id=1, source_target_pairs={{4,0},{8,4},{12,8},{16,12},{20,16},{24,20},{28,24},{32,28},{36,32}... | collective-permute-start | bytes 1572872 | tf_op jit(solution)/shard_map/ppermute | solution.py:21
  109.6 33.6 %collective-permute-start.11 = (bf16[32,64,128]{2,1,0:T(8,128)(2,1)}, bf16[32,64,128]{2,1,0:T(8,128)(2,1)}, u32[]{:S(2)}, u32[]{:S(2)}) collective-permute-start(bf16[32,64,128]{2,1,0:T(8,128)(2,1)} %get-tuple-element.26), channel_id=1, source_target_pairs={{508,0},{0,4},{4,8},{8,12},{12,16},{16,20},{20,24},{24,28},{28,32}... | collective-permute-start | bytes 1572872 | tf_op jit(solution)/shard_map/ppermute | solution.py:21
  112.2 6.7 %copy-start.8 = (s32[1,2,4,4]{3,2,1,0:T(4,128)S(1)}, s32[1,2,4,4]{3,2,1,0:T(4,128)}, u32[]{:S(2)}) copy-start(s32[1,2,4,4]{3,2,1,0:T(4,128)} %param.10) | copy-start | bytes 388
  112.2 26.3 %collective-permute-start.8 = (bf16[16,64,128]{2,1,0:T(8,128)(2,1)}, bf16[16,64,128]{2,1,0:T(8,128)(2,1)S(1)}, u32[]{:S(2)}, u32[]{:S(2)}) collective-permute-start(bf16[16,64,128]{2,1,0:T(8,128)(2,1)} %slice.15), channel_id=1, source_target_pairs={{1,0},{2,1},{3,2},{0,3},{5,4},{6,5},{7,6},{4,7},{9,8},{10,9},{11,1... | collective-permute-start | bytes 786440 | tf_op jit(solution)/shard_map/ppermute | solution.py:21
  115.0 23.5 %collective-permute-start.9 = (bf16[16,64,128]{2,1,0:T(8,128)(2,1)}, bf16[16,64,128]{2,1,0:T(8,128)(2,1)}, u32[]{:S(2)}, u32[]{:S(2)}) collective-permute-start(bf16[16,64,128]{2,1,0:T(8,128)(2,1)} %get-tuple-element.25), channel_id=1, source_target_pairs={{3,0},{0,1},{1,2},{2,3},{7,4},{4,5},{5,6},{6,7},{11,8},{8,9},{9,10... | collective-permute-start | bytes 786440 | tf_op jit(solution)/shard_map/ppermute | solution.py:21
  138.5 1.2 copy-start.6
  139.8 3.4 %copy-start.7 = (bf16[1,2,4,4,64,64]{5,4,3,2,1,0:T(8,128)(2,1)S(1)}, bf16[1,2,4,4,64,64]{5,4,3,2,1,0:T(8,128)(2,1)}, u32[]{:S(2)}) copy-start(bf16[1,2,4,4,64,64]{5,4,3,2,1,0:T(8,128)(2,1)} %param.11) | copy-start | bytes 786436
  145.5 9.1 %collective-permute-start.12 = (bf16[4,64,128]{2,1,0:T(8,128)(2,1)S(1)}, bf16[4,64,128]{2,1,0:T(8,128)(2,1)S(1)}, u32[]{:S(2)}, u32[]{:S(2)}) collective-permute-start(bf16[4,64,128]{2,1,0:T(8,128)(2,1)S(1)} %get-tuple-element.29), channel_id=1, source_target_pairs={{0,1},{1,0},{2,3},{3,2},{4,5},{5,4},{6,7},{7,6},{8,9},{9,8},{10,11... | collective-permute-start | bytes 196616 | tf_op jit(solution)/shard_map/ppermute | solution.py:159
  149.2 5.6 %collective-permute-start.13 = (bf16[4,64,128]{2,1,0:T(8,128)(2,1)S(1)}, bf16[4,64,128]{2,1,0:T(8,128)(2,1)S(1)}, u32[]{:S(2)}, u32[]{:S(2)}) collective-permute-start(bf16[4,64,128]{2,1,0:T(8,128)(2,1)S(1)} %get-tuple-element.30), channel_id=1, source_target_pairs={{0,2},{1,3},{2,0},{3,1},{4,6},{5,7},{6,4},{7,5},{8,10},{9,11},{10,... | collective-permute-start | bytes 196616 | tf_op jit(solution)/shard_map/ppermute | solution.py:159
  151.1 5.7 %collective-permute-start.14 = (bf16[4,64,128]{2,1,0:T(8,128)(2,1)S(1)}, bf16[4,64,128]{2,1,0:T(8,128)(2,1)S(1)}, u32[]{:S(2)}, u32[]{:S(2)}) collective-permute-start(bf16[4,64,128]{2,1,0:T(8,128)(2,1)S(1)} %get-tuple-element.31), channel_id=1, source_target_pairs={{0,3},{1,2},{2,1},{3,0},{4,7},{5,6},{6,5},{7,4},{8,11},{9,10},{10,... | collective-permute-start | bytes 196616 | tf_op jit(solution)/shard_map/ppermute | solution.py:159

commit v2 on v1

v2 whole, which is shorter than its diff:
```python
import functools

import jax
import jax.numpy as jnp
from jax import lax
from jax.experimental import pallas as pl
from jax.experimental.pallas import tpu as pltpu
from jax.sharding import PartitionSpec as P

ITERS = 3
OMEGA = 0.5
AGG = 16
PIECES = 4
F32 = jnp.float32
BF16 = jnp.bfloat16
VMEM = pl.BlockSpec(memory_space=pltpu.VMEM)
HBM = pl.BlockSpec(memory_space=pltpu.HBM)
SMEM = pl.BlockSpec(memory_space=pltpu.SMEM)
PARAMS = pltpu.CompilerParams(vmem_limit_bytes=12 * 1024 * 1024)

GROUP = 32
FORWARD_RELAY = {1: 24, 2: 0, 3: 7}
BACKWARD_RELAY = {1: 7, 2: 31, 3: 24}
FORWARD_SEAM, BACKWARD_SEAM = 1, 2


def routes(slices, members):
    forward, backward, out, back = [], [], [], []
    for t in range(slices):
        for g in range(members):
            here, ahead, behind = (((t + k) % slices) * members + g for k in (0, 1, -1))
            first = t // GROUP * GROUP
            if t % GROUP == GROUP - 1 and g in FORWARD_RELAY:
                relay = (first + FORWARD_RELAY[g]) * members + g
                out.append((here, relay))
                back.append((relay, ahead))
            else:
                forward.append((here, ahead))
            if t % GROUP == 0 and g in BACKWARD_RELAY:
                relay = (first + BACKWARD_RELAY[g]) * members + g
                out.append((here, relay))
                back.append((relay, behind))
            else:
                backward.append((here, behind))
    return forward, backward, out, back


def shifted(block, axis, distance):
    n = lax.axis_size(axis)
    return lax.ppermute(block, axis, [((i - distance) % n, i) for i in range(n)])


def dot(a, b):
    return jnp.dot(a, b, preferred_element_type=F32)


def dot_t(a, b):
    return lax.dot_general(a, b, (((0,), (0,)), ((), ())), preferred_element_type=F32)


def fill_detour(role, t_terms, vector, detour):
    @pl.when(role[0] == FORWARD_SEAM)
    def _():
        detour[...] = t_terms[...]

    @pl.when(role[0] == BACKWARD_SEAM)
    def _():
        detour[...] = vector[...]


def first_terms(role, scales, source, hops, t_terms, z_terms, detour, vector, codes, sems):
    sites, d = vector.shape[:2]
    xs, ys = scales.shape[2:4]
    last = sites - z_terms.shape[0]
    pieces = sems.shape[1]
    n = sites // pieces
    copies = []
    for i in range(pieces):
        part = pl.ds(i * n, n)
        copies.append(
            [
                pltpu.make_async_copy(hops.at[part, :, pl.ds(2 * d, 2 * d)], codes.at[part], sems.at[0, i]),
                pltpu.make_async_copy(source.at[part], vector.at[part], sems.at[1, i]),
            ]
        )
    for pair in copies:
        for copy in pair:
            copy.start()
    for s in range(sites):
        if s % n == 0:
            for copy in copies[s // n]:
                copy.wait()
        z, x, y = s // (xs * ys), s // ys % xs, s % ys
        scale = scales[0, z, x].astype(F32)
        t_terms[s] = (scale[y : y + 1, 4:5] * dot_t(codes[s, :, d:], vector[s])).astype(BF16)
        if s >= last:
            z_terms[s - last] = (scale[y : y + 1, 3:4] * dot_t(codes[s, :, :d], vector[s])).astype(BF16)
    fill_detour(role, t_terms, vector, detour)


def hop_terms(role, scales, vector, hops, t_terms, z_terms, detour):
    sites, d = vector.shape[:2]
    last = sites - z_terms.shape[0]
    for s in range(sites):
        t_terms[s] = (scales[5 * s + 4] * dot_t(hops[s, :, 3 * d :], vector[s])).astype(BF16)
    for s in range(last, sites):
        z_terms[s - last] = (scales[5 * s + 3] * dot_t(hops[s, :, 2 * d : 3 * d], vector[s])).astype(BF16)
    fill_detour(role, t_terms, vector, detour)


def local_terms(shape, scales, estimate, source, vector, selfs, hops, partial):
    zs, xs, ys, d = shape

    def at(z, x, y):
        return (z * xs + x % xs) * ys + y % ys

    def fwd(m, s, p):
        return scales[5 * s + m + 1] * dot(hops[s, :, m * d : (m + 1) * d], p)

    def bwd(m, s):
        return scales[5 * s + m + 1] * dot_t(hops[s, :, m * d : (m + 1) * d], vector[s])

    for z in range(zs):
        for x in range(xs):
            for y in range(ys):
                s = at(z, x, y)
                p = vector[s]
                total = p.astype(F32) + scales[5 * s] * dot(selfs[s], p)
                total += fwd(0, s, vector[at(z, x + 1, y)])
                total += fwd(1, s, vector[at(z, x, y + 1)])
                total += bwd(0, at(z, x - 1, y))
                total += bwd(1, at(z, x, y - 1))
                if z + 1 < zs:
                    total += fwd(2, s, vector[at(z + 1, x, y)])
                if z:
                    total += bwd(2, at(z - 1, x, y))
                partial[s] = estimate[s].astype(F32) + OMEGA * (source[s].astype(F32) - total)


def new_estimate(s, role, scales, partial, t_next, t_back, relayed, z_next, z_back, hops):
    sites, d = partial.shape[:2]
    edge = z_next.shape[0]
    last = sites - edge
    ahead = jnp.where(role[0] == FORWARD_SEAM, relayed[s], t_next[s])
    behind = jnp.where(role[0] == BACKWARD_SEAM, relayed[s], t_back[s])
    total = scales[5 * s + 4] * dot(hops[s, :, 3 * d :], ahead) + behind.astype(F32)
    if s >= last:
        total += scales[5 * s + 3] * dot(hops[s, :, 2 * d : 3 * d], z_next[s - last])
    if s < edge:
        total += z_back[s].astype(F32)
    return partial[s] - OMEGA * total


def sweep_end(role, scales, partial, t_next, t_back, relayed, z_next, z_back, hops, estimate, vector, *terms):
    for s in range(vector.shape[0]):
        e = new_estimate(s, role, scales, partial, t_next, t_back, relayed, z_next, z_back, hops)
        estimate[s] = e
        vector[s] = e.astype(BF16)
    hop_terms(role, scales, vector, hops, *terms)


def last_end(role, scales, labels, partial, t_next, t_back, relayed, z_next, z_back, hops, restrictor, vector, own, away, sums):
    half = own.shape[0] // 2
    sums[...] = jnp.zeros_like(sums)
    for s in range(vector.shape[0]):
        e = new_estimate(s, role, scales, partial, t_next, t_back, relayed, z_next, z_back, hops)
        vector[s] = e.astype(BF16)
    for s in range(vector.shape[0]):
        sums[labels[s]] += dot(restrictor[s], vector[s])
    core = role[1] % 2
    for chip in range(2):
        rows = pl.ds(chip * half, half)
        own[rows] = sums[pl.ds((2 * chip + core) * half, half)]
        away[rows] = sums[pl.ds((2 * chip + 1 - core) * half, half)].astype(BF16)


def coarse_step(role, own, came, mine, away):
    half = mine.shape[0]
    chip = role[1] // 2
    here, there = pl.ds(chip * half, half), pl.ds((1 - chip) * half, half)
    mine[...] = own[here] + came[here].astype(F32)
    away[...] = (own[there] + came[there].astype(F32)).astype(BF16)


def shards(source, self_codes, hop_codes, link_scales, restrict_map, restrictor):
    ts, zs, xs, ys, d, cols = source.shape
    assert ts == 1
    sites, edge = zs * xs * ys, xs * ys
    slices, members = lax.axis_size("ta"), lax.axis_size("gz")
    forward, backward, out, back = routes(slices, members)
    t, g = lax.axis_index("ta"), lax.axis_index("gz")
    seam = jnp.where(t % GROUP == GROUP - 1, FORWARD_SEAM, jnp.where(t % GROUP == 0, BACKWARD_SEAM, 0))
    role = jnp.stack([jnp.where(g == 0, 0, seam), g]).astype(jnp.int32)

    b = source.reshape(sites, d, cols)
    selfs = self_codes.reshape(sites, d, d)
    hops = hop_codes.reshape(sites, d, 4 * d)
    restricts = restrictor.reshape(sites, -1, d)
    labels = restrict_map.reshape(sites)
    field = jax.ShapeDtypeStruct((sites, d, cols), BF16)
    wide = jax.ShapeDtypeStruct((sites, d, cols), F32)
    slab = jax.ShapeDtypeStruct((edge, d, cols), BF16)
    both = ("ta", "gz")

    t_terms, z_terms, detour = pl.pallas_call(
        first_terms,
        out_shape=(field, slab, field),
        in_specs=[SMEM, VMEM, HBM, HBM],
        out_specs=(VMEM,) * 3,
        scratch_shapes=[
            pltpu.VMEM((sites, d, cols), BF16),
            pltpu.VMEM((sites, d, 2 * d), BF16),
            pltpu.SemaphoreType.DMA((2, PIECES)),
        ],
        compiler_params=PARAMS,
    )(role, link_scales, b, hops)
    late_scales, t_terms = lax.optimization_barrier((link_scales, t_terms))
    scales = late_scales.astype(F32).reshape(sites * 5)
    vector, estimate = b, b
    for sweep in range(ITERS):
        at_relay = lax.ppermute(detour, both, out)
        t_back = lax.ppermute(t_terms, both, forward)
        t_next = lax.ppermute(vector, both, backward)
        z_next = shifted(vector[:edge], "gz", -1)
        z_back = shifted(z_terms, "gz", 1)
        partial = pl.pallas_call(
            functools.partial(local_terms, (zs, xs, ys, d)),
            out_shape=wide,
            in_specs=[SMEM] + [VMEM] * 5,
            out_specs=VMEM,
            input_output_aliases={1: 0} if sweep else {},
            compiler_params=PARAMS,
        )(scales, estimate, b, vector, selfs, hops)
        relayed = lax.ppermute(at_relay, both, back)
        came = (partial, t_next, t_back, relayed, z_next, z_back, hops)
        if sweep + 1 < ITERS:
            estimate, vector, t_terms, z_terms, detour = pl.pallas_call(
                sweep_end,
                out_shape=(wide, field, field, slab, field),
                in_specs=[SMEM] * 2 + [VMEM] * 7,
                out_specs=(VMEM,) * 5,
                input_output_aliases={2: 0},
                compiler_params=PARAMS,
            )(role, scales, *came)
    keep = AGG // members
    coarse_d = restricts.shape[1]
    chunk = (keep, coarse_d, cols)
    pair = (2 * keep, coarse_d, cols)
    smoothed, own, away = pl.pallas_call(
        last_end,
        out_shape=(field, jax.ShapeDtypeStruct(pair, F32), jax.ShapeDtypeStruct(pair, BF16)),
        in_specs=[SMEM] * 3 + [VMEM] * 8,
        out_specs=(VMEM,) * 3,
        scratch_shapes=[pltpu.VMEM((AGG, coarse_d, cols), F32)],
        compiler_params=PARAMS,
    )(role, scales, labels, *came, restricts)
    from_core = lax.ppermute(away, "gz", [(i, i ^ 1) for i in range(members)])
    mine, away = pl.pallas_call(
        coarse_step,
        out_shape=(jax.ShapeDtypeStruct(chunk, F32), jax.ShapeDtypeStruct(chunk, BF16)),
        in_specs=[SMEM] + [VMEM] * 2,
        out_specs=(VMEM,) * 2,
        compiler_params=PARAMS,
    )(role, own, from_core)
    from_chip = lax.ppermute(away, "gz", [(i, i ^ 2) for i in range(members)])
    coarse = mine + from_chip.astype(F32)
    return smoothed.reshape(source.shape), coarse.reshape(1, keep, coarse_d, cols)


def solution(mesh):
    site = P("ta", "gz", None, None, None, None)
    return jax.shard_map(
        shards,
        mesh=mesh,
        in_specs=(site, site, site, P("ta", "gz", None, None, None), P("ta", "gz", None, None), site),
        out_specs=(site, P("ta", "gz", None, None)),
        check_vma=False,
    )
```

time: 158 us -> 128 us (0.81)
  waiting for transfers between devices: 66.1 us -> 17.6 us
  starting transfers between devices: 62.9 us -> 79.1 us
  Pallas kernels: 20.7 us -> 24.1 us
  local copies, waits for them, and re-layouts: 6.16 us -> 4.48 us
    ppermute x12 -> x6, waiting for transfers between devices: 64 us -> 7.79 us  [shifted(): lax.ppermute(block, axis, [((i - distance) % n, i) for i in range(n)])]
    ppermute x3 -> x14, starting transfers between devices: 9.1 us -> 45.5 us  [the longest x3 18.1 us: shards(): at_relay = lax.ppermute(detour, both, out)]
    ppermute x12 -> x6, starting transfers between devices: 53.8 us -> 33.6 us  [shifted(): lax.ppermute(block, axis, [((i - distance) % n, i) for i in range(n)])]
    ppermute x3 -> x14, waiting for transfers between devices: 2.16 us -> 9.85 us  [the longest x3 6.35 us: shards(): at_relay = lax.ppermute(detour, both, out)]
    unnamed x18 -> x12, local copies, waits for them, and re-layouts: 4.52 us -> 1.85 us
    pallas_call x4 -> x5, Pallas kernels: 11.6 us -> 13.3 us  [the longest x2 6.11 us: shards(): pl.pallas_call(sweep_end, out_shape=(wide, field, field, slab, field), in...]
    slice x3, local copies, waits for them, and re-layouts: 0.75 us -> 2.43 us  [shards(): z_next = shifted(vector[:edge], 'gz', -1)]
    pallas_call x3, Pallas kernels: 9.12 us -> 10.8 us  [shards(): pl.pallas_call(functools.partial(local_terms, (zs, xs, ys, d)), out_shape...]
  transfers between devices with their start and end apart: 15 -> 20, of which waited for: 7 -> 6; matrix products, arithmetic and copies ran while one was open for 1% -> 2% of each run, Pallas kernels for 6% -> 8%
where the time goes in v2:
time: 128 us; the launch traced here: 127 us
  starting transfers between devices  79.1 us (62%)
  Pallas kernels  24.1 us (19%)
  waiting for transfers between devices  17.6 us (14%)
  local copies, waits for them, and re-layouts  4.48 us (4%)
    ppermute x6, starting transfers between devices, shifted(): lax.ppermute(block, axis, [((i - distance) % n, i) for i in range(n)])  33.6 us
    ppermute x3, starting transfers between devices, shards(): at_relay = lax.ppermute(detour, both, out)  18.1 us
    ppermute x3, starting transfers between devices, shards(): t_back = lax.ppermute(t_terms, both, forward)  13.7 us
    pallas_call x3, Pallas kernels, shards(): pl.pallas_call(functools.partial(local_terms, (zs, xs, ys, d)), out_shape...  10.8 us
    ppermute x6, waiting for transfers between devices, shifted(): lax.ppermute(block, axis, [((i - distance) % n, i) for i in range(n)])  7.79 us
    ppermute x3, waiting for transfers between devices, shards(): at_relay = lax.ppermute(detour, both, out)  6.35 us
    pallas_call x2, Pallas kernels, shards(): pl.pallas_call(sweep_end, out_shape=(wide, field, field, slab, field), in...  6.11 us
    ppermute x1, starting transfers between devices, shards(): from_chip = lax.ppermute(away, 'gz', [(i, i ^ 2) for i in range(members)])  4.14 us
  transfers between devices with their start and end apart: 20, of which 6 were waited for; matrix products, arithmetic and copies ran while one was open for 2% of the time, Pallas kernels for 8%

profile of v2, /device:TPU:1, one launch (start us, length us, event | category | flops | bytes accessed | tf_op | source)
XLA Modules:
  0.0 127.0 jit_solution(8642043449184193184)
XLA Ops:
  0.6 0.0 copy-start.4
  0.7 0.1 pad_add_fusion.role
  0.7 0.6 copy-done.4
  1.3 0.0 copy-start
  1.3 1.2 copy-done
  2.6 3.8 %shard_map.77 = (bf16[32,64,128]{2,1,0:T(8,128)(2,1)}, bf16[16,64,128]{2,1,0:T(8,128)(2,1)}, bf16[32,64,128]{2,1,0:T(8,128)(2,1)S(1)}) custom-call(s32[2]{0:T(128)S(1)} %pad_add_fusion.role, bf16[1,2,4,4,5]{4,3,2,1,0:T(4,128)(2,1)S(1)} %copy-done.4, bf16[32,64,128]{2,1,0:T(8,128)(2,1)} %bitcast.2.source.estimate.vector, bf16[32,64,256]{2,1,0:T(8,128)(2,1)S(1)} %bitcast.10), custom_call_target="tpu_custom_call" | custom-call | tf_op jit(solution)/shard_map/pallas_call | solution.py:205
  6.3 0.0 copy-start.2
  6.3 12.4 %collective-permute-start.2 = (bf16[32,64,128]{2,1,0:T(8,128)(2,1)S(1)}, bf16[32,64,128]{2,1,0:T(8,128)(2,1)}, u32[]{:S(2)}, u32[]{:S(2)}) collective-permute-start(bf16[32,64,128]{2,1,0:T(8,128)(2,1)S(1)} %get-tuple-element.25), channel_id=1, source_target_pairs={{1,29},{2,126},{3,99},{125,97},{126,2},{127,31},{129,157},{130,254... | collective-permute-start | bytes 1572872 | tf_op jit(solution)/shard_map/ppermute | solution.py:221
  18.8 1.3 %collective-permute-start = (bf16[32,64,128]{2,1,0:T(8,128)(2,1)}, bf16[32,64,128]{2,1,0:T(8,128)(2,1)S(1)}, u32[]{:S(2)}, u32[]{:S(2)}) collective-permute-start(bf16[32,64,128]{2,1,0:T(8,128)(2,1)} %bitcast.2.source.estimate.vector), channel_id=1, source_target_pairs={{0,508},{4,0},{5,1},{6,2},{7,3},{8,4},{9,5},{10,6},{11,7},{12,8},{... | collective-permute-start | bytes 1572872 | tf_op jit(solution)/shard_map/ppermute | solution.py:223
  20.0 4.8 %collective-permute-start.1 = (bf16[32,64,128]{2,1,0:T(8,128)(2,1)}, bf16[32,64,128]{2,1,0:T(8,128)(2,1)}, u32[]{:S(2)}, u32[]{:S(2)}) collective-permute-start(bf16[32,64,128]{2,1,0:T(8,128)(2,1)} %get-tuple-element.24), channel_id=1, source_target_pairs={{0,4},{1,5},{2,6},{3,7},{4,8},{5,9},{6,10},{7,11},{8,12},{9,13},{1... | collective-permute-start | bytes 1572872 | tf_op jit(solution)/shard_map/ppermute | solution.py:222
  24.9 0.0 collective-permute-done.2
  24.9 1.3 %collective-permute-start.3 = (bf16[32,64,128]{2,1,0:T(8,128)(2,1)}, bf16[32,64,128]{2,1,0:T(8,128)(2,1)}, u32[]{:S(2)}, u32[]{:S(2)}) collective-permute-start(bf16[32,64,128]{2,1,0:T(8,128)(2,1)} %collective-permute-done.2), channel_id=1, source_target_pairs={{29,509},{126,510},{99,511},{97,129},{2,130},{31,131},{157,125},{2... | collective-permute-start | bytes 1572872 | tf_op jit(solution)/shard_map/ppermute | solution.py:234
  26.2 9.8 %collective-permute-start.5 = (bf16[16,64,128]{2,1,0:T(8,128)(2,1)}, bf16[16,64,128]{2,1,0:T(8,128)(2,1)S(1)}, u32[]{:S(2)}, u32[]{:S(2)}) collective-permute-start(bf16[16,64,128]{2,1,0:T(8,128)(2,1)} %get-tuple-element.26), channel_id=1, source_target_pairs={{3,0},{0,1},{1,2},{2,3},{7,4},{4,5},{5,6},{6,7},{11,8},{8,9},{9,10... | collective-permute-start | bytes 786440 | tf_op jit(solution)/shard_map/ppermute | solution.py:50
  36.0 1.7 %slice.12 = bf16[1,1,4,4,64,128]{5,4,3,2,1,0:T(8,128)(2,1)} slice(bf16[1,2,4,4,64,128]{5,4,3,2,1,0:T(8,128)(2,1)} %param.6), slice={[0:1], [0:1], [0:4], [0:4], [0:64], [0:128]} | slice | bytes 524288 | tf_op jit(solution)/shard_map/slice | solution.py:224
  37.6 1.9 %collective-permute-start.4 = (bf16[16,64,128]{2,1,0:T(8,128)(2,1)}, bf16[16,64,128]{2,1,0:T(8,128)(2,1)}, u32[]{:S(2)}, u32[]{:S(2)}) collective-permute-start(bf16[16,64,128]{2,1,0:T(8,128)(2,1)} %bitcast.5), channel_id=1, source_target_pairs={{1,0},{2,1},{3,2},{0,3},{5,4},{6,5},{7,6},{4,7},{9,8},{10,9},{11,1... | collective-permute-start | bytes 786440 | tf_op jit(solution)/shard_map/ppermute | solution.py:50
  39.6 0.1 reshape.41.scales
  39.7 0.0 copy-done.1
  39.7 0.0 copy-done.2
  39.7 3.8 %shard_map.78.partial = f32[32,64,128]{2,1,0:T(8,128)S(1)} custom-call(f32[160]{0:T(256)S(1)} %reshape.41.scales, bf16[32,64,128]{2,1,0:T(8,128)(2,1)} %bitcast.2.source.estimate.vector, bf16[32,64,128]{2,1,0:T(8,128)(2,1)} %bitcast.2.source.estimate.vector, bf16[32,64,128]{2,1,0:T(8,128)(2,1)} %bitcast.2.source.estimate.vector, ...), custom_call_target="tpu_custom_call" | custom-call | tf_op jit(solution)/shard_map/pallas_call | solution.py:226
  43.5 2.6 %collective-permute-done.5.z_back = bf16[16,64,128]{2,1,0:T(8,128)(2,1)S(1)} collective-permute-done((bf16[16,64,128]{2,1,0:T(8,128)(2,1)}, bf16[16,64,128]{2,1,0:T(8,128)(2,1)S(1)}, u32[]{:S(2)}, u32[]{:S(2)}) %collective-permute-start.5) | collective-permute-done | bytes 262176 | tf_op jit(solution)/shard_map/ppermute | solution.py:50
  46.1 0.0 collective-permute-done.4.z_next
  46.1 0.0 collective-permute-done.1.t_back
  46.1 0.0 collective-permute-done.t_next
  46.1 0.0 collective-permute-done.3.relayed
  46.1 3.0 %shard_map.79 = (f32[32,64,128]{2,1,0:T(8,128)S(1)}, bf16[32,64,128]{2,1,0:T(8,128)(2,1)S(1)}, bf16[32,64,128]{2,1,0:T(8,128)(2,1)S(1)}, bf16[16,64,128]{2,1,0:T(8,128)(2,1)S(1)}, bf16[32,64,128]{2,1,0:T(8,128)(2,1)S(1)}) custom-call(s32[2]{0:T(128)S(1)} %pad_add_fusion.role, f32[160]{0:T(256)S(1)} %reshape.41.scales, ...), custom_call_target="tpu_custom_call", output_to_operand_aliasing={{0}: (2, {})} | custom-call | tf_op jit(solution)/shard_map/pallas_call | solution.py:237
  49.1 1.3 %collective-permute-start.8 = (bf16[32,64,128]{2,1,0:T(8,128)(2,1)S(1)}, bf16[32,64,128]{2,1,0:T(8,128)(2,1)S(1)}, u32[]{:S(2)}, u32[]{:S(2)}) collective-permute-start(bf16[32,64,128]{2,1,0:T(8,128)(2,1)S(1)} %get-tuple-element.30), channel_id=1, source_target_pairs={{1,29},{2,126},{3,99},{125,97},{126,2},{127,31},{129,157},{130,254... | collective-permute-start | bytes 1572872 | tf_op jit(solution)/shard_map/ppermute | solution.py:221
  50.4 1.3 %collective-permute-start.6 = (bf16[32,64,128]{2,1,0:T(8,128)(2,1)S(1)}, bf16[32,64,128]{2,1,0:T(8,128)(2,1)S(1)}, u32[]{:S(2)}, u32[]{:S(2)}) collective-permute-start(bf16[32,64,128]{2,1,0:T(8,128)(2,1)S(1)} %get-tuple-element.28.vector), channel_id=1, source_target_pairs={{0,508},{4,0},{5,1},{6,2},{7,3},{8,4},{9,5},{10,6},{11,7},{12,8},{... | collective-permute-start | bytes 1572872 | tf_op jit(solution)/shard_map/ppermute | solution.py:223
  51.7 4.0 %collective-permute-start.7 = (bf16[32,64,128]{2,1,0:T(8,128)(2,1)S(1)}, bf16[32,64,128]{2,1,0:T(8,128)(2,1)S(1)}, u32[]{:S(2)}, u32[]{:S(2)}) collective-permute-start(bf16[32,64,128]{2,1,0:T(8,128)(2,1)S(1)} %get-tuple-element.29), channel_id=1, source_target_pairs={{0,4},{1,5},{2,6},{3,7},{4,8},{5,9},{6,10},{7,11},{8,12},{9,13},{1... | collective-permute-start | bytes 1572872 | tf_op jit(solution)/shard_map/ppermute | solution.py:222
  55.7 6.3 %collective-permute-done.8 = bf16[32,64,128]{2,1,0:T(8,128)(2,1)S(1)} collective-permute-done((bf16[32,64,128]{2,1,0:T(8,128)(2,1)S(1)}, bf16[32,64,128]{2,1,0:T(8,128)(2,1)S(1)}, u32[]{:S(2)}, u32[]{:S(2)}) %collective-permute-start.8) | collective-permute-done | bytes 524320 | tf_op jit(solution)/shard_map/ppermute | solution.py:221
  62.1 1.3 %collective-permute-start.9 = (bf16[32,64,128]{2,1,0:T(8,128)(2,1)S(1)}, bf16[32,64,128]{2,1,0:T(8,128)(2,1)S(1)}, u32[]{:S(2)}, u32[]{:S(2)}) collective-permute-start(bf16[32,64,128]{2,1,0:T(8,128)(2,1)S(1)} %collective-permute-done.8), channel_id=1, source_target_pairs={{29,509},{126,510},{99,511},{97,129},{2,130},{31,131},{157,125},{2... | collective-permute-start | bytes 1572872 | tf_op jit(solution)/shard_map/ppermute | solution.py:234
  63.4 1.9 %collective-permute-start.10 = (bf16[16,64,128]{2,1,0:T(8,128)(2,1)S(1)}, bf16[16,64,128]{2,1,0:T(8,128)(2,1)S(1)}, u32[]{:S(2)}, u32[]{:S(2)}) collective-permute-start(bf16[16,64,128]{2,1,0:T(8,128)(2,1)S(1)} %slice.14), channel_id=1, source_target_pairs={{1,0},{2,1},{3,2},{0,3},{5,4},{6,5},{7,6},{4,7},{9,8},{10,9},{11,1... | collective-permute-start | bytes 786440 | tf_op jit(solution)/shard_map/ppermute | solution.py:50
  65.3 7.7 %collective-permute-start.11 = (bf16[16,64,128]{2,1,0:T(8,128)(2,1)S(1)}, bf16[16,64,128]{2,1,0:T(8,128)(2,1)S(1)}, u32[]{:S(2)}, u32[]{:S(2)}) collective-permute-start(bf16[16,64,128]{2,1,0:T(8,128)(2,1)S(1)} %get-tuple-element.31), channel_id=1, source_target_pairs={{3,0},{0,1},{1,2},{2,3},{7,4},{4,5},{5,6},{6,7},{11,8},{8,9},{9,10... | collective-permute-start | bytes 786440 | tf_op jit(solution)/shard_map/ppermute | solution.py:50
  73.1 3.5 %shard_map.80.partial = f32[32,64,128]{2,1,0:T(8,128)S(1)} custom-call(f32[160]{0:T(256)S(1)} %reshape.41.scales, f32[32,64,128]{2,1,0:T(8,128)S(1)} %get-tuple-element.27.estimate, bf16[32,64,128]{2,1,0:T(8,128)(2,1)} %bitcast.2.source.estimate.vector, bf16[32,64,128]{2,1,0:T(8,128)(2,1)S(1)} %get-tuple-element.28.vector, ...), custom_call_target="tpu_custom_call", output_to_operand_aliasing={{}: (1, {})} | custom-call | tf_op jit(solution)/shard_map/pallas_call | solution.py:226
  76.6 0.0 collective-permute-done.10.z_next
  76.6 2.8 %collective-permute-done.11.z_back = bf16[16,64,128]{2,1,0:T(8,128)(2,1)S(1)} collective-permute-done((bf16[16,64,128]{2,1,0:T(8,128)(2,1)S(1)}, bf16[16,64,128]{2,1,0:T(8,128)(2,1)S(1)}, u32[]{:S(2)}, u32[]{:S(2)}) %collective-permute-start.11) | collective-permute-done | bytes 262176 | tf_op jit(solution)/shard_map/ppermute | solution.py:50
  79.3 0.0 collective-permute-done.6.t_next
  79.3 0.0 collective-permute-done.7.t_back
  79.3 0.0 collective-permute-done.9.relayed
  79.3 3.2 %shard_map.81 = (f32[32,64,128]{2,1,0:T(8,128)S(1)}, bf16[32,64,128]{2,1,0:T(8,128)(2,1)S(1)}, bf16[32,64,128]{2,1,0:T(8,128)(2,1)}, bf16[16,64,128]{2,1,0:T(8,128)(2,1)}, bf16[32,64,128]{2,1,0:T(8,128)(2,1)S(1)}) custom-call(s32[2]{0:T(128)S(1)} %pad_add_fusion.role, f32[160]{0:T(256)S(1)} %reshape.41.scales, ...), custom_call_target="tpu_custom_call", output_to_operand_aliasing={{0}: (2, {})} | custom-call | tf_op jit(solution)/shard_map/pallas_call | solution.py:237
  82.5 4.4 %collective-permute-start.14 = (bf16[32,64,128]{2,1,0:T(8,128)(2,1)S(1)}, bf16[32,64,128]{2,1,0:T(8,128)(2,1)}, u32[]{:S(2)}, u32[]{:S(2)}) collective-permute-start(bf16[32,64,128]{2,1,0:T(8,128)(2,1)S(1)} %get-tuple-element.35), channel_id=1, source_target_pairs={{1,29},{2,126},{3,99},{125,97},{126,2},{127,31},{129,157},{130,254... | collective-permute-start | bytes 1572872 | tf_op jit(solution)/shard_map/ppermute | solution.py:221
  86.9 1.3 %collective-permute-start.12 = (bf16[32,64,128]{2,1,0:T(8,128)(2,1)S(1)}, bf16[32,64,128]{2,1,0:T(8,128)(2,1)}, u32[]{:S(2)}, u32[]{:S(2)}) collective-permute-start(bf16[32,64,128]{2,1,0:T(8,128)(2,1)S(1)} %get-tuple-element.33.vector), channel_id=1, source_target_pairs={{0,508},{4,0},{5,1},{6,2},{7,3},{8,4},{9,5},{10,6},{11,7},{12,8},{... | collective-permute-start | bytes 1572872 | tf_op jit(solution)/shard_map/ppermute | solution.py:223
  88.2 4.8 %collective-permute-start.13 = (bf16[32,64,128]{2,1,0:T(8,128)(2,1)}, bf16[32,64,128]{2,1,0:T(8,128)(2,1)}, u32[]{:S(2)}, u32[]{:S(2)}) collective-permute-start(bf16[32,64,128]{2,1,0:T(8,128)(2,1)} %get-tuple-element.34), channel_id=1, source_target_pairs={{0,4},{1,5},{2,6},{3,7},{4,8},{5,9},{6,10},{7,11},{8,12},{9,13},{1... | collective-permute-start | bytes 1572872 | tf_op jit(solution)/shard_map/ppermute | solution.py:222
  93.0 0.0 collective-permute-done.14
  93.0 1.3 %collective-permute-start.15 = (bf16[32,64,128]{2,1,0:T(8,128)(2,1)}, bf16[32,64,128]{2,1,0:T(8,128)(2,1)}, u32[]{:S(2)}, u32[]{:S(2)}) collective-permute-start(bf16[32,64,128]{2,1,0:T(8,128)(2,1)} %collective-permute-done.14), channel_id=1, source_target_pairs={{29,509},{126,510},{99,511},{97,129},{2,130},{31,131},{157,125},{2... | collective-permute-start | bytes 1572872 | tf_op jit(solution)/shard_map/ppermute | solution.py:234
  94.3 0.0 copy-start.5
  94.3 0.7 slice.15
  95.0 2.6 %collective-permute-start.16 = (bf16[16,64,128]{2,1,0:T(8,128)(2,1)}, bf16[16,64,128]{2,1,0:T(8,128)(2,1)S(1)}, u32[]{:S(2)}, u32[]{:S(2)}) collective-permute-start(bf16[16,64,128]{2,1,0:T(8,128)(2,1)} %slice.15), channel_id=1, source_target_pairs={{1,0},{2,1},{3,2},{0,3},{5,4},{6,5},{7,6},{4,7},{9,8},{10,9},{11,1... | collective-permute-start | bytes 786440 | tf_op jit(solution)/shard_map/ppermute | solution.py:50
  97.6 9.6 %collective-permute-start.17 = (bf16[16,64,128]{2,1,0:T(8,128)(2,1)}, bf16[16,64,128]{2,1,0:T(8,128)(2,1)}, u32[]{:S(2)}, u32[]{:S(2)}) collective-permute-start(bf16[16,64,128]{2,1,0:T(8,128)(2,1)} %get-tuple-element.36), channel_id=1, source_target_pairs={{3,0},{0,1},{1,2},{2,3},{7,4},{4,5},{5,6},{6,7},{11,8},{8,9},{9,10... | collective-permute-start | bytes 786440 | tf_op jit(solution)/shard_map/ppermute | solution.py:50
  107.2 0.0 copy-done.5
  107.2 0.1 reshape.35.labels
  107.3 3.5 %shard_map.82.partial = f32[32,64,128]{2,1,0:T(8,128)S(1)} custom-call(f32[160]{0:T(256)S(1)} %reshape.41.scales, f32[32,64,128]{2,1,0:T(8,128)S(1)} %get-tuple-element.32.estimate, bf16[32,64,128]{2,1,0:T(8,128)(2,1)} %bitcast.2.source.estimate.vector, bf16[32,64,128]{2,1,0:T(8,128)(2,1)S(1)} %get-tuple-element.33.vector, ...), custom_call_target="tpu_custom_call", output_to_operand_aliasing={{}: (1, {})} | custom-call | tf_op jit(solution)/shard_map/pallas_call | solution.py:226
  110.8 0.0 collective-permute-done.16.z_next
  110.8 2.4 %collective-permute-done.17.z_back = bf16[16,64,128]{2,1,0:T(8,128)(2,1)} collective-permute-done((bf16[16,64,128]{2,1,0:T(8,128)(2,1)}, bf16[16,64,128]{2,1,0:T(8,128)(2,1)}, u32[]{:S(2)}, u32[]{:S(2)}) %collective-permute-start.17) | collective-permute-done | bytes 262176 | tf_op jit(solution)/shard_map/ppermute | solution.py:50
  113.3 0.0 collective-permute-done.12.t_next
  113.3 0.0 collective-permute-done.13.t_back
  113.3 0.0 collective-permute-done.15.relayed
  113.3 0.0 copy-done.3
  113.3 2.9 %shard_map.83 = (bf16[32,64,128]{2,1,0:T(8,128)(2,1)}, f32[8,64,128]{2,1,0:T(8,128)S(1)}, bf16[8,64,128]{2,1,0:T(8,128)(2,1)S(1)}) custom-call(s32[2]{0:T(128)S(1)} %pad_add_fusion.role, f32[160]{0:T(256)S(1)} %reshape.41.scales, s32[32]{0:T(128)S(1)} %reshape.35.labels, f32[32,64,128]{2,1,0:T(8,128)S(1)} %shard_map.82.partial, ...), custom_call_target="tpu_custom_call" | custom-call | tf_op jit(solution)/shard_map/pallas_call | solution.py:249
  116.2 1.9 %collective-permute-start.18 = (bf16[8,64,128]{2,1,0:T(8,128)(2,1)S(1)}, bf16[8,64,128]{2,1,0:T(8,128)(2,1)S(1)}, u32[]{:S(2)}, u32[]{:S(2)}) collective-permute-start(bf16[8,64,128]{2,1,0:T(8,128)(2,1)S(1)} %get-tuple-element.39), channel_id=1, source_target_pairs={{0,1},{1,0},{2,3},{3,2},{4,5},{5,4},{6,7},{7,6},{8,9},{9,8},{10,11... | collective-permute-start | bytes 393224 | tf_op jit(solution)/shard_map/ppermute | solution.py:257
  118.1 1.3 %collective-permute-done.18.came = bf16[8,64,128]{2,1,0:T(8,128)(2,1)S(1)} collective-permute-done((bf16[8,64,128]{2,1,0:T(8,128)(2,1)S(1)}, bf16[8,64,128]{2,1,0:T(8,128)(2,1)S(1)}, u32[]{:S(2)}, u32[]{:S(2)}) %collective-permute-start.18) | collective-permute-done | bytes 131104 | tf_op jit(solution)/shard_map/ppermute | solution.py:257
  119.4 0.6 shard_map.84
  120.0 4.1 %collective-permute-start.19 = (bf16[4,64,128]{2,1,0:T(8,128)(2,1)S(1)}, bf16[4,64,128]{2,1,0:T(8,128)(2,1)S(1)}, u32[]{:S(2)}, u32[]{:S(2)}) collective-permute-start(bf16[4,64,128]{2,1,0:T(8,128)(2,1)S(1)} %get-tuple-element.41), channel_id=1, source_target_pairs={{0,2},{1,3},{2,0},{3,1},{4,6},{5,7},{6,4},{7,5},{8,10},{9,11},{10,... | collective-permute-start | bytes 196616 | tf_op jit(solution)/shard_map/ppermute | solution.py:265
  124.2 2.2 %collective-permute-done.19 = bf16[4,64,128]{2,1,0:T(8,128)(2,1)S(1)} collective-permute-done((bf16[4,64,128]{2,1,0:T(8,128)(2,1)S(1)}, bf16[4,64,128]{2,1,0:T(8,128)(2,1)S(1)}, u32[]{:S(2)}, u32[]{:S(2)}) %collective-permute-start.19) | collective-permute-done | bytes 65568 | tf_op jit(solution)/shard_map/ppermute | solution.py:265
  126.3 0.7 add_bitcast_fusion
  (3 shorter events, 0.0 us)
Async XLA Ops:
  0.6 0.7 copy-start.4
  1.3 1.2 copy-start
  2.6 37.1 %copy-start.1 = (bf16[1,2,4,4,64,256]{5,4,3,2,1,0:T(8,128)(2,1)S(1)}, bf16[1,2,4,4,64,256]{5,4,3,2,1,0:T(8,128)(2,1)}, u32[]{:S(2)}) copy-start(bf16[1,2,4,4,64,256]{5,4,3,2,1,0:T(8,128)(2,1)} %param.8) | copy-start | bytes 3145732
  6.3 33.3 %copy-start.2 = (bf16[1,2,4,4,64,64]{5,4,3,2,1,0:T(8,128)(2,1)S(1)}, bf16[1,2,4,4,64,64]{5,4,3,2,1,0:T(8,128)(2,1)}, u32[]{:S(2)}) copy-start(bf16[1,2,4,4,64,64]{5,4,3,2,1,0:T(8,128)(2,1)} %param.7) | copy-start | bytes 786436
  6.3 18.5 %collective-permute-start.2 = (bf16[32,64,128]{2,1,0:T(8,128)(2,1)S(1)}, bf16[32,64,128]{2,1,0:T(8,128)(2,1)}, u32[]{:S(2)}, u32[]{:S(2)}) collective-permute-start(bf16[32,64,128]{2,1,0:T(8,128)(2,1)S(1)} %get-tuple-element.25), channel_id=1, source_target_pairs={{1,29},{2,126},{3,99},{125,97},{126,2},{127,31},{129,157},{130,254... | collective-permute-start | bytes 1572872 | tf_op jit(solution)/shard_map/ppermute | solution.py:221
  18.8 27.3 %collective-permute-start = (bf16[32,64,128]{2,1,0:T(8,128)(2,1)}, bf16[32,64,128]{2,1,0:T(8,128)(2,1)S(1)}, u32[]{:S(2)}, u32[]{:S(2)}) collective-permute-start(bf16[32,64,128]{2,1,0:T(8,128)(2,1)} %bitcast.2.source.estimate.vector), channel_id=1, source_target_pairs={{0,508},{4,0},{5,1},{6,2},{7,3},{8,4},{9,5},{10,6},{11,7},{12,8},{... | collective-permute-start | bytes 1572872 | tf_op jit(solution)/shard_map/ppermute | solution.py:223
  20.0 26.0 %collective-permute-start.1 = (bf16[32,64,128]{2,1,0:T(8,128)(2,1)}, bf16[32,64,128]{2,1,0:T(8,128)(2,1)}, u32[]{:S(2)}, u32[]{:S(2)}) collective-permute-start(bf16[32,64,128]{2,1,0:T(8,128)(2,1)} %get-tuple-element.24), channel_id=1, source_target_pairs={{0,4},{1,5},{2,6},{3,7},{4,8},{5,9},{6,10},{7,11},{8,12},{9,13},{1... | collective-permute-start | bytes 1572872 | tf_op jit(solution)/shard_map/ppermute | solution.py:222
  24.9 21.2 %collective-permute-start.3 = (bf16[32,64,128]{2,1,0:T(8,128)(2,1)}, bf16[32,64,128]{2,1,0:T(8,128)(2,1)}, u32[]{:S(2)}, u32[]{:S(2)}) collective-permute-start(bf16[32,64,128]{2,1,0:T(8,128)(2,1)} %collective-permute-done.2), channel_id=1, source_target_pairs={{29,509},{126,510},{99,511},{97,129},{2,130},{31,131},{157,125},{2... | collective-permute-start | bytes 1572872 | tf_op jit(solution)/shard_map/ppermute | solution.py:234
  26.2 19.9 %collective-permute-start.5 = (bf16[16,64,128]{2,1,0:T(8,128)(2,1)}, bf16[16,64,128]{2,1,0:T(8,128)(2,1)S(1)}, u32[]{:S(2)}, u32[]{:S(2)}) collective-permute-start(bf16[16,64,128]{2,1,0:T(8,128)(2,1)} %get-tuple-element.26), channel_id=1, source_target_pairs={{3,0},{0,1},{1,2},{2,3},{7,4},{4,5},{5,6},{6,7},{11,8},{8,9},{9,10... | collective-permute-start | bytes 786440 | tf_op jit(solution)/shard_map/ppermute | solution.py:50
  37.6 8.4 %collective-permute-start.4 = (bf16[16,64,128]{2,1,0:T(8,128)(2,1)}, bf16[16,64,128]{2,1,0:T(8,128)(2,1)}, u32[]{:S(2)}, u32[]{:S(2)}) collective-permute-start(bf16[16,64,128]{2,1,0:T(8,128)(2,1)} %bitcast.5), channel_id=1, source_target_pairs={{1,0},{2,1},{3,2},{0,3},{5,4},{6,5},{7,6},{4,7},{9,8},{10,9},{11,1... | collective-permute-start | bytes 786440 | tf_op jit(solution)/shard_map/ppermute | solution.py:50
  49.1 13.0 %collective-permute-start.8 = (bf16[32,64,128]{2,1,0:T(8,128)(2,1)S(1)}, bf16[32,64,128]{2,1,0:T(8,128)(2,1)S(1)}, u32[]{:S(2)}, u32[]{:S(2)}) collective-permute-start(bf16[32,64,128]{2,1,0:T(8,128)(2,1)S(1)} %get-tuple-element.30), channel_id=1, source_target_pairs={{1,29},{2,126},{3,99},{125,97},{126,2},{127,31},{129,157},{130,254... | collective-permute-start | bytes 1572872 | tf_op jit(solution)/shard_map/ppermute | solution.py:221
  50.4 28.9 %collective-permute-start.6 = (bf16[32,64,128]{2,1,0:T(8,128)(2,1)S(1)}, bf16[32,64,128]{2,1,0:T(8,128)(2,1)S(1)}, u32[]{:S(2)}, u32[]{:S(2)}) collective-permute-start(bf16[32,64,128]{2,1,0:T(8,128)(2,1)S(1)} %get-tuple-element.28.vector), channel_id=1, source_target_pairs={{0,508},{4,0},{5,1},{6,2},{7,3},{8,4},{9,5},{10,6},{11,7},{12,8},{... | collective-permute-start | bytes 1572872 | tf_op jit(solution)/shard_map/ppermute | solution.py:223
  51.7 27.6 %collective-permute-start.7 = (bf16[32,64,128]{2,1,0:T(8,128)(2,1)S(1)}, bf16[32,64,128]{2,1,0:T(8,128)(2,1)S(1)}, u32[]{:S(2)}, u32[]{:S(2)}) collective-permute-start(bf16[32,64,128]{2,1,0:T(8,128)(2,1)S(1)} %get-tuple-element.29), channel_id=1, source_target_pairs={{0,4},{1,5},{2,6},{3,7},{4,8},{5,9},{6,10},{7,11},{8,12},{9,13},{1... | collective-permute-start | bytes 1572872 | tf_op jit(solution)/shard_map/ppermute | solution.py:222
  62.1 17.3 %collective-permute-start.9 = (bf16[32,64,128]{2,1,0:T(8,128)(2,1)S(1)}, bf16[32,64,128]{2,1,0:T(8,128)(2,1)S(1)}, u32[]{:S(2)}, u32[]{:S(2)}) collective-permute-start(bf16[32,64,128]{2,1,0:T(8,128)(2,1)S(1)} %collective-permute-done.8), channel_id=1, source_target_pairs={{29,509},{126,510},{99,511},{97,129},{2,130},{31,131},{157,125},{2... | collective-permute-start | bytes 1572872 | tf_op jit(solution)/shard_map/ppermute | solution.py:234
  63.4 13.2 %collective-permute-start.10 = (bf16[16,64,128]{2,1,0:T(8,128)(2,1)S(1)}, bf16[16,64,128]{2,1,0:T(8,128)(2,1)S(1)}, u32[]{:S(2)}, u32[]{:S(2)}) collective-permute-start(bf16[16,64,128]{2,1,0:T(8,128)(2,1)S(1)} %slice.14), channel_id=1, source_target_pairs={{1,0},{2,1},{3,2},{0,3},{5,4},{6,5},{7,6},{4,7},{9,8},{10,9},{11,1... | collective-permute-start | bytes 786440 | tf_op jit(solution)/shard_map/ppermute | solution.py:50
  65.3 14.0 %collective-permute-start.11 = (bf16[16,64,128]{2,1,0:T(8,128)(2,1)S(1)}, bf16[16,64,128]{2,1,0:T(8,128)(2,1)S(1)}, u32[]{:S(2)}, u32[]{:S(2)}) collective-permute-start(bf16[16,64,128]{2,1,0:T(8,128)(2,1)S(1)} %get-tuple-element.31), channel_id=1, source_target_pairs={{3,0},{0,1},{1,2},{2,3},{7,4},{4,5},{5,6},{6,7},{11,8},{8,9},{9,10... | collective-permute-start | bytes 786440 | tf_op jit(solution)/shard_map/ppermute | solution.py:50
  82.5 10.5 %collective-permute-start.14 = (bf16[32,64,128]{2,1,0:T(8,128)(2,1)S(1)}, bf16[32,64,128]{2,1,0:T(8,128)(2,1)}, u32[]{:S(2)}, u32[]{:S(2)}) collective-permute-start(bf16[32,64,128]{2,1,0:T(8,128)(2,1)S(1)} %get-tuple-element.35), channel_id=1, source_target_pairs={{1,29},{2,126},{3,99},{125,97},{126,2},{127,31},{129,157},{130,254... | collective-permute-start | bytes 1572872 | tf_op jit(solution)/shard_map/ppermute | solution.py:221
  86.9 26.4 %collective-permute-start.12 = (bf16[32,64,128]{2,1,0:T(8,128)(2,1)S(1)}, bf16[32,64,128]{2,1,0:T(8,128)(2,1)}, u32[]{:S(2)}, u32[]{:S(2)}) collective-permute-start(bf16[32,64,128]{2,1,0:T(8,128)(2,1)S(1)} %get-tuple-element.33.vector), channel_id=1, source_target_pairs={{0,508},{4,0},{5,1},{6,2},{7,3},{8,4},{9,5},{10,6},{11,7},{12,8},{... | collective-permute-start | bytes 1572872 | tf_op jit(solution)/shard_map/ppermute | solution.py:223
  88.2 25.1 %collective-permute-start.13 = (bf16[32,64,128]{2,1,0:T(8,128)(2,1)}, bf16[32,64,128]{2,1,0:T(8,128)(2,1)}, u32[]{:S(2)}, u32[]{:S(2)}) collective-permute-start(bf16[32,64,128]{2,1,0:T(8,128)(2,1)} %get-tuple-element.34), channel_id=1, source_target_pairs={{0,4},{1,5},{2,6},{3,7},{4,8},{5,9},{6,10},{7,11},{8,12},{9,13},{1... | collective-permute-start | bytes 1572872 | tf_op jit(solution)/shard_map/ppermute | solution.py:222
  93.0 20.3 %collective-permute-start.15 = (bf16[32,64,128]{2,1,0:T(8,128)(2,1)}, bf16[32,64,128]{2,1,0:T(8,128)(2,1)}, u32[]{:S(2)}, u32[]{:S(2)}) collective-permute-start(bf16[32,64,128]{2,1,0:T(8,128)(2,1)} %collective-permute-done.14), channel_id=1, source_target_pairs={{29,509},{126,510},{99,511},{97,129},{2,130},{31,131},{157,125},{2... | collective-permute-start | bytes 1572872 | tf_op jit(solution)/shard_map/ppermute | solution.py:234
  94.3 12.9 %copy-start.5 = (s32[1,2,4,4]{3,2,1,0:T(4,128)S(1)}, s32[1,2,4,4]{3,2,1,0:T(4,128)}, u32[]{:S(2)}) copy-start(s32[1,2,4,4]{3,2,1,0:T(4,128)} %param.10) | copy-start | bytes 388
  95.0 15.8 %collective-permute-start.16 = (bf16[16,64,128]{2,1,0:T(8,128)(2,1)}, bf16[16,64,128]{2,1,0:T(8,128)(2,1)S(1)}, u32[]{:S(2)}, u32[]{:S(2)}) collective-permute-start(bf16[16,64,128]{2,1,0:T(8,128)(2,1)} %slice.15), channel_id=1, source_target_pairs={{1,0},{2,1},{3,2},{0,3},{5,4},{6,5},{7,6},{4,7},{9,8},{10,9},{11,1... | collective-permute-start | bytes 786440 | tf_op jit(solution)/shard_map/ppermute | solution.py:50
  97.6 15.6 %collective-permute-start.17 = (bf16[16,64,128]{2,1,0:T(8,128)(2,1)}, bf16[16,64,128]{2,1,0:T(8,128)(2,1)}, u32[]{:S(2)}, u32[]{:S(2)}) collective-permute-start(bf16[16,64,128]{2,1,0:T(8,128)(2,1)} %get-tuple-element.36), channel_id=1, source_target_pairs={{3,0},{0,1},{1,2},{2,3},{7,4},{4,5},{5,6},{6,7},{11,8},{8,9},{9,10... | collective-permute-start | bytes 786440 | tf_op jit(solution)/shard_map/ppermute | solution.py:50
  107.3 6.0 %copy-start.3 = (bf16[1,2,4,4,64,64]{5,4,3,2,1,0:T(8,128)(2,1)S(1)}, bf16[1,2,4,4,64,64]{5,4,3,2,1,0:T(8,128)(2,1)}, u32[]{:S(2)}) copy-start(bf16[1,2,4,4,64,64]{5,4,3,2,1,0:T(8,128)(2,1)} %param.11) | copy-start | bytes 786436
  116.2 3.2 %collective-permute-start.18 = (bf16[8,64,128]{2,1,0:T(8,128)(2,1)S(1)}, bf16[8,64,128]{2,1,0:T(8,128)(2,1)S(1)}, u32[]{:S(2)}, u32[]{:S(2)}) collective-permute-start(bf16[8,64,128]{2,1,0:T(8,128)(2,1)S(1)} %get-tuple-element.39), channel_id=1, source_target_pairs={{0,1},{1,0},{2,3},{3,2},{4,5},{5,4},{6,7},{7,6},{8,9},{9,8},{10,11... | collective-permute-start | bytes 393224 | tf_op jit(solution)/shard_map/ppermute | solution.py:257
  120.0 6.3 %collective-permute-start.19 = (bf16[4,64,128]{2,1,0:T(8,128)(2,1)S(1)}, bf16[4,64,128]{2,1,0:T(8,128)(2,1)S(1)}, u32[]{:S(2)}, u32[]{:S(2)}) collective-permute-start(bf16[4,64,128]{2,1,0:T(8,128)(2,1)S(1)} %get-tuple-element.41), channel_id=1, source_target_pairs={{0,2},{1,3},{2,0},{3,1},{4,6},{5,7},{6,4},{7,5},{8,10},{9,11},{10,... | collective-permute-start | bytes 196616 | tf_op jit(solution)/shard_map/ppermute | solution.py:265

commit v3 on v2

--- a/solution.py
+++ b/solution.py
@@ -10,17 +10,15 @@
 ITERS = 3
 OMEGA = 0.5
 AGG = 16
-PIECES = 4
 F32 = jnp.float32
 BF16 = jnp.bfloat16
 VMEM = pl.BlockSpec(memory_space=pltpu.VMEM)
-HBM = pl.BlockSpec(memory_space=pltpu.HBM)
 SMEM = pl.BlockSpec(memory_space=pltpu.SMEM)
 PARAMS = pltpu.CompilerParams(vmem_limit_bytes=12 * 1024 * 1024)
 
 GROUP = 32
-FORWARD_RELAY = {1: 24, 2: 0, 3: 7}
-BACKWARD_RELAY = {1: 7, 2: 31, 3: 24}
+FORWARD_RELAY = {1: 7, 3: 24}
+BACKWARD_RELAY = {1: 24, 3: 7}
 FORWARD_SEAM, BACKWARD_SEAM = 1, 2
 
 
@@ -58,46 +56,6 @@
     return lax.dot_general(a, b, (((0,), (0,)), ((), ())), preferred_element_type=F32)
 
 
-def fill_detour(role, t_terms, vector, detour):
-    @pl.when(role[0] == FORWARD_SEAM)
-    def _():
-        detour[...] = t_terms[...]
-
-    @pl.when(role[0] == BACKWARD_SEAM)
-    def _():
-        detour[...] = vector[...]
-
-
-def first_terms(role, scales, source, hops, t_terms, z_terms, detour, vector, codes, sems):
-    sites, d = vector.shape[:2]
-    xs, ys = scales.shape[2:4]
-    last = sites - z_terms.shape[0]
-    pieces = sems.shape[1]
-    n = sites // pieces
-    copies = []
-    for i in range(pieces):
-        part = pl.ds(i * n, n)
-        copies.append(
-            [
-                pltpu.make_async_copy(hops.at[part, :, pl.ds(2 * d, 2 * d)], codes.at[part], sems.at[0, i]),
-                pltpu.make_async_copy(source.at[part], vector.at[part], sems.at[1, i]),
-            ]
-        )
-    for pair in copies:
-        for copy in pair:
-            copy.start()
-    for s in range(sites):
-        if s % n == 0:
-            for copy in copies[s // n]:
-                copy.wait()
-        z, x, y = s // (xs * ys), s // ys % xs, s % ys
-        scale = scales[0, z, x].astype(F32)
-        t_terms[s] = (scale[y : y + 1, 4:5] * dot_t(codes[s, :, d:], vector[s])).astype(BF16)
-        if s >= last:
-            z_terms[s - last] = (scale[y : y + 1, 3:4] * dot_t(codes[s, :, :d], vector[s])).astype(BF16)
-    fill_detour(role, t_terms, vector, detour)
-
-
 def hop_terms(role, scales, vector, hops, t_terms, z_terms, detour):
     sites, d = vector.shape[:2]
     last = sites - z_terms.shape[0]
@@ -105,7 +63,11 @@
         t_terms[s] = (scales[5 * s + 4] * dot_t(hops[s, :, 3 * d :], vector[s])).astype(BF16)
     for s in range(last, sites):
         z_terms[s - last] = (scales[5 * s + 3] * dot_t(hops[s, :, 2 * d : 3 * d], vector[s])).astype(BF16)
-    fill_detour(role, t_terms, vector, detour)
+    for seam, field in ((FORWARD_SEAM, t_terms), (BACKWARD_SEAM, vector)):
+
+        @pl.when(role[0] == seam)
+        def _():
+            detour[...] = field[...]
 
 
 def local_terms(shape, scales, estimate, source, vector, selfs, hops, partial):
@@ -137,36 +99,42 @@
                 partial[s] = estimate[s].astype(F32) + OMEGA * (source[s].astype(F32) - total)
 
 
-def new_estimate(s, role, scales, partial, t_next, t_back, relayed, z_next, z_back, hops):
+def z_edge_terms(scales, partial, z_next, z_back, hops, done):
     sites, d = partial.shape[:2]
     edge = z_next.shape[0]
     last = sites - edge
+    for s in range(edge):
+        done[s] = partial[s] - OMEGA * z_back[s].astype(F32)
+    for s in range(last, sites):
+        done[s] = partial[s] - OMEGA * scales[5 * s + 3] * dot(hops[s, :, 2 * d : 3 * d], z_next[s - last])
+
+
+def new_estimate(s, role, scales, partial, t_next, t_back, relayed, hops):
+    d = partial.shape[1]
     ahead = jnp.where(role[0] == FORWARD_SEAM, relayed[s], t_next[s])
     behind = jnp.where(role[0] == BACKWARD_SEAM, relayed[s], t_back[s])
     total = scales[5 * s + 4] * dot(hops[s, :, 3 * d :], ahead) + behind.astype(F32)
-    if s >= last:
-        total += scales[5 * s + 3] * dot(hops[s, :, 2 * d : 3 * d], z_next[s - last])
-    if s < edge:
-        total += z_back[s].astype(F32)
     return partial[s] - OMEGA * total
 
 
-def sweep_end(role, scales, partial, t_next, t_back, relayed, z_next, z_back, hops, estimate, vector, *terms):
+def sweep_end(role, scales, partial, t_next, t_back, relayed, hops, estimate, vector, *terms):
     for s in range(vector.shape[0]):
-        e = new_estimate(s, role, scales, partial, t_next, t_back, relayed, z_next, z_back, hops)
+        e = new_estimate(s, role, scales, partial, t_next, t_back, relayed, hops)
         estimate[s] = e
         vector[s] = e.astype(BF16)
     hop_terms(role, scales, vector, hops, *terms)
 
 
-def last_end(role, scales, labels, partial, t_next, t_back, relayed, z_next, z_back, hops, restrictor, vector, own, away, sums):
+def last_end(role, scales, labels, partial, t_next, t_back, relayed, hops, restrictor, vector, own, away, sums):
     half = own.shape[0] // 2
+    xs, ys = labels.shape[2:]
     sums[...] = jnp.zeros_like(sums)
     for s in range(vector.shape[0]):
-        e = new_estimate(s, role, scales, partial, t_next, t_back, relayed, z_next, z_back, hops)
+        e = new_estimate(s, role, scales, partial, t_next, t_back, relayed, hops)
         vector[s] = e.astype(BF16)
     for s in range(vector.shape[0]):
-        sums[labels[s]] += dot(restrictor[s], vector[s])
+        label = labels[0, s // (xs * ys), s // ys % xs, s % ys]
+        sums[label] += dot(restrictor[s], vector[s])
     core = role[1] % 2
     for chip in range(2):
         rows = pl.ds(chip * half, half)
@@ -184,38 +152,31 @@
 
 def shards(source, self_codes, hop_codes, link_scales, restrict_map, restrictor):
     ts, zs, xs, ys, d, cols = source.shape
-    assert ts == 1
+    assert ts == 1 and zs == 2
     sites, edge = zs * xs * ys, xs * ys
     slices, members = lax.axis_size("ta"), lax.axis_size("gz")
     forward, backward, out, back = routes(slices, members)
     t, g = lax.axis_index("ta"), lax.axis_index("gz")
     seam = jnp.where(t % GROUP == GROUP - 1, FORWARD_SEAM, jnp.where(t % GROUP == 0, BACKWARD_SEAM, 0))
-    role = jnp.stack([jnp.where(g == 0, 0, seam), g]).astype(jnp.int32)
+    role = jnp.stack([jnp.where(g % 2 == 1, seam, 0), g]).astype(jnp.int32)
 
     b = source.reshape(sites, d, cols)
     selfs = self_codes.reshape(sites, d, d)
     hops = hop_codes.reshape(sites, d, 4 * d)
     restricts = restrictor.reshape(sites, -1, d)
-    labels = restrict_map.reshape(sites)
     field = jax.ShapeDtypeStruct((sites, d, cols), BF16)
     wide = jax.ShapeDtypeStruct((sites, d, cols), F32)
     slab = jax.ShapeDtypeStruct((edge, d, cols), BF16)
     both = ("ta", "gz")
 
+    scales = link_scales.astype(F32).reshape(sites * 5)
     t_terms, z_terms, detour = pl.pallas_call(
-        first_terms,
+        hop_terms,
         out_shape=(field, slab, field),
-        in_specs=[SMEM, VMEM, HBM, HBM],
+        in_specs=[SMEM] * 2 + [VMEM] * 2,
         out_specs=(VMEM,) * 3,
-        scratch_shapes=[
-            pltpu.VMEM((sites, d, cols), BF16),
-            pltpu.VMEM((sites, d, 2 * d), BF16),
-            pltpu.SemaphoreType.DMA((2, PIECES)),
-        ],
         compiler_params=PARAMS,
-    )(role, link_scales, b, hops)
-    late_scales, t_terms = lax.optimization_barrier((link_scales, t_terms))
-    scales = late_scales.astype(F32).reshape(sites * 5)
+    )(role, scales, b, hops)
     vector, estimate = b, b
     for sweep in range(ITERS):
         at_relay = lax.ppermute(detour, both, out)
@@ -232,12 +193,20 @@
             compiler_params=PARAMS,
         )(scales, estimate, b, vector, selfs, hops)
         relayed = lax.ppermute(at_relay, both, back)
-        came = (partial, t_next, t_back, relayed, z_next, z_back, hops)
+        partial = pl.pallas_call(
+            z_edge_terms,
+            out_shape=wide,
+            in_specs=[SMEM] + [VMEM] * 4,
+            out_specs=VMEM,
+            input_output_aliases={1: 0},
+            compiler_params=PARAMS,
+        )(scales, partial, z_next, z_back, hops)
+        came = (partial, t_next, t_back, relayed, hops)
         if sweep + 1 < ITERS:
             estimate, vector, t_terms, z_terms, detour = pl.pallas_call(
                 sweep_end,
                 out_shape=(wide, field, field, slab, field),
-                in_specs=[SMEM] * 2 + [VMEM] * 7,
+                in_specs=[SMEM] * 2 + [VMEM] * 5,
                 out_specs=(VMEM,) * 5,
                 input_output_aliases={2: 0},
                 compiler_params=PARAMS,
@@ -249,11 +218,11 @@
     smoothed, own, away = pl.pallas_call(
         last_end,
         out_shape=(field, jax.ShapeDtypeStruct(pair, F32), jax.ShapeDtypeStruct(pair, BF16)),
-        in_specs=[SMEM] * 3 + [VMEM] * 8,
+        in_specs=[SMEM] * 3 + [VMEM] * 6,
         out_specs=(VMEM,) * 3,
         scratch_shapes=[pltpu.VMEM((AGG, coarse_d, cols), F32)],
         compiler_params=PARAMS,
-    )(role, scales, labels, *came, restricts)
+    )(role, scales, restrict_map, *came, restricts)
     from_core = lax.ppermute(away, "gz", [(i, i ^ 1) for i in range(members)])
     mine, away = pl.pallas_call(
         coarse_step,

time: 128 us -> 125 us (0.977)
  waiting for transfers between devices: 17.6 us -> 36.7 us
  starting transfers between devices: 79.1 us -> 62.6 us
  Pallas kernels: 24.1 us -> 20.4 us
  local copies, waits for them, and re-layouts: 4.48 us -> 3.13 us
    ppermute x6, waiting for transfers between devices: 7.79 us -> 24.2 us  [shifted(): lax.ppermute(block, axis, [((i - distance) % n, i) for i in range(n)])]
    ppermute x3, starting transfers between devices: 18.1 us -> 9.12 us  [shards(): at_relay = lax.ppermute(detour, both, out)]
    ppermute x3, starting transfers between devices: 13.7 us -> 6.66 us  [shards(): t_back = lax.ppermute(t_terms, both, forward)]
    slice x3, local copies, waits for them, and re-layouts: 2.43 us -> 0.06 us  [shards(): z_next = shifted(vector[:edge], 'gz', -1)]
    ppermute x1, starting transfers between devices: 4.14 us -> 1.92 us  [shards(): from_chip = lax.ppermute(away, 'gz', [(i, i ^ 2) for i in range(members)])]
    pallas_call x3, Pallas kernels: 10.8 us -> 8.83 us  [shards(): pl.pallas_call(functools.partial(local_terms, (zs, xs, ys, d)), out_shape...]
    ppermute x6, starting transfers between devices: 33.6 us -> 35.3 us  [shifted(): lax.ppermute(block, axis, [((i - distance) % n, i) for i in range(n)])]
    pallas_call x2, Pallas kernels: 6.11 us -> 4.66 us  [shards(): pl.pallas_call(sweep_end, out_shape=(wide, field, field, slab, field), in...]
  transfers between devices with their start and end apart: 20 -> 20, of which waited for: 6 -> 8; matrix products, arithmetic and copies ran while one was open for 2% -> 0% of each run, Pallas kernels for 8% -> 9%
where the time goes in v3:
time: 125 us
  starting transfers between devices  62.6 us (50%)
  waiting for transfers between devices  36.7 us (29%)
  Pallas kernels  20.4 us (16%)
  local copies, waits for them, and re-layouts  3.13 us (3%)
    ppermute x6, starting transfers between devices, shifted(): lax.ppermute(block, axis, [((i - distance) % n, i) for i in range(n)])  35.3 us
    ppermute x6, waiting for transfers between devices, shifted(): lax.ppermute(block, axis, [((i - distance) % n, i) for i in range(n)])  24.2 us
    ppermute x3, starting transfers between devices, shards(): at_relay = lax.ppermute(detour, both, out)  9.12 us
    pallas_call x3, Pallas kernels, shards(): pl.pallas_call(functools.partial(local_terms, (zs, xs, ys, d)), out_shape...  8.83 us
    ppermute x3, waiting for transfers between devices, shards(): at_relay = lax.ppermute(detour, both, out)  7.64 us
    ppermute x3, starting transfers between devices, shards(): t_back = lax.ppermute(t_terms, both, forward)  6.66 us
    pallas_call x2, Pallas kernels, shards(): pl.pallas_call(sweep_end, out_shape=(wide, field, field, slab, field), in...  4.66 us
    ppermute x3, starting transfers between devices, shards(): t_next = lax.ppermute(vector, both, backward)  3.88 us
  transfers between devices with their start and end apart: 20, of which 8 were waited for; matrix products, arithmetic and copies ran while one was open for 0% of the time, Pallas kernels for 9%

profile of v3, /device:TPU:1, one launch (start us, length us, event | category | flops | bytes accessed | tf_op | source)
XLA Modules:
  0.0 124.6 jit_solution(217667579488076644)
XLA Ops:
  0.6 0.0 copy-start.6
  0.7 0.7 copy-done.6
  1.3 0.1 reshape.37.scales
  1.5 0.1 pad_add_fusion.role
  1.5 1.2 copy-done
  2.8 1.0 copy-done.2
  3.8 1.7 %shard_map.78 = (bf16[32,64,128]{2,1,0:T(8,128)(2,1)S(1)}, bf16[16,64,128]{2,1,0:T(8,128)(2,1)S(1)}, bf16[32,64,128]{2,1,0:T(8,128)(2,1)S(1)}) custom-call(s32[2]{0:T(128)S(1)} %pad_add_fusion.role, f32[160]{0:T(256)S(1)} %reshape.37.scales, bf16[32,64,128]{2,1,0:T(8,128)(2,1)S(1)} %bitcast.20, bf16[32,64,256]{2,1,0:T(8,128)(2,1)S(1)} %bitcast.10), custom_call_target="tpu_custom_call" | custom-call | tf_op jit(solution)/shard_map/pallas_call | solution.py:173
  5.5 0.0 copy-start.3
  5.5 5.4 %collective-permute-start.4 = (bf16[32,64,128]{2,1,0:T(8,128)(2,1)S(1)}, bf16[32,64,128]{2,1,0:T(8,128)(2,1)S(1)}, u32[]{:S(2)}, u32[]{:S(2)}) collective-permute-start(bf16[32,64,128]{2,1,0:T(8,128)(2,1)S(1)} %get-tuple-element.22), channel_id=1, source_target_pairs={{1,97},{3,31},{125,29},{127,99},{129,225},{131,159},{253,157},{255... | collective-permute-start | bytes 1572872 | tf_op jit(solution)/shard_map/ppermute | solution.py:182
  10.9 1.3 %collective-permute-start.2 = (bf16[32,64,128]{2,1,0:T(8,128)(2,1)S(1)}, bf16[32,64,128]{2,1,0:T(8,128)(2,1)S(1)}, u32[]{:S(2)}, u32[]{:S(2)}) collective-permute-start(bf16[32,64,128]{2,1,0:T(8,128)(2,1)S(1)} %bitcast.21), channel_id=1, source_target_pairs={{0,508},{2,510},{4,0},{5,1},{6,2},{7,3},{8,4},{9,5},{10,6},{11,7},... | collective-permute-start | bytes 1572872 | tf_op jit(solution)/shard_map/ppermute | solution.py:184
  12.2 4.0 %collective-permute-start.3 = (bf16[32,64,128]{2,1,0:T(8,128)(2,1)S(1)}, bf16[32,64,128]{2,1,0:T(8,128)(2,1)S(1)}, u32[]{:S(2)}, u32[]{:S(2)}) collective-permute-start(bf16[32,64,128]{2,1,0:T(8,128)(2,1)S(1)} %get-tuple-element.21), channel_id=1, source_target_pairs={{0,4},{1,5},{2,6},{3,7},{4,8},{5,9},{6,10},{7,11},{8,12},{9,13},{1... | collective-permute-start | bytes 1572872 | tf_op jit(solution)/shard_map/ppermute | solution.py:183
  16.2 0.7 collective-permute-done.4
  16.9 1.3 %collective-permute-start.5 = (bf16[32,64,128]{2,1,0:T(8,128)(2,1)S(1)}, bf16[32,64,128]{2,1,0:T(8,128)(2,1)S(1)}, u32[]{:S(2)}, u32[]{:S(2)}) collective-permute-start(bf16[32,64,128]{2,1,0:T(8,128)(2,1)S(1)} %collective-permute-done.4), channel_id=1, source_target_pairs={{97,509},{31,511},{29,129},{99,131},{225,125},{159,127},{157,257},... | collective-permute-start | bytes 1572872 | tf_op jit(solution)/shard_map/ppermute | solution.py:195
  18.3 11.0 %collective-permute-start = (bf16[16,64,128]{2,1,0:T(8,128)(2,1)S(1)}, bf16[16,64,128]{2,1,0:T(8,128)(2,1)S(1)}, u32[]{:S(2)}, u32[]{:S(2)}) collective-permute-start(bf16[16,64,128]{2,1,0:T(8,128)(2,1)S(1)} %bitcast.31), channel_id=1, source_target_pairs={{1,0},{2,1},{3,2},{0,3},{5,4},{6,5},{7,6},{4,7},{9,8},{10,9},{11,1... | collective-permute-start | bytes 786440 | tf_op jit(solution)/shard_map/ppermute | solution.py:48
  29.2 2.2 %collective-permute-start.1 = (bf16[16,64,128]{2,1,0:T(8,128)(2,1)S(1)}, bf16[16,64,128]{2,1,0:T(8,128)(2,1)S(1)}, u32[]{:S(2)}, u32[]{:S(2)}) collective-permute-start(bf16[16,64,128]{2,1,0:T(8,128)(2,1)S(1)} %get-tuple-element.20), channel_id=1, source_target_pairs={{3,0},{0,1},{1,2},{2,3},{7,4},{4,5},{5,6},{6,7},{11,8},{8,9},{9,10... | collective-permute-start | bytes 786440 | tf_op jit(solution)/shard_map/ppermute | solution.py:48
  31.5 0.0 copy-done.1
  31.5 0.0 copy-done.3
  31.5 3.0 %shard_map.77.partial = f32[32,64,128]{2,1,0:T(8,128)S(1)} custom-call(f32[160]{0:T(256)S(1)} %reshape.37.scales, bf16[32,64,128]{2,1,0:T(8,128)(2,1)S(1)} %bitcast.22, bf16[32,64,128]{2,1,0:T(8,128)(2,1)S(1)} %bitcast.23, bf16[32,64,128]{2,1,0:T(8,128)(2,1)S(1)} %bitcast.24, bf16[32,64,64]{2,1,0:T(8,128)(2,1)S(1)} %bitcast.27, bf16[32,64,256]{2,1,0:T(8,128)(2,1)S(1)} %bitcast.11), custom_call_target="tpu_custom_call" | custom-call | tf_op jit(solution)/shard_map/pallas_call | solution.py:187
  34.4 7.8 %collective-permute-done.z_next = bf16[16,64,128]{2,1,0:T(8,128)(2,1)S(1)} collective-permute-done((bf16[16,64,128]{2,1,0:T(8,128)(2,1)S(1)}, bf16[16,64,128]{2,1,0:T(8,128)(2,1)S(1)}, u32[]{:S(2)}, u32[]{:S(2)}) %collective-permute-start) | collective-permute-done | bytes 262176 | tf_op jit(solution)/shard_map/ppermute | solution.py:48
  42.3 0.0 collective-permute-done.1.z_back
  42.3 0.9 shard_map.79.partial
  43.2 0.0 collective-permute-done.2.t_next
  43.2 0.0 collective-permute-done.3.t_back
  43.2 0.0 collective-permute-done.5.relayed
  43.2 2.3 %shard_map.80 = (f32[32,64,128]{2,1,0:T(8,128)S(1)}, bf16[32,64,128]{2,1,0:T(8,128)(2,1)S(1)}, bf16[32,64,128]{2,1,0:T(8,128)(2,1)S(1)}, bf16[16,64,128]{2,1,0:T(8,128)(2,1)S(1)}, bf16[32,64,128]{2,1,0:T(8,128)(2,1)S(1)}) custom-call(s32[2]{0:T(128)S(1)} %pad_add_fusion.role, f32[160]{0:T(256)S(1)} %reshape.37.scales, ...), custom_call_target="tpu_custom_call", output_to_operand_aliasing={{0}: (2, {})} | custom-call | tf_op jit(solution)/shard_map/pallas_call | solution.py:206
  45.5 2.3 %collective-permute-start.10 = (bf16[32,64,128]{2,1,0:T(8,128)(2,1)S(1)}, bf16[32,64,128]{2,1,0:T(8,128)(2,1)S(1)}, u32[]{:S(2)}, u32[]{:S(2)}) collective-permute-start(bf16[32,64,128]{2,1,0:T(8,128)(2,1)S(1)} %get-tuple-element.27), channel_id=1, source_target_pairs={{1,97},{3,31},{125,29},{127,99},{129,225},{131,159},{253,157},{255... | collective-permute-start | bytes 1572872 | tf_op jit(solution)/shard_map/ppermute | solution.py:182
  47.8 1.3 %collective-permute-start.9 = (bf16[32,64,128]{2,1,0:T(8,128)(2,1)S(1)}, bf16[32,64,128]{2,1,0:T(8,128)(2,1)S(1)}, u32[]{:S(2)}, u32[]{:S(2)}) collective-permute-start(bf16[32,64,128]{2,1,0:T(8,128)(2,1)S(1)} %get-tuple-element.26), channel_id=1, source_target_pairs={{0,4},{1,5},{2,6},{3,7},{4,8},{5,9},{6,10},{7,11},{8,12},{9,13},{1... | collective-permute-start | bytes 1572872 | tf_op jit(solution)/shard_map/ppermute | solution.py:183
  49.1 1.3 %collective-permute-start.8 = (bf16[32,64,128]{2,1,0:T(8,128)(2,1)S(1)}, bf16[32,64,128]{2,1,0:T(8,128)(2,1)S(1)}, u32[]{:S(2)}, u32[]{:S(2)}) collective-permute-start(bf16[32,64,128]{2,1,0:T(8,128)(2,1)S(1)} %get-tuple-element.24.vector), channel_id=1, source_target_pairs={{0,508},{2,510},{4,0},{5,1},{6,2},{7,3},{8,4},{9,5},{10,6},{11,7},... | collective-permute-start | bytes 1572872 | tf_op jit(solution)/shard_map/ppermute | solution.py:184
  50.4 3.4 %collective-permute-done.10 = bf16[32,64,128]{2,1,0:T(8,128)(2,1)S(1)} collective-permute-done((bf16[32,64,128]{2,1,0:T(8,128)(2,1)S(1)}, bf16[32,64,128]{2,1,0:T(8,128)(2,1)S(1)}, u32[]{:S(2)}, u32[]{:S(2)}) %collective-permute-start.10) | collective-permute-done | bytes 524320 | tf_op jit(solution)/shard_map/ppermute | solution.py:182
  53.9 1.3 %collective-permute-start.11 = (bf16[32,64,128]{2,1,0:T(8,128)(2,1)S(1)}, bf16[32,64,128]{2,1,0:T(8,128)(2,1)S(1)}, u32[]{:S(2)}, u32[]{:S(2)}) collective-permute-start(bf16[32,64,128]{2,1,0:T(8,128)(2,1)S(1)} %collective-permute-done.10), channel_id=1, source_target_pairs={{97,509},{31,511},{29,129},{99,131},{225,125},{159,127},{157,257},... | collective-permute-start | bytes 1572872 | tf_op jit(solution)/shard_map/ppermute | solution.py:195
  55.2 11.6 %collective-permute-start.6 = (bf16[16,64,128]{2,1,0:T(8,128)(2,1)S(1)}, bf16[16,64,128]{2,1,0:T(8,128)(2,1)S(1)}, u32[]{:S(2)}, u32[]{:S(2)}) collective-permute-start(bf16[16,64,128]{2,1,0:T(8,128)(2,1)S(1)} %slice.14), channel_id=1, source_target_pairs={{1,0},{2,1},{3,2},{0,3},{5,4},{6,5},{7,6},{4,7},{9,8},{10,9},{11,1... | collective-permute-start | bytes 786440 | tf_op jit(solution)/shard_map/ppermute | solution.py:48
  66.8 1.9 %collective-permute-start.7 = (bf16[16,64,128]{2,1,0:T(8,128)(2,1)S(1)}, bf16[16,64,128]{2,1,0:T(8,128)(2,1)S(1)}, u32[]{:S(2)}, u32[]{:S(2)}) collective-permute-start(bf16[16,64,128]{2,1,0:T(8,128)(2,1)S(1)} %get-tuple-element.25), channel_id=1, source_target_pairs={{3,0},{0,1},{1,2},{2,3},{7,4},{4,5},{5,6},{6,7},{11,8},{8,9},{9,10... | collective-permute-start | bytes 786440 | tf_op jit(solution)/shard_map/ppermute | solution.py:48
  68.7 2.9 %shard_map.81.partial = f32[32,64,128]{2,1,0:T(8,128)S(1)} custom-call(f32[160]{0:T(256)S(1)} %reshape.37.scales, f32[32,64,128]{2,1,0:T(8,128)S(1)} %get-tuple-element.23.estimate, bf16[32,64,128]{2,1,0:T(8,128)(2,1)S(1)} %bitcast.25, bf16[32,64,128]{2,1,0:T(8,128)(2,1)S(1)} %get-tuple-element.24.vector, ...), custom_call_target="tpu_custom_call", output_to_operand_aliasing={{}: (1, {})} | custom-call | tf_op jit(solution)/shard_map/pallas_call | solution.py:187
  71.7 6.2 %collective-permute-done.6.z_next = bf16[16,64,128]{2,1,0:T(8,128)(2,1)S(1)} collective-permute-done((bf16[16,64,128]{2,1,0:T(8,128)(2,1)S(1)}, bf16[16,64,128]{2,1,0:T(8,128)(2,1)S(1)}, u32[]{:S(2)}, u32[]{:S(2)}) %collective-permute-start.6) | collective-permute-done | bytes 262176 | tf_op jit(solution)/shard_map/ppermute | solution.py:48
  77.9 0.0 collective-permute-done.7.z_back
  77.9 0.9 shard_map.82.partial
  78.8 0.0 collective-permute-done.9.t_back
  78.8 0.0 collective-permute-done.8.t_next
  78.8 0.0 collective-permute-done.11.relayed
  78.8 2.3 %shard_map.83 = (f32[32,64,128]{2,1,0:T(8,128)S(1)}, bf16[32,64,128]{2,1,0:T(8,128)(2,1)S(1)}, bf16[32,64,128]{2,1,0:T(8,128)(2,1)S(1)}, bf16[16,64,128]{2,1,0:T(8,128)(2,1)S(1)}, bf16[32,64,128]{2,1,0:T(8,128)(2,1)S(1)}) custom-call(s32[2]{0:T(128)S(1)} %pad_add_fusion.role, f32[160]{0:T(256)S(1)} %reshape.37.scales, ...), custom_call_target="tpu_custom_call", output_to_operand_aliasing={{0}: (2, {})} | custom-call | tf_op jit(solution)/shard_map/pallas_call | solution.py:206
  81.1 1.5 %collective-permute-start.16 = (bf16[32,64,128]{2,1,0:T(8,128)(2,1)S(1)}, bf16[32,64,128]{2,1,0:T(8,128)(2,1)S(1)}, u32[]{:S(2)}, u32[]{:S(2)}) collective-permute-start(bf16[32,64,128]{2,1,0:T(8,128)(2,1)S(1)} %get-tuple-element.32), channel_id=1, source_target_pairs={{1,97},{3,31},{125,29},{127,99},{129,225},{131,159},{253,157},{255... | collective-permute-start | bytes 1572872 | tf_op jit(solution)/shard_map/ppermute | solution.py:182
  82.7 1.3 %collective-permute-start.15 = (bf16[32,64,128]{2,1,0:T(8,128)(2,1)S(1)}, bf16[32,64,128]{2,1,0:T(8,128)(2,1)S(1)}, u32[]{:S(2)}, u32[]{:S(2)}) collective-permute-start(bf16[32,64,128]{2,1,0:T(8,128)(2,1)S(1)} %get-tuple-element.31), channel_id=1, source_target_pairs={{0,4},{1,5},{2,6},{3,7},{4,8},{5,9},{6,10},{7,11},{8,12},{9,13},{1... | collective-permute-start | bytes 1572872 | tf_op jit(solution)/shard_map/ppermute | solution.py:183
  84.0 1.3 %collective-permute-start.14 = (bf16[32,64,128]{2,1,0:T(8,128)(2,1)S(1)}, bf16[32,64,128]{2,1,0:T(8,128)(2,1)S(1)}, u32[]{:S(2)}, u32[]{:S(2)}) collective-permute-start(bf16[32,64,128]{2,1,0:T(8,128)(2,1)S(1)} %get-tuple-element.29.vector), channel_id=1, source_target_pairs={{0,508},{2,510},{4,0},{5,1},{6,2},{7,3},{8,4},{9,5},{10,6},{11,7},... | collective-permute-start | bytes 1572872 | tf_op jit(solution)/shard_map/ppermute | solution.py:184
  85.3 3.4 %collective-permute-done.16 = bf16[32,64,128]{2,1,0:T(8,128)(2,1)S(1)} collective-permute-done((bf16[32,64,128]{2,1,0:T(8,128)(2,1)S(1)}, bf16[32,64,128]{2,1,0:T(8,128)(2,1)S(1)}, u32[]{:S(2)}, u32[]{:S(2)}) %collective-permute-start.16) | collective-permute-done | bytes 524320 | tf_op jit(solution)/shard_map/ppermute | solution.py:182
  88.7 1.3 %collective-permute-start.17 = (bf16[32,64,128]{2,1,0:T(8,128)(2,1)S(1)}, bf16[32,64,128]{2,1,0:T(8,128)(2,1)S(1)}, u32[]{:S(2)}, u32[]{:S(2)}) collective-permute-start(bf16[32,64,128]{2,1,0:T(8,128)(2,1)S(1)} %collective-permute-done.16), channel_id=1, source_target_pairs={{97,509},{31,511},{29,129},{99,131},{225,125},{159,127},{157,257},... | collective-permute-start | bytes 1572872 | tf_op jit(solution)/shard_map/ppermute | solution.py:195
  90.0 6.1 %collective-permute-start.12 = (bf16[16,64,128]{2,1,0:T(8,128)(2,1)S(1)}, bf16[16,64,128]{2,1,0:T(8,128)(2,1)S(1)}, u32[]{:S(2)}, u32[]{:S(2)}) collective-permute-start(bf16[16,64,128]{2,1,0:T(8,128)(2,1)S(1)} %slice.15), channel_id=1, source_target_pairs={{1,0},{2,1},{3,2},{0,3},{5,4},{6,5},{7,6},{4,7},{9,8},{10,9},{11,1... | collective-permute-start | bytes 786440 | tf_op jit(solution)/shard_map/ppermute | solution.py:48
  96.1 2.5 %collective-permute-start.13 = (bf16[16,64,128]{2,1,0:T(8,128)(2,1)S(1)}, bf16[16,64,128]{2,1,0:T(8,128)(2,1)S(1)}, u32[]{:S(2)}, u32[]{:S(2)}) collective-permute-start(bf16[16,64,128]{2,1,0:T(8,128)(2,1)S(1)} %get-tuple-element.30), channel_id=1, source_target_pairs={{3,0},{0,1},{1,2},{2,3},{7,4},{4,5},{5,6},{6,7},{11,8},{8,9},{9,10... | collective-permute-start | bytes 786440 | tf_op jit(solution)/shard_map/ppermute | solution.py:48
  98.6 2.9 %shard_map.84.partial = f32[32,64,128]{2,1,0:T(8,128)S(1)} custom-call(f32[160]{0:T(256)S(1)} %reshape.37.scales, f32[32,64,128]{2,1,0:T(8,128)S(1)} %get-tuple-element.28.estimate, bf16[32,64,128]{2,1,0:T(8,128)(2,1)S(1)} %bitcast.26, bf16[32,64,128]{2,1,0:T(8,128)(2,1)S(1)} %get-tuple-element.29.vector, ...), custom_call_target="tpu_custom_call", output_to_operand_aliasing={{}: (1, {})} | custom-call | tf_op jit(solution)/shard_map/pallas_call | solution.py:187
  101.5 0.0 copy-start.4
  101.6 10.1 %collective-permute-done.12.z_next = bf16[16,64,128]{2,1,0:T(8,128)(2,1)S(1)} collective-permute-done((bf16[16,64,128]{2,1,0:T(8,128)(2,1)S(1)}, bf16[16,64,128]{2,1,0:T(8,128)(2,1)S(1)}, u32[]{:S(2)}, u32[]{:S(2)}) %collective-permute-start.12) | collective-permute-done | bytes 262176 | tf_op jit(solution)/shard_map/ppermute | solution.py:48
  111.7 0.0 collective-permute-done.13.z_back
  111.7 0.9 shard_map.85.partial
  112.5 0.0 collective-permute-done.15.t_back
  112.6 0.0 collective-permute-done.14.t_next
  112.6 0.0 collective-permute-done.17.relayed
  112.6 0.0 copy-done.4
  112.6 0.0 copy-done.5
  112.6 2.1 %shard_map.86 = (bf16[32,64,128]{2,1,0:T(8,128)(2,1)}, f32[8,64,128]{2,1,0:T(8,128)S(1)}, bf16[8,64,128]{2,1,0:T(8,128)(2,1)S(1)}) custom-call(s32[2]{0:T(128)S(1)} %pad_add_fusion.role, f32[160]{0:T(256)S(1)} %reshape.37.scales, s32[1,2,4,4]{3,2,1,0:T(4,128)S(1)} %copy-done.5, f32[32,64,128]{2,1,0:T(8,128)S(1)} %shard_map.85.partial, ...), custom_call_target="tpu_custom_call" | custom-call | tf_op jit(solution)/shard_map/pallas_call | solution.py:218
  114.7 1.9 %collective-permute-start.18 = (bf16[8,64,128]{2,1,0:T(8,128)(2,1)S(1)}, bf16[8,64,128]{2,1,0:T(8,128)(2,1)S(1)}, u32[]{:S(2)}, u32[]{:S(2)}) collective-permute-start(bf16[8,64,128]{2,1,0:T(8,128)(2,1)S(1)} %get-tuple-element.35), channel_id=1, source_target_pairs={{0,1},{1,0},{2,3},{3,2},{4,5},{5,4},{6,7},{7,6},{8,9},{9,8},{10,11... | collective-permute-start | bytes 393224 | tf_op jit(solution)/shard_map/ppermute | solution.py:226
  116.6 1.3 %collective-permute-done.18.came = bf16[8,64,128]{2,1,0:T(8,128)(2,1)S(1)} collective-permute-done((bf16[8,64,128]{2,1,0:T(8,128)(2,1)S(1)}, bf16[8,64,128]{2,1,0:T(8,128)(2,1)S(1)}, u32[]{:S(2)}, u32[]{:S(2)}) %collective-permute-start.18) | collective-permute-done | bytes 131104 | tf_op jit(solution)/shard_map/ppermute | solution.py:226
  117.9 0.6 shard_map.87
  118.5 1.9 %collective-permute-start.19 = (bf16[4,64,128]{2,1,0:T(8,128)(2,1)S(1)}, bf16[4,64,128]{2,1,0:T(8,128)(2,1)S(1)}, u32[]{:S(2)}, u32[]{:S(2)}) collective-permute-start(bf16[4,64,128]{2,1,0:T(8,128)(2,1)S(1)} %get-tuple-element.37), channel_id=1, source_target_pairs={{0,2},{1,3},{2,0},{3,1},{4,6},{5,7},{6,4},{7,5},{8,10},{9,11},{10,... | collective-permute-start | bytes 196616 | tf_op jit(solution)/shard_map/ppermute | solution.py:234
  120.4 3.5 %collective-permute-done.19 = bf16[4,64,128]{2,1,0:T(8,128)(2,1)S(1)} collective-permute-done((bf16[4,64,128]{2,1,0:T(8,128)(2,1)S(1)}, bf16[4,64,128]{2,1,0:T(8,128)(2,1)S(1)}, u32[]{:S(2)}, u32[]{:S(2)}) %collective-permute-start.19) | collective-permute-done | bytes 65568 | tf_op jit(solution)/shard_map/ppermute | solution.py:234
  123.9 0.7 add_bitcast_fusion
  (7 shorter events, 0.1 us)
Async XLA Ops:
  0.6 0.7 copy-start.6
  1.5 1.2 copy-start
  2.8 1.0 copy-start.2
  3.8 27.6 %copy-start.1 = (bf16[1,2,4,4,64,256]{5,4,3,2,1,0:T(8,128)(2,1)S(1)}, bf16[1,2,4,4,64,256]{5,4,3,2,1,0:T(8,128)(2,1)}, u32[]{:S(2)}) copy-start(bf16[1,2,4,4,64,256]{5,4,3,2,1,0:T(8,128)(2,1)} %param.8) | copy-start | bytes 3145732
  5.5 26.0 %copy-start.3 = (bf16[1,2,4,4,64,64]{5,4,3,2,1,0:T(8,128)(2,1)S(1)}, bf16[1,2,4,4,64,64]{5,4,3,2,1,0:T(8,128)(2,1)}, u32[]{:S(2)}) copy-start(bf16[1,2,4,4,64,64]{5,4,3,2,1,0:T(8,128)(2,1)} %param.7) | copy-start | bytes 786436
  5.5 11.4 %collective-permute-start.4 = (bf16[32,64,128]{2,1,0:T(8,128)(2,1)S(1)}, bf16[32,64,128]{2,1,0:T(8,128)(2,1)S(1)}, u32[]{:S(2)}, u32[]{:S(2)}) collective-permute-start(bf16[32,64,128]{2,1,0:T(8,128)(2,1)S(1)} %get-tuple-element.22), channel_id=1, source_target_pairs={{1,97},{3,31},{125,29},{127,99},{129,225},{131,159},{253,157},{255... | collective-permute-start | bytes 1572872 | tf_op jit(solution)/shard_map/ppermute | solution.py:182
  10.9 32.3 %collective-permute-start.2 = (bf16[32,64,128]{2,1,0:T(8,128)(2,1)S(1)}, bf16[32,64,128]{2,1,0:T(8,128)(2,1)S(1)}, u32[]{:S(2)}, u32[]{:S(2)}) collective-permute-start(bf16[32,64,128]{2,1,0:T(8,128)(2,1)S(1)} %bitcast.21), channel_id=1, source_target_pairs={{0,508},{2,510},{4,0},{5,1},{6,2},{7,3},{8,4},{9,5},{10,6},{11,7},... | collective-permute-start | bytes 1572872 | tf_op jit(solution)/shard_map/ppermute | solution.py:184
  12.2 31.0 %collective-permute-start.3 = (bf16[32,64,128]{2,1,0:T(8,128)(2,1)S(1)}, bf16[32,64,128]{2,1,0:T(8,128)(2,1)S(1)}, u32[]{:S(2)}, u32[]{:S(2)}) collective-permute-start(bf16[32,64,128]{2,1,0:T(8,128)(2,1)S(1)} %get-tuple-element.21), channel_id=1, source_target_pairs={{0,4},{1,5},{2,6},{3,7},{4,8},{5,9},{6,10},{7,11},{8,12},{9,13},{1... | collective-permute-start | bytes 1572872 | tf_op jit(solution)/shard_map/ppermute | solution.py:183
  16.9 26.2 %collective-permute-start.5 = (bf16[32,64,128]{2,1,0:T(8,128)(2,1)S(1)}, bf16[32,64,128]{2,1,0:T(8,128)(2,1)S(1)}, u32[]{:S(2)}, u32[]{:S(2)}) collective-permute-start(bf16[32,64,128]{2,1,0:T(8,128)(2,1)S(1)} %collective-permute-done.4), channel_id=1, source_target_pairs={{97,509},{31,511},{29,129},{99,131},{225,125},{159,127},{157,257},... | collective-permute-start | bytes 1572872 | tf_op jit(solution)/shard_map/ppermute | solution.py:195
  18.3 24.0 %collective-permute-start = (bf16[16,64,128]{2,1,0:T(8,128)(2,1)S(1)}, bf16[16,64,128]{2,1,0:T(8,128)(2,1)S(1)}, u32[]{:S(2)}, u32[]{:S(2)}) collective-permute-start(bf16[16,64,128]{2,1,0:T(8,128)(2,1)S(1)} %bitcast.31), channel_id=1, source_target_pairs={{1,0},{2,1},{3,2},{0,3},{5,4},{6,5},{7,6},{4,7},{9,8},{10,9},{11,1... | collective-permute-start | bytes 786440 | tf_op jit(solution)/shard_map/ppermute | solution.py:48
  29.2 13.0 %collective-permute-start.1 = (bf16[16,64,128]{2,1,0:T(8,128)(2,1)S(1)}, bf16[16,64,128]{2,1,0:T(8,128)(2,1)S(1)}, u32[]{:S(2)}, u32[]{:S(2)}) collective-permute-start(bf16[16,64,128]{2,1,0:T(8,128)(2,1)S(1)} %get-tuple-element.20), channel_id=1, source_target_pairs={{3,0},{0,1},{1,2},{2,3},{7,4},{4,5},{5,6},{6,7},{11,8},{8,9},{9,10... | collective-permute-start | bytes 786440 | tf_op jit(solution)/shard_map/ppermute | solution.py:48
  45.5 8.3 %collective-permute-start.10 = (bf16[32,64,128]{2,1,0:T(8,128)(2,1)S(1)}, bf16[32,64,128]{2,1,0:T(8,128)(2,1)S(1)}, u32[]{:S(2)}, u32[]{:S(2)}) collective-permute-start(bf16[32,64,128]{2,1,0:T(8,128)(2,1)S(1)} %get-tuple-element.27), channel_id=1, source_target_pairs={{1,97},{3,31},{125,29},{127,99},{129,225},{131,159},{253,157},{255... | collective-permute-start | bytes 1572872 | tf_op jit(solution)/shard_map/ppermute | solution.py:182
  47.8 31.0 %collective-permute-start.9 = (bf16[32,64,128]{2,1,0:T(8,128)(2,1)S(1)}, bf16[32,64,128]{2,1,0:T(8,128)(2,1)S(1)}, u32[]{:S(2)}, u32[]{:S(2)}) collective-permute-start(bf16[32,64,128]{2,1,0:T(8,128)(2,1)S(1)} %get-tuple-element.26), channel_id=1, source_target_pairs={{0,4},{1,5},{2,6},{3,7},{4,8},{5,9},{6,10},{7,11},{8,12},{9,13},{1... | collective-permute-start | bytes 1572872 | tf_op jit(solution)/shard_map/ppermute | solution.py:183
  49.1 29.6 %collective-permute-start.8 = (bf16[32,64,128]{2,1,0:T(8,128)(2,1)S(1)}, bf16[32,64,128]{2,1,0:T(8,128)(2,1)S(1)}, u32[]{:S(2)}, u32[]{:S(2)}) collective-permute-start(bf16[32,64,128]{2,1,0:T(8,128)(2,1)S(1)} %get-tuple-element.24.vector), channel_id=1, source_target_pairs={{0,508},{2,510},{4,0},{5,1},{6,2},{7,3},{8,4},{9,5},{10,6},{11,7},... | collective-permute-start | bytes 1572872 | tf_op jit(solution)/shard_map/ppermute | solution.py:184
  53.9 24.9 %collective-permute-start.11 = (bf16[32,64,128]{2,1,0:T(8,128)(2,1)S(1)}, bf16[32,64,128]{2,1,0:T(8,128)(2,1)S(1)}, u32[]{:S(2)}, u32[]{:S(2)}) collective-permute-start(bf16[32,64,128]{2,1,0:T(8,128)(2,1)S(1)} %collective-permute-done.10), channel_id=1, source_target_pairs={{97,509},{31,511},{29,129},{99,131},{225,125},{159,127},{157,257},... | collective-permute-start | bytes 1572872 | tf_op jit(solution)/shard_map/ppermute | solution.py:195
  55.2 22.7 %collective-permute-start.6 = (bf16[16,64,128]{2,1,0:T(8,128)(2,1)S(1)}, bf16[16,64,128]{2,1,0:T(8,128)(2,1)S(1)}, u32[]{:S(2)}, u32[]{:S(2)}) collective-permute-start(bf16[16,64,128]{2,1,0:T(8,128)(2,1)S(1)} %slice.14), channel_id=1, source_target_pairs={{1,0},{2,1},{3,2},{0,3},{5,4},{6,5},{7,6},{4,7},{9,8},{10,9},{11,1... | collective-permute-start | bytes 786440 | tf_op jit(solution)/shard_map/ppermute | solution.py:48
  66.8 11.1 %collective-permute-start.7 = (bf16[16,64,128]{2,1,0:T(8,128)(2,1)S(1)}, bf16[16,64,128]{2,1,0:T(8,128)(2,1)S(1)}, u32[]{:S(2)}, u32[]{:S(2)}) collective-permute-start(bf16[16,64,128]{2,1,0:T(8,128)(2,1)S(1)} %get-tuple-element.25), channel_id=1, source_target_pairs={{3,0},{0,1},{1,2},{2,3},{7,4},{4,5},{5,6},{6,7},{11,8},{8,9},{9,10... | collective-permute-start | bytes 786440 | tf_op jit(solution)/shard_map/ppermute | solution.py:48
  81.1 7.6 %collective-permute-start.16 = (bf16[32,64,128]{2,1,0:T(8,128)(2,1)S(1)}, bf16[32,64,128]{2,1,0:T(8,128)(2,1)S(1)}, u32[]{:S(2)}, u32[]{:S(2)}) collective-permute-start(bf16[32,64,128]{2,1,0:T(8,128)(2,1)S(1)} %get-tuple-element.32), channel_id=1, source_target_pairs={{1,97},{3,31},{125,29},{127,99},{129,225},{131,159},{253,157},{255... | collective-permute-start | bytes 1572872 | tf_op jit(solution)/shard_map/ppermute | solution.py:182
  82.7 29.9 %collective-permute-start.15 = (bf16[32,64,128]{2,1,0:T(8,128)(2,1)S(1)}, bf16[32,64,128]{2,1,0:T(8,128)(2,1)S(1)}, u32[]{:S(2)}, u32[]{:S(2)}) collective-permute-start(bf16[32,64,128]{2,1,0:T(8,128)(2,1)S(1)} %get-tuple-element.31), channel_id=1, source_target_pairs={{0,4},{1,5},{2,6},{3,7},{4,8},{5,9},{6,10},{7,11},{8,12},{9,13},{1... | collective-permute-start | bytes 1572872 | tf_op jit(solution)/shard_map/ppermute | solution.py:183
  84.0 28.6 %collective-permute-start.14 = (bf16[32,64,128]{2,1,0:T(8,128)(2,1)S(1)}, bf16[32,64,128]{2,1,0:T(8,128)(2,1)S(1)}, u32[]{:S(2)}, u32[]{:S(2)}) collective-permute-start(bf16[32,64,128]{2,1,0:T(8,128)(2,1)S(1)} %get-tuple-element.29.vector), channel_id=1, source_target_pairs={{0,508},{2,510},{4,0},{5,1},{6,2},{7,3},{8,4},{9,5},{10,6},{11,7},... | collective-permute-start | bytes 1572872 | tf_op jit(solution)/shard_map/ppermute | solution.py:184
  88.7 23.8 %collective-permute-start.17 = (bf16[32,64,128]{2,1,0:T(8,128)(2,1)S(1)}, bf16[32,64,128]{2,1,0:T(8,128)(2,1)S(1)}, u32[]{:S(2)}, u32[]{:S(2)}) collective-permute-start(bf16[32,64,128]{2,1,0:T(8,128)(2,1)S(1)} %collective-permute-done.16), channel_id=1, source_target_pairs={{97,509},{31,511},{29,129},{99,131},{225,125},{159,127},{157,257},... | collective-permute-start | bytes 1572872 | tf_op jit(solution)/shard_map/ppermute | solution.py:195
  90.0 21.6 %collective-permute-start.12 = (bf16[16,64,128]{2,1,0:T(8,128)(2,1)S(1)}, bf16[16,64,128]{2,1,0:T(8,128)(2,1)S(1)}, u32[]{:S(2)}, u32[]{:S(2)}) collective-permute-start(bf16[16,64,128]{2,1,0:T(8,128)(2,1)S(1)} %slice.15), channel_id=1, source_target_pairs={{1,0},{2,1},{3,2},{0,3},{5,4},{6,5},{7,6},{4,7},{9,8},{10,9},{11,1... | collective-permute-start | bytes 786440 | tf_op jit(solution)/shard_map/ppermute | solution.py:48
  96.1 15.5 %collective-permute-start.13 = (bf16[16,64,128]{2,1,0:T(8,128)(2,1)S(1)}, bf16[16,64,128]{2,1,0:T(8,128)(2,1)S(1)}, u32[]{:S(2)}, u32[]{:S(2)}) collective-permute-start(bf16[16,64,128]{2,1,0:T(8,128)(2,1)S(1)} %get-tuple-element.30), channel_id=1, source_target_pairs={{3,0},{0,1},{1,2},{2,3},{7,4},{4,5},{5,6},{6,7},{11,8},{8,9},{9,10... | collective-permute-start | bytes 786440 | tf_op jit(solution)/shard_map/ppermute | solution.py:48
  101.5 11.0 %copy-start.4 = (bf16[1,2,4,4,64,64]{5,4,3,2,1,0:T(8,128)(2,1)S(1)}, bf16[1,2,4,4,64,64]{5,4,3,2,1,0:T(8,128)(2,1)}, u32[]{:S(2)}) copy-start(bf16[1,2,4,4,64,64]{5,4,3,2,1,0:T(8,128)(2,1)} %param.11) | copy-start | bytes 786436
  111.7 0.9 copy-start.5
  114.7 3.2 %collective-permute-start.18 = (bf16[8,64,128]{2,1,0:T(8,128)(2,1)S(1)}, bf16[8,64,128]{2,1,0:T(8,128)(2,1)S(1)}, u32[]{:S(2)}, u32[]{:S(2)}) collective-permute-start(bf16[8,64,128]{2,1,0:T(8,128)(2,1)S(1)} %get-tuple-element.35), channel_id=1, source_target_pairs={{0,1},{1,0},{2,3},{3,2},{4,5},{5,4},{6,7},{7,6},{8,9},{9,8},{10,11... | collective-permute-start | bytes 393224 | tf_op jit(solution)/shard_map/ppermute | solution.py:226
  118.5 5.4 %collective-permute-start.19 = (bf16[4,64,128]{2,1,0:T(8,128)(2,1)S(1)}, bf16[4,64,128]{2,1,0:T(8,128)(2,1)S(1)}, u32[]{:S(2)}, u32[]{:S(2)}) collective-permute-start(bf16[4,64,128]{2,1,0:T(8,128)(2,1)S(1)} %get-tuple-element.37), channel_id=1, source_target_pairs={{0,2},{1,3},{2,0},{3,1},{4,6},{5,7},{6,4},{7,5},{8,10},{9,11},{10,... | collective-permute-start | bytes 196616 | tf_op jit(solution)/shard_map/ppermute | solution.py:234

commit v4 on v3

v4 whole, which is shorter than its diff:
```python
import functools

import jax
import jax.numpy as jnp
from jax import lax
from jax.experimental import pallas as pl
from jax.experimental.pallas import tpu as pltpu
from jax.sharding import PartitionSpec as P

ITERS = 3
OMEGA = 0.5
AGG = 16
F32 = jnp.float32
BF16 = jnp.bfloat16
VMEM = pl.BlockSpec(memory_space=pltpu.VMEM)
SMEM = pl.BlockSpec(memory_space=pltpu.SMEM)
PARAMS = pltpu.CompilerParams(vmem_limit_bytes=12 * 1024 * 1024)

GROUP = 32
FORWARD_RELAY = {1: 7, 3: 24}
BACKWARD_RELAY = {1: 24, 3: 7}


def routes(slices, members):
    inner, outer, out, back = [], [], [], []
    for t in range(slices):
        for g in range(members):
            here, ahead, behind = (((t + k) % slices) * members + g for k in (0, 1, -1))
            first = t // GROUP * GROUP
            inner.append((here, behind if t % 2 else ahead))
            across = ahead if t % 2 else behind
            relays = {GROUP - 1: FORWARD_RELAY, 0: BACKWARD_RELAY}.get(t % GROUP, {})
            if g in relays:
                relay = (first + relays[g]) * members + g
                out.append((here, relay))
                back.append((relay, across))
            else:
                outer.append((here, across))
    return inner, outer, out, back


def dot(a, b):
    return jnp.dot(a, b, preferred_element_type=F32)


def dot_t(a, b):
    return lax.dot_general(a, b, (((0,), (0,)), ((), ())), preferred_element_type=F32)


def either(parity, first, second):
    for value, pair in enumerate(((first, second), (second, first))):
        yield pl.when(parity == value), *pair


def hop_terms(role, scales, vector, hops, outer, inner, z_outer, z_inner, detour):
    sites, d = vector.shape[:2]
    edge = z_inner.shape[0]
    last = sites - edge
    for when, ahead, behind in either(role[2], inner, outer):

        @when
        def _():
            for s in range(sites):
                ahead[s] = (scales[5 * s + 4] * dot_t(hops[s, :, 3 * d :], vector[s])).astype(BF16)
            behind[...] = vector[...]

    for when, ahead, behind in either(role[3], z_inner, z_outer):

        @when
        def _():
            for s in range(last, sites):
                ahead[s - last] = (scales[5 * s + 3] * dot_t(hops[s, :, 2 * d : 3 * d], vector[s])).astype(BF16)
            behind[...] = vector[:edge]

    @pl.when(role[0] != 0)
    def _():
        detour[...] = outer[...]


def local_terms(shape, scales, estimate, source, vector, selfs, hops, partial):
    zs, xs, ys, d = shape

    def at(z, x, y):
        return (z * xs + x % xs) * ys + y % ys

    def fwd(m, s, p):
        return scales[5 * s + m + 1] * dot(hops[s, :, m * d : (m + 1) * d], p)

    def bwd(m, s):
        return scales[5 * s + m + 1] * dot_t(hops[s, :, m * d : (m + 1) * d], vector[s])

    for z in range(zs):
        for x in range(xs):
            for y in range(ys):
                s = at(z, x, y)
                p = vector[s]
                total = p.astype(F32) + scales[5 * s] * dot(selfs[s], p)
                total += fwd(0, s, vector[at(z, x + 1, y)])
                total += fwd(1, s, vector[at(z, x, y + 1)])
                total += bwd(0, at(z, x - 1, y))
                total += bwd(1, at(z, x, y - 1))
                if z + 1 < zs:
                    total += fwd(2, s, vector[at(z + 1, x, y)])
                if z:
                    total += bwd(2, at(z - 1, x, y))
                partial[s] = estimate[s].astype(F32) + OMEGA * (source[s].astype(F32) - total)


def z_edge_terms(role, scales, partial, z_inner, z_outer, hops, done):
    sites, d = partial.shape[:2]
    edge = z_inner.shape[0]
    last = sites - edge
    for when, z_next, z_back in either(role[3], z_inner, z_outer):

        @when
        def _():
            for s in range(edge):
                done[s] = partial[s] - OMEGA * z_back[s].astype(F32)
            for s in range(last, sites):
                term = dot(hops[s, :, 2 * d : 3 * d], z_next[s - last])
                done[s] = partial[s] - OMEGA * scales[5 * s + 3] * term


def new_estimates(role, scales, partial, inner, outer, relayed, hops, store):
    sites, d = partial.shape[:2]
    for when, t_next, t_back in either(role[2], inner, outer):

        @when
        def _():
            for s in range(sites):
                came = [jnp.where(role[0] != 0, relayed[s], ref[s]) if ref is outer else ref[s] for ref in (t_next, t_back)]
                total = scales[5 * s + 4] * dot(hops[s, :, 3 * d :], came[0]) + came[1].astype(F32)
                store(s, partial[s] - OMEGA * total)


def sweep_end(role, scales, partial, inner, outer, relayed, hops, estimate, vector, *messages):
    def store(s, e):
        estimate[s] = e
        vector[s] = e.astype(BF16)

    new_estimates(role, scales, partial, inner, outer, relayed, hops, store)
    hop_terms(role, scales, vector, hops, *messages)


def last_end(role, scales, labels, partial, inner, outer, relayed, hops, restrictor, vector, own, away, sums):
    half = own.shape[0] // 2
    xs, ys = labels.shape[2:]
    sums[...] = jnp.zeros_like(sums)

    def store(s, e):
        vector[s] = e.astype(BF16)

    new_estimates(role, scales, partial, inner, outer, relayed, hops, store)
    for s in range(vector.shape[0]):
        label = labels[0, s // (xs * ys), s // ys % xs, s % ys]
        sums[label] += dot(restrictor[s], vector[s])
    core = role[3]
    for chip in range(2):
        rows = pl.ds(chip * half, half)
        own[rows] = sums[pl.ds((2 * chip + core) * half, half)]
        away[rows] = sums[pl.ds((2 * chip + 1 - core) * half, half)].astype(BF16)


def coarse_step(role, own, came, mine, away):
    half = mine.shape[0]
    chip = role[1] // 2
    here, there = pl.ds(chip * half, half), pl.ds((1 - chip) * half, half)
    mine[...] = own[here] + came[here].astype(F32)
    away[...] = (own[there] + came[there].astype(F32)).astype(BF16)


def shards(source, self_codes, hop_codes, link_scales, restrict_map, restrictor):
    ts, zs, xs, ys, d, cols = source.shape
    assert ts == 1 and zs == 2
    sites, edge = zs * xs * ys, xs * ys
    slices, members = lax.axis_size("ta"), lax.axis_size("gz")
    inner, outer, out, back = routes(slices, members)
    z_inner = [(i, i ^ 1) for i in range(members)]
    z_outer = [(i, (i + 2 * (i % 2) - 1) % members) for i in range(members)]
    t, g = lax.axis_index("ta"), lax.axis_index("gz")
    seam = jnp.logical_or(t % GROUP == GROUP - 1, t % GROUP == 0)
    role = jnp.stack([jnp.logical_and(g % 2 == 1, seam).astype(jnp.int32), g, t % 2, g % 2]).astype(jnp.int32)

    b = source.reshape(sites, d, cols)
    selfs = self_codes.reshape(sites, d, d)
    hops = hop_codes.reshape(sites, d, 4 * d)
    restricts = restrictor.reshape(sites, -1, d)
    field = jax.ShapeDtypeStruct((sites, d, cols), BF16)
    wide = jax.ShapeDtypeStruct((sites, d, cols), F32)
    slab = jax.ShapeDtypeStruct((edge, d, cols), BF16)
    both = ("ta", "gz")

    scales = link_scales.astype(F32).reshape(sites * 5)
    messages = (field, field, slab, slab, field)
    sent = pl.pallas_call(
        hop_terms,
        out_shape=messages,
        in_specs=[SMEM] * 2 + [VMEM] * 2,
        out_specs=(VMEM,) * 5,
        compiler_params=PARAMS,
    )(role, scales, b, hops)
    vector, estimate = b, b
    for sweep in range(ITERS):
        at_relay = lax.ppermute(sent[4], both, out)
        t_outer = lax.ppermute(sent[0], both, outer)
        t_inner = lax.ppermute(sent[1], both, inner)
        from_z_outer = lax.ppermute(sent[2], "gz", z_outer)
        from_z_inner = lax.ppermute(sent[3], "gz", z_inner)
        partial = pl.pallas_call(
            functools.partial(local_terms, (zs, xs, ys, d)),
            out_shape=wide,
            in_specs=[SMEM] + [VMEM] * 5,
            out_specs=VMEM,
            input_output_aliases={1: 0} if sweep else {},
            compiler_params=PARAMS,
        )(scales, estimate, b, vector, selfs, hops)
        relayed = lax.ppermute(at_relay, both, back)
        partial = pl.pallas_call(
            z_edge_terms,
            out_shape=wide,
            in_specs=[SMEM] * 2 + [VMEM] * 4,
            out_specs=VMEM,
            input_output_aliases={2: 0},
            compiler_params=PARAMS,
        )(role, scales, partial, from_z_inner, from_z_outer, hops)
        came = (partial, t_inner, t_outer, relayed, hops)
        if sweep + 1 < ITERS:
            estimate, vector, *sent = pl.pallas_call(
                sweep_end,
                out_shape=(wide, field) + messages,
                in_specs=[SMEM] * 2 + [VMEM] * 5,
                out_specs=(VMEM,) * 7,
                input_output_aliases={2: 0},
                compiler_params=PARAMS,
            )(role, scales, *came)
    keep = AGG // members
    coarse_d = restricts.shape[1]
    chunk = (keep, coarse_d, cols)
    pair = (2 * keep, coarse_d, cols)
    smoothed, own, away = pl.pallas_call(
        last_end,
        out_shape=(field, jax.ShapeDtypeStruct(pair, F32), jax.ShapeDtypeStruct(pair, BF16)),
        in_specs=[SMEM] * 3 + [VMEM] * 6,
        out_specs=(VMEM,) * 3,
        scratch_shapes=[pltpu.VMEM((AGG, coarse_d, cols), F32)],
        compiler_params=PARAMS,
    )(role, scales, restrict_map, *came, restricts)
    from_core = lax.ppermute(away, "gz", [(i, i ^ 1) for i in range(members)])
    mine, away = pl.pallas_call(
        coarse_step,
        out_shape=(jax.ShapeDtypeStruct(chunk, F32), jax.ShapeDtypeStruct(chunk, BF16)),
        in_specs=[SMEM] + [VMEM] * 2,
        out_specs=(VMEM,) * 2,
        compiler_params=PARAMS,
    )(role, own, from_core)
    from_chip = lax.ppermute(away, "gz", [(i, i ^ 2) for i in range(members)])
    coarse = mine + from_chip.astype(F32)
    return smoothed.reshape(source.shape), coarse.reshape(1, keep, coarse_d, cols)


def solution(mesh):
    site = P("ta", "gz", None, None, None, None)
    return jax.shard_map(
        shards,
        mesh=mesh,
        in_specs=(site, site, site, P("ta", "gz", None, None, None), P("ta", "gz", None, None), site),
        out_specs=(site, P("ta", "gz", None, None)),
        check_vma=False,
    )
```

time: 125 us -> 119 us (0.952)
  starting transfers between devices: 62.6 us -> 51.1 us
  waiting for transfers between devices: 36.7 us -> 40.8 us
    ppermute x15, starting transfers between devices: 54.9 us -> 43.5 us  [the longest x3 15.4 us: shards(): from_z_inner = lax.ppermute(sent[3], 'gz', z_inner)]
    ppermute x15, waiting for transfers between devices: 31.8 us -> 36 us  [the longest x3 25.7 us: shards(): from_z_outer = lax.ppermute(sent[2], 'gz', z_outer)]
  transfers between devices with their start and end apart: 20 -> 20, of which waited for: 8 -> 8; matrix products, arithmetic and copies ran while one was open for 0% -> 0% of each run, Pallas kernels for 9% -> 10%
where the time goes in v4:
time: 119 us; the launch traced here: 118 us
  starting transfers between devices  51.1 us (43%)
  waiting for transfers between devices  40.8 us (34%)
  Pallas kernels  21.5 us (18%)
  local copies, waits for them, and re-layouts  3.07 us (3%)
    ppermute x3, waiting for transfers between devices, shards(): from_z_outer = lax.ppermute(sent[2], 'gz', z_outer)  25.7 us
    ppermute x3, starting transfers between devices, shards(): from_z_inner = lax.ppermute(sent[3], 'gz', z_inner)  15.4 us
    ppermute x3, starting transfers between devices, shards(): at_relay = lax.ppermute(sent[4], both, out)  11.9 us
    ppermute x3, waiting for transfers between devices, shards(): at_relay = lax.ppermute(sent[4], both, out)  10.3 us
    pallas_call x3, Pallas kernels, shards(): pl.pallas_call(functools.partial(local_terms, (zs, xs, ys, d)), out_shape...  8.81 us
    ppermute x3, starting transfers between devices, shards(): from_z_outer = lax.ppermute(sent[2], 'gz', z_outer)  8.34 us
    ppermute x3, starting transfers between devices, shards(): t_inner = lax.ppermute(sent[1], both, inner)  5.76 us
    pallas_call x2, Pallas kernels, shards(): pl.pallas_call(sweep_end, out_shape=(wide, field) + messages, in_specs=[S...  5.47 us
  transfers between devices with their start and end apart: 20, of which 8 were waited for; matrix products, arithmetic and copies ran while one was open for 0% of the time, Pallas kernels for 10%

profile of v4, /device:TPU:1, one launch (start us, length us, event | category | flops | bytes accessed | tf_op | source)
XLA Modules:
  0.0 118.3 jit_solution(173842675186974704)
XLA Ops:
  0.7 0.0 copy-start.6
  0.7 0.7 copy-done.6
  1.3 0.1 reshape.37.scales
  1.5 0.1 pad_add_fusion.role
  1.5 0.0 copy-start
  1.5 1.2 %copy-done = bf16[1,2,4,4,64,256]{5,4,3,2,1,0:T(8,128)(2,1)S(1)} copy-done((bf16[1,2,4,4,64,256]{5,4,3,2,1,0:T(8,128)(2,1)S(1)}, bf16[1,2,4,4,64,256]{5,4,3,2,1,0:T(8,128)(2,1)}, u32[]{:S(2)}) %copy-start) | copy-done | bytes 1048600
  2.8 1.0 copy-done.2
  3.8 1.9 %shard_map.78 = (bf16[32,64,128]{2,1,0:T(8,128)(2,1)S(1)}, bf16[32,64,128]{2,1,0:T(8,128)(2,1)S(1)}, bf16[16,64,128]{2,1,0:T(8,128)(2,1)S(1)}, bf16[16,64,128]{2,1,0:T(8,128)(2,1)S(1)}, bf16[32,64,128]{2,1,0:T(8,128)(2,1)S(1)}) custom-call(s32[4]{0:T(128)S(1)} %pad_add_fusion.role, f32[160]{0:T(256)S(1)} %reshape.37.scales, ...), custom_call_target="tpu_custom_call" | custom-call | tf_op jit(solution)/shard_map/pallas_call | solution.py:195
  5.7 5.2 %collective-permute-start.4 = (bf16[32,64,128]{2,1,0:T(8,128)(2,1)S(1)}, bf16[32,64,128]{2,1,0:T(8,128)(2,1)S(1)}, u32[]{:S(2)}, u32[]{:S(2)}) collective-permute-start(bf16[32,64,128]{2,1,0:T(8,128)(2,1)S(1)} %get-tuple-element.30), channel_id=1, source_target_pairs={{1,97},{3,31},{125,29},{127,99},{129,225},{131,159},{253,157},{255... | collective-permute-start | bytes 1572872 | tf_op jit(solution)/shard_map/ppermute | solution.py:204
  10.9 1.9 %collective-permute-start.2 = (bf16[32,64,128]{2,1,0:T(8,128)(2,1)S(1)}, bf16[32,64,128]{2,1,0:T(8,128)(2,1)S(1)}, u32[]{:S(2)}, u32[]{:S(2)}) collective-permute-start(bf16[32,64,128]{2,1,0:T(8,128)(2,1)S(1)} %get-tuple-element.28), channel_id=1, source_target_pairs={{0,4},{1,5},{2,6},{3,7},{4,0},{5,1},{6,2},{7,3},{8,12},{9,13},{10,... | collective-permute-start | bytes 1572872 | tf_op jit(solution)/shard_map/ppermute | solution.py:206
  12.8 0.7 collective-permute-start.3
  13.6 3.4 %collective-permute-done.4 = bf16[32,64,128]{2,1,0:T(8,128)(2,1)S(1)} collective-permute-done((bf16[32,64,128]{2,1,0:T(8,128)(2,1)S(1)}, bf16[32,64,128]{2,1,0:T(8,128)(2,1)S(1)}, u32[]{:S(2)}, u32[]{:S(2)}) %collective-permute-start.4) | collective-permute-done | bytes 524320 | tf_op jit(solution)/shard_map/ppermute | solution.py:204
  17.0 1.3 %collective-permute-start.5 = (bf16[32,64,128]{2,1,0:T(8,128)(2,1)S(1)}, bf16[32,64,128]{2,1,0:T(8,128)(2,1)S(1)}, u32[]{:S(2)}, u32[]{:S(2)}) collective-permute-start(bf16[32,64,128]{2,1,0:T(8,128)(2,1)S(1)} %collective-permute-done.4), channel_id=1, source_target_pairs={{97,509},{31,511},{29,129},{99,131},{225,125},{159,127},{157,257},... | collective-permute-start | bytes 1572872 | tf_op jit(solution)/shard_map/ppermute | solution.py:217
  18.3 11.5 %collective-permute-start = (bf16[16,64,128]{2,1,0:T(8,128)(2,1)S(1)}, bf16[16,64,128]{2,1,0:T(8,128)(2,1)S(1)}, u32[]{:S(2)}, u32[]{:S(2)}) collective-permute-start(bf16[16,64,128]{2,1,0:T(8,128)(2,1)S(1)} %get-tuple-element.26), channel_id=1, source_target_pairs={{0,1},{1,0},{2,3},{3,2},{4,5},{5,4},{6,7},{7,6},{8,9},{9,8},{10,11... | collective-permute-start | bytes 786440 | tf_op jit(solution)/shard_map/ppermute | solution.py:208
  29.8 2.2 %collective-permute-start.1 = (bf16[16,64,128]{2,1,0:T(8,128)(2,1)S(1)}, bf16[16,64,128]{2,1,0:T(8,128)(2,1)S(1)}, u32[]{:S(2)}, u32[]{:S(2)}) collective-permute-start(bf16[16,64,128]{2,1,0:T(8,128)(2,1)S(1)} %get-tuple-element.27), channel_id=1, source_target_pairs={{0,3},{1,2},{2,1},{3,0},{4,7},{5,6},{6,5},{7,4},{8,11},{9,10},{10,... | collective-permute-start | bytes 786440 | tf_op jit(solution)/shard_map/ppermute | solution.py:207
  32.0 0.0 copy-done.1
  32.0 0.0 copy-done.3
  32.0 3.0 %shard_map.77.partial = f32[32,64,128]{2,1,0:T(8,128)S(1)} custom-call(f32[160]{0:T(256)S(1)} %reshape.37.scales, bf16[32,64,128]{2,1,0:T(8,128)(2,1)S(1)} %bitcast.22, bf16[32,64,128]{2,1,0:T(8,128)(2,1)S(1)} %bitcast.23, bf16[32,64,128]{2,1,0:T(8,128)(2,1)S(1)} %bitcast.24, bf16[32,64,64]{2,1,0:T(8,128)(2,1)S(1)} %bitcast.27, bf16[32,64,256]{2,1,0:T(8,128)(2,1)S(1)} %bitcast.12), custom_call_target="tpu_custom_call" | custom-call | tf_op jit(solution)/shard_map/pallas_call | solution.py:209
  35.0 0.0 collective-permute-done.z_inner
  35.0 9.5 %collective-permute-done.1.z_outer = bf16[16,64,128]{2,1,0:T(8,128)(2,1)S(1)} collective-permute-done((bf16[16,64,128]{2,1,0:T(8,128)(2,1)S(1)}, bf16[16,64,128]{2,1,0:T(8,128)(2,1)S(1)}, u32[]{:S(2)}, u32[]{:S(2)}) %collective-permute-start.1) | collective-permute-done | bytes 262176 | tf_op jit(solution)/shard_map/ppermute | solution.py:207
  44.5 0.9 shard_map.79.partial
  45.4 0.0 collective-permute-done.2.inner
  45.4 0.0 collective-permute-done.3.outer
  45.4 0.0 collective-permute-done.5.relayed
  45.4 2.6 %shard_map.80 = (f32[32,64,128]{2,1,0:T(8,128)S(1)}, bf16[32,64,128]{2,1,0:T(8,128)(2,1)S(1)}, bf16[32,64,128]{2,1,0:T(8,128)(2,1)S(1)}, bf16[32,64,128]{2,1,0:T...) custom-call(s32[4]{0:T(128)S(1)} %pad_add_fusion.role, ...), custom_call_target="tpu_custom_call", output_to_operand_aliasing={{0}: (2, {})} | custom-call | tf_op jit(solution)/shard_map/pallas_call | solution.py:228
  48.1 1.3 %collective-permute-start.10 = (bf16[32,64,128]{2,1,0:T(8,128)(2,1)S(1)}, bf16[32,64,128]{2,1,0:T(8,128)(2,1)S(1)}, u32[]{:S(2)}, u32[]{:S(2)}) collective-permute-start(bf16[32,64,128]{2,1,0:T(8,128)(2,1)S(1)} %get-tuple-element.37), channel_id=1, source_target_pairs={{1,97},{3,31},{125,29},{127,99},{129,225},{131,159},{253,157},{255... | collective-permute-start | bytes 1572872 | tf_op jit(solution)/shard_map/ppermute | solution.py:204
  49.4 1.9 %collective-permute-start.8 = (bf16[32,64,128]{2,1,0:T(8,128)(2,1)S(1)}, bf16[32,64,128]{2,1,0:T(8,128)(2,1)S(1)}, u32[]{:S(2)}, u32[]{:S(2)}) collective-permute-start(bf16[32,64,128]{2,1,0:T(8,128)(2,1)S(1)} %get-tuple-element.35), channel_id=1, source_target_pairs={{0,4},{1,5},{2,6},{3,7},{4,0},{5,1},{6,2},{7,3},{8,12},{9,13},{10,... | collective-permute-start | bytes 1572872 | tf_op jit(solution)/shard_map/ppermute | solution.py:206
  51.3 0.7 collective-permute-start.9
  52.0 3.4 %collective-permute-done.10 = bf16[32,64,128]{2,1,0:T(8,128)(2,1)S(1)} collective-permute-done((bf16[32,64,128]{2,1,0:T(8,128)(2,1)S(1)}, bf16[32,64,128]{2,1,0:T(8,128)(2,1)S(1)}, u32[]{:S(2)}, u32[]{:S(2)}) %collective-permute-start.10) | collective-permute-done | bytes 524320 | tf_op jit(solution)/shard_map/ppermute | solution.py:204
  55.5 1.3 %collective-permute-start.11 = (bf16[32,64,128]{2,1,0:T(8,128)(2,1)S(1)}, bf16[32,64,128]{2,1,0:T(8,128)(2,1)S(1)}, u32[]{:S(2)}, u32[]{:S(2)}) collective-permute-start(bf16[32,64,128]{2,1,0:T(8,128)(2,1)S(1)} %collective-permute-done.10), channel_id=1, source_target_pairs={{97,509},{31,511},{29,129},{99,131},{225,125},{159,127},{157,257},... | collective-permute-start | bytes 1572872 | tf_op jit(solution)/shard_map/ppermute | solution.py:217
  56.8 1.9 %collective-permute-start.6 = (bf16[16,64,128]{2,1,0:T(8,128)(2,1)S(1)}, bf16[16,64,128]{2,1,0:T(8,128)(2,1)S(1)}, u32[]{:S(2)}, u32[]{:S(2)}) collective-permute-start(bf16[16,64,128]{2,1,0:T(8,128)(2,1)S(1)} %get-tuple-element.33), channel_id=1, source_target_pairs={{0,1},{1,0},{2,3},{3,2},{4,5},{5,4},{6,7},{7,6},{8,9},{9,8},{10,11... | collective-permute-start | bytes 786440 | tf_op jit(solution)/shard_map/ppermute | solution.py:208
  58.7 2.8 %collective-permute-start.7 = (bf16[16,64,128]{2,1,0:T(8,128)(2,1)S(1)}, bf16[16,64,128]{2,1,0:T(8,128)(2,1)S(1)}, u32[]{:S(2)}, u32[]{:S(2)}) collective-permute-start(bf16[16,64,128]{2,1,0:T(8,128)(2,1)S(1)} %get-tuple-element.34), channel_id=1, source_target_pairs={{0,3},{1,2},{2,1},{3,0},{4,7},{5,6},{6,5},{7,4},{8,11},{9,10},{10,... | collective-permute-start | bytes 786440 | tf_op jit(solution)/shard_map/ppermute | solution.py:207
  61.5 2.9 %shard_map.81.partial = f32[32,64,128]{2,1,0:T(8,128)S(1)} custom-call(f32[160]{0:T(256)S(1)} %reshape.37.scales, f32[32,64,128]{2,1,0:T(8,128)S(1)} %get-tuple-element.31.estimate, bf16[32,64,128]{2,1,0:T(8,128)(2,1)S(1)} %bitcast.25, bf16[32,64,128]{2,1,0:T(8,128)(2,1)S(1)} %get-tuple-element.32.vector, ...), custom_call_target="tpu_custom_call", output_to_operand_aliasing={{}: (1, {})} | custom-call | tf_op jit(solution)/shard_map/pallas_call | solution.py:209
  64.4 0.0 collective-permute-done.6.z_inner
  64.4 6.7 %collective-permute-done.7.z_outer = bf16[16,64,128]{2,1,0:T(8,128)(2,1)S(1)} collective-permute-done((bf16[16,64,128]{2,1,0:T(8,128)(2,1)S(1)}, bf16[16,64,128]{2,1,0:T(8,128)(2,1)S(1)}, u32[]{:S(2)}, u32[]{:S(2)}) %collective-permute-start.7) | collective-permute-done | bytes 262176 | tf_op jit(solution)/shard_map/ppermute | solution.py:207
  71.1 0.9 shard_map.82.partial
  72.0 0.0 collective-permute-done.8.inner
  72.0 0.0 collective-permute-done.9.outer
  72.0 0.0 collective-permute-done.11.relayed
  72.1 2.8 %shard_map.83 = (f32[32,64,128]{2,1,0:T(8,128)S(1)}, bf16[32,64,128]{2,1,0:T(8,128)(2,1)S(1)}, bf16[32,64,128]{2,1,0:T(8,128)(2,1)S(1)}, bf16[32,64,128]{2,1,0:T...) custom-call(s32[4]{0:T(128)S(1)} %pad_add_fusion.role, ...), custom_call_target="tpu_custom_call", output_to_operand_aliasing={{0}: (2, {})} | custom-call | tf_op jit(solution)/shard_map/pallas_call | solution.py:228
  74.9 5.4 %collective-permute-start.16 = (bf16[32,64,128]{2,1,0:T(8,128)(2,1)S(1)}, bf16[32,64,128]{2,1,0:T(8,128)(2,1)S(1)}, u32[]{:S(2)}, u32[]{:S(2)}) collective-permute-start(bf16[32,64,128]{2,1,0:T(8,128)(2,1)S(1)} %get-tuple-element.44), channel_id=1, source_target_pairs={{1,97},{3,31},{125,29},{127,99},{129,225},{131,159},{253,157},{255... | collective-permute-start | bytes 1572872 | tf_op jit(solution)/shard_map/ppermute | solution.py:204
  80.3 1.9 %collective-permute-start.14 = (bf16[32,64,128]{2,1,0:T(8,128)(2,1)S(1)}, bf16[32,64,128]{2,1,0:T(8,128)(2,1)S(1)}, u32[]{:S(2)}, u32[]{:S(2)}) collective-permute-start(bf16[32,64,128]{2,1,0:T(8,128)(2,1)S(1)} %get-tuple-element.42), channel_id=1, source_target_pairs={{0,4},{1,5},{2,6},{3,7},{4,0},{5,1},{6,2},{7,3},{8,12},{9,13},{10,... | collective-permute-start | bytes 1572872 | tf_op jit(solution)/shard_map/ppermute | solution.py:206
  82.2 0.7 collective-permute-start.15
  82.9 3.4 %collective-permute-done.16 = bf16[32,64,128]{2,1,0:T(8,128)(2,1)S(1)} collective-permute-done((bf16[32,64,128]{2,1,0:T(8,128)(2,1)S(1)}, bf16[32,64,128]{2,1,0:T(8,128)(2,1)S(1)}, u32[]{:S(2)}, u32[]{:S(2)}) %collective-permute-start.16) | collective-permute-done | bytes 524320 | tf_op jit(solution)/shard_map/ppermute | solution.py:204
  86.4 1.3 %collective-permute-start.17 = (bf16[32,64,128]{2,1,0:T(8,128)(2,1)S(1)}, bf16[32,64,128]{2,1,0:T(8,128)(2,1)S(1)}, u32[]{:S(2)}, u32[]{:S(2)}) collective-permute-start(bf16[32,64,128]{2,1,0:T(8,128)(2,1)S(1)} %collective-permute-done.16), channel_id=1, source_target_pairs={{97,509},{31,511},{29,129},{99,131},{225,125},{159,127},{157,257},... | collective-permute-start | bytes 1572872 | tf_op jit(solution)/shard_map/ppermute | solution.py:217
  87.7 1.9 %collective-permute-start.12 = (bf16[16,64,128]{2,1,0:T(8,128)(2,1)S(1)}, bf16[16,64,128]{2,1,0:T(8,128)(2,1)S(1)}, u32[]{:S(2)}, u32[]{:S(2)}) collective-permute-start(bf16[16,64,128]{2,1,0:T(8,128)(2,1)S(1)} %get-tuple-element.40), channel_id=1, source_target_pairs={{0,1},{1,0},{2,3},{3,2},{4,5},{5,4},{6,7},{7,6},{8,9},{9,8},{10,11... | collective-permute-start | bytes 786440 | tf_op jit(solution)/shard_map/ppermute | solution.py:208
  89.6 3.3 %collective-permute-start.13 = (bf16[16,64,128]{2,1,0:T(8,128)(2,1)S(1)}, bf16[16,64,128]{2,1,0:T(8,128)(2,1)S(1)}, u32[]{:S(2)}, u32[]{:S(2)}) collective-permute-start(bf16[16,64,128]{2,1,0:T(8,128)(2,1)S(1)} %get-tuple-element.41), channel_id=1, source_target_pairs={{0,3},{1,2},{2,1},{3,0},{4,7},{5,6},{6,5},{7,4},{8,11},{9,10},{10,... | collective-permute-start | bytes 786440 | tf_op jit(solution)/shard_map/ppermute | solution.py:207
  92.9 2.9 %shard_map.84.partial = f32[32,64,128]{2,1,0:T(8,128)S(1)} custom-call(f32[160]{0:T(256)S(1)} %reshape.37.scales, f32[32,64,128]{2,1,0:T(8,128)S(1)} %get-tuple-element.38.estimate, bf16[32,64,128]{2,1,0:T(8,128)(2,1)S(1)} %bitcast.26, bf16[32,64,128]{2,1,0:T(8,128)(2,1)S(1)} %get-tuple-element.39.vector, ...), custom_call_target="tpu_custom_call", output_to_operand_aliasing={{}: (1, {})} | custom-call | tf_op jit(solution)/shard_map/pallas_call | solution.py:209
  95.9 0.0 copy-start.4
  95.9 0.0 collective-permute-done.12.z_inner
  95.9 9.4 %collective-permute-done.13.z_outer = bf16[16,64,128]{2,1,0:T(8,128)(2,1)S(1)} collective-permute-done((bf16[16,64,128]{2,1,0:T(8,128)(2,1)S(1)}, bf16[16,64,128]{2,1,0:T(8,128)(2,1)S(1)}, u32[]{:S(2)}, u32[]{:S(2)}) %collective-permute-start.13) | collective-permute-done | bytes 262176 | tf_op jit(solution)/shard_map/ppermute | solution.py:207
  105.3 0.9 shard_map.85.partial
  106.2 0.0 collective-permute-done.14.inner
  106.2 0.0 collective-permute-done.15.outer
  106.2 0.0 collective-permute-done.17.relayed
  106.3 0.0 copy-done.4
  106.3 0.0 copy-done.5
  106.3 2.1 %shard_map.86 = (bf16[32,64,128]{2,1,0:T(8,128)(2,1)}, f32[8,64,128]{2,1,0:T(8,128)S(1)}, bf16[8,64,128]{2,1,0:T(8,128)(2,1)S(1)}) custom-call(s32[4]{0:T(128)S(1)} %pad_add_fusion.role, f32[160]{0:T(256)S(1)} %reshape.37.scales, s32[1,2,4,4]{3,2,1,0:T(4,128)S(1)} %copy-done.5, f32[32,64,128]{2,1,0:T(8,128)S(1)} %shard_map.85.partial, ...), custom_call_target="tpu_custom_call" | custom-call | tf_op jit(solution)/shard_map/pallas_call | solution.py:240
  108.4 1.9 %collective-permute-start.18 = (bf16[8,64,128]{2,1,0:T(8,128)(2,1)S(1)}, bf16[8,64,128]{2,1,0:T(8,128)(2,1)S(1)}, u32[]{:S(2)}, u32[]{:S(2)}) collective-permute-start(bf16[8,64,128]{2,1,0:T(8,128)(2,1)S(1)} %get-tuple-element.47), channel_id=1, source_target_pairs={{0,1},{1,0},{2,3},{3,2},{4,5},{5,4},{6,7},{7,6},{8,9},{9,8},{10,11... | collective-permute-start | bytes 393224 | tf_op jit(solution)/shard_map/ppermute | solution.py:248
  110.3 1.3 %collective-permute-done.18.came = bf16[8,64,128]{2,1,0:T(8,128)(2,1)S(1)} collective-permute-done((bf16[8,64,128]{2,1,0:T(8,128)(2,1)S(1)}, bf16[8,64,128]{2,1,0:T(8,128)(2,1)S(1)}, u32[]{:S(2)}, u32[]{:S(2)}) %collective-permute-start.18) | collective-permute-done | bytes 131104 | tf_op jit(solution)/shard_map/ppermute | solution.py:248
  111.6 0.6 shard_map.87
  112.2 1.9 %collective-permute-start.19 = (bf16[4,64,128]{2,1,0:T(8,128)(2,1)S(1)}, bf16[4,64,128]{2,1,0:T(8,128)(2,1)S(1)}, u32[]{:S(2)}, u32[]{:S(2)}) collective-permute-start(bf16[4,64,128]{2,1,0:T(8,128)(2,1)S(1)} %get-tuple-element.49), channel_id=1, source_target_pairs={{0,2},{1,3},{2,0},{3,1},{4,6},{5,7},{6,4},{7,5},{8,10},{9,11},{10,... | collective-permute-start | bytes 196616 | tf_op jit(solution)/shard_map/ppermute | solution.py:256
  114.2 3.5 %collective-permute-done.19 = bf16[4,64,128]{2,1,0:T(8,128)(2,1)S(1)} collective-permute-done((bf16[4,64,128]{2,1,0:T(8,128)(2,1)S(1)}, bf16[4,64,128]{2,1,0:T(8,128)(2,1)S(1)}, u32[]{:S(2)}, u32[]{:S(2)}) %collective-permute-start.19) | collective-permute-done | bytes 65568 | tf_op jit(solution)/shard_map/ppermute | solution.py:256
  117.7 0.7 add_bitcast_fusion
  (4 shorter events, 0.0 us)
Async XLA Ops:
  0.7 0.7 copy-start.6
  1.5 1.2 %copy-start = (bf16[1,2,4,4,64,256]{5,4,3,2,1,0:T(8,128)(2,1)S(1)}, bf16[1,2,4,4,64,256]{5,4,3,2,1,0:T(8,128)(2,1)}, u32[]{:S(2)}) copy-start(bf16[1,2,4,4,64,256]{5,4,3,2,1,0:T(8,128)(2,1)} %param.8) | copy-start | bytes 3145732
  2.8 1.0 copy-start.2
  3.8 28.2 %copy-start.1 = (bf16[1,2,4,4,64,256]{5,4,3,2,1,0:T(8,128)(2,1)S(1)}, bf16[1,2,4,4,64,256]{5,4,3,2,1,0:T(8,128)(2,1)}, u32[]{:S(2)}) copy-start(bf16[1,2,4,4,64,256]{5,4,3,2,1,0:T(8,128)(2,1)} %param.8) | copy-start | bytes 3145732
  3.8 28.2 %copy-start.3 = (bf16[1,2,4,4,64,64]{5,4,3,2,1,0:T(8,128)(2,1)S(1)}, bf16[1,2,4,4,64,64]{5,4,3,2,1,0:T(8,128)(2,1)}, u32[]{:S(2)}) copy-start(bf16[1,2,4,4,64,64]{5,4,3,2,1,0:T(8,128)(2,1)} %param.7) | copy-start | bytes 786436
  5.7 11.3 %collective-permute-start.4 = (bf16[32,64,128]{2,1,0:T(8,128)(2,1)S(1)}, bf16[32,64,128]{2,1,0:T(8,128)(2,1)S(1)}, u32[]{:S(2)}, u32[]{:S(2)}) collective-permute-start(bf16[32,64,128]{2,1,0:T(8,128)(2,1)S(1)} %get-tuple-element.30), channel_id=1, source_target_pairs={{1,97},{3,31},{125,29},{127,99},{129,225},{131,159},{253,157},{255... | collective-permute-start | bytes 1572872 | tf_op jit(solution)/shard_map/ppermute | solution.py:204
  10.9 34.5 %collective-permute-start.2 = (bf16[32,64,128]{2,1,0:T(8,128)(2,1)S(1)}, bf16[32,64,128]{2,1,0:T(8,128)(2,1)S(1)}, u32[]{:S(2)}, u32[]{:S(2)}) collective-permute-start(bf16[32,64,128]{2,1,0:T(8,128)(2,1)S(1)} %get-tuple-element.28), channel_id=1, source_target_pairs={{0,4},{1,5},{2,6},{3,7},{4,0},{5,1},{6,2},{7,3},{8,12},{9,13},{10,... | collective-permute-start | bytes 1572872 | tf_op jit(solution)/shard_map/ppermute | solution.py:206
  12.8 32.6 %collective-permute-start.3 = (bf16[32,64,128]{2,1,0:T(8,128)(2,1)S(1)}, bf16[32,64,128]{2,1,0:T(8,128)(2,1)S(1)}, u32[]{:S(2)}, u32[]{:S(2)}) collective-permute-start(bf16[32,64,128]{2,1,0:T(8,128)(2,1)S(1)} %get-tuple-element.29), channel_id=1, source_target_pairs={{0,508},{2,510},{4,8},{5,9},{6,10},{7,11},{8,4},{9,5},{10,6},{11,7... | collective-permute-start | bytes 1572872 | tf_op jit(solution)/shard_map/ppermute | solution.py:205
  17.0 28.4 %collective-permute-start.5 = (bf16[32,64,128]{2,1,0:T(8,128)(2,1)S(1)}, bf16[32,64,128]{2,1,0:T(8,128)(2,1)S(1)}, u32[]{:S(2)}, u32[]{:S(2)}) collective-permute-start(bf16[32,64,128]{2,1,0:T(8,128)(2,1)S(1)} %collective-permute-done.4), channel_id=1, source_target_pairs={{97,509},{31,511},{29,129},{99,131},{225,125},{159,127},{157,257},... | collective-permute-start | bytes 1572872 | tf_op jit(solution)/shard_map/ppermute | solution.py:217
  18.3 16.7 %collective-permute-start = (bf16[16,64,128]{2,1,0:T(8,128)(2,1)S(1)}, bf16[16,64,128]{2,1,0:T(8,128)(2,1)S(1)}, u32[]{:S(2)}, u32[]{:S(2)}) collective-permute-start(bf16[16,64,128]{2,1,0:T(8,128)(2,1)S(1)} %get-tuple-element.26), channel_id=1, source_target_pairs={{0,1},{1,0},{2,3},{3,2},{4,5},{5,4},{6,7},{7,6},{8,9},{9,8},{10,11... | collective-permute-start | bytes 786440 | tf_op jit(solution)/shard_map/ppermute | solution.py:208
  29.8 14.7 %collective-permute-start.1 = (bf16[16,64,128]{2,1,0:T(8,128)(2,1)S(1)}, bf16[16,64,128]{2,1,0:T(8,128)(2,1)S(1)}, u32[]{:S(2)}, u32[]{:S(2)}) collective-permute-start(bf16[16,64,128]{2,1,0:T(8,128)(2,1)S(1)} %get-tuple-element.27), channel_id=1, source_target_pairs={{0,3},{1,2},{2,1},{3,0},{4,7},{5,6},{6,5},{7,4},{8,11},{9,10},{10,... | collective-permute-start | bytes 786440 | tf_op jit(solution)/shard_map/ppermute | solution.py:207
  48.1 7.4 %collective-permute-start.10 = (bf16[32,64,128]{2,1,0:T(8,128)(2,1)S(1)}, bf16[32,64,128]{2,1,0:T(8,128)(2,1)S(1)}, u32[]{:S(2)}, u32[]{:S(2)}) collective-permute-start(bf16[32,64,128]{2,1,0:T(8,128)(2,1)S(1)} %get-tuple-element.37), channel_id=1, source_target_pairs={{1,97},{3,31},{125,29},{127,99},{129,225},{131,159},{253,157},{255... | collective-permute-start | bytes 1572872 | tf_op jit(solution)/shard_map/ppermute | solution.py:204
  49.4 22.6 %collective-permute-start.8 = (bf16[32,64,128]{2,1,0:T(8,128)(2,1)S(1)}, bf16[32,64,128]{2,1,0:T(8,128)(2,1)S(1)}, u32[]{:S(2)}, u32[]{:S(2)}) collective-permute-start(bf16[32,64,128]{2,1,0:T(8,128)(2,1)S(1)} %get-tuple-element.35), channel_id=1, source_target_pairs={{0,4},{1,5},{2,6},{3,7},{4,0},{5,1},{6,2},{7,3},{8,12},{9,13},{10,... | collective-permute-start | bytes 1572872 | tf_op jit(solution)/shard_map/ppermute | solution.py:206
  51.3 20.7 %collective-permute-start.9 = (bf16[32,64,128]{2,1,0:T(8,128)(2,1)S(1)}, bf16[32,64,128]{2,1,0:T(8,128)(2,1)S(1)}, u32[]{:S(2)}, u32[]{:S(2)}) collective-permute-start(bf16[32,64,128]{2,1,0:T(8,128)(2,1)S(1)} %get-tuple-element.36), channel_id=1, source_target_pairs={{0,508},{2,510},{4,8},{5,9},{6,10},{7,11},{8,4},{9,5},{10,6},{11,7... | collective-permute-start | bytes 1572872 | tf_op jit(solution)/shard_map/ppermute | solution.py:205
  55.5 16.6 %collective-permute-start.11 = (bf16[32,64,128]{2,1,0:T(8,128)(2,1)S(1)}, bf16[32,64,128]{2,1,0:T(8,128)(2,1)S(1)}, u32[]{:S(2)}, u32[]{:S(2)}) collective-permute-start(bf16[32,64,128]{2,1,0:T(8,128)(2,1)S(1)} %collective-permute-done.10), channel_id=1, source_target_pairs={{97,509},{31,511},{29,129},{99,131},{225,125},{159,127},{157,257},... | collective-permute-start | bytes 1572872 | tf_op jit(solution)/shard_map/ppermute | solution.py:217
  56.8 7.7 %collective-permute-start.6 = (bf16[16,64,128]{2,1,0:T(8,128)(2,1)S(1)}, bf16[16,64,128]{2,1,0:T(8,128)(2,1)S(1)}, u32[]{:S(2)}, u32[]{:S(2)}) collective-permute-start(bf16[16,64,128]{2,1,0:T(8,128)(2,1)S(1)} %get-tuple-element.33), channel_id=1, source_target_pairs={{0,1},{1,0},{2,3},{3,2},{4,5},{5,4},{6,7},{7,6},{8,9},{9,8},{10,11... | collective-permute-start | bytes 786440 | tf_op jit(solution)/shard_map/ppermute | solution.py:208
  58.7 12.4 %collective-permute-start.7 = (bf16[16,64,128]{2,1,0:T(8,128)(2,1)S(1)}, bf16[16,64,128]{2,1,0:T(8,128)(2,1)S(1)}, u32[]{:S(2)}, u32[]{:S(2)}) collective-permute-start(bf16[16,64,128]{2,1,0:T(8,128)(2,1)S(1)} %get-tuple-element.34), channel_id=1, source_target_pairs={{0,3},{1,2},{2,1},{3,0},{4,7},{5,6},{6,5},{7,4},{8,11},{9,10},{10,... | collective-permute-start | bytes 786440 | tf_op jit(solution)/shard_map/ppermute | solution.py:207
  74.9 11.5 %collective-permute-start.16 = (bf16[32,64,128]{2,1,0:T(8,128)(2,1)S(1)}, bf16[32,64,128]{2,1,0:T(8,128)(2,1)S(1)}, u32[]{:S(2)}, u32[]{:S(2)}) collective-permute-start(bf16[32,64,128]{2,1,0:T(8,128)(2,1)S(1)} %get-tuple-element.44), channel_id=1, source_target_pairs={{1,97},{3,31},{125,29},{127,99},{129,225},{131,159},{253,157},{255... | collective-permute-start | bytes 1572872 | tf_op jit(solution)/shard_map/ppermute | solution.py:204
  80.3 25.9 %collective-permute-start.14 = (bf16[32,64,128]{2,1,0:T(8,128)(2,1)S(1)}, bf16[32,64,128]{2,1,0:T(8,128)(2,1)S(1)}, u32[]{:S(2)}, u32[]{:S(2)}) collective-permute-start(bf16[32,64,128]{2,1,0:T(8,128)(2,1)S(1)} %get-tuple-element.42), channel_id=1, source_target_pairs={{0,4},{1,5},{2,6},{3,7},{4,0},{5,1},{6,2},{7,3},{8,12},{9,13},{10,... | collective-permute-start | bytes 1572872 | tf_op jit(solution)/shard_map/ppermute | solution.py:206
  82.2 24.0 %collective-permute-start.15 = (bf16[32,64,128]{2,1,0:T(8,128)(2,1)S(1)}, bf16[32,64,128]{2,1,0:T(8,128)(2,1)S(1)}, u32[]{:S(2)}, u32[]{:S(2)}) collective-permute-start(bf16[32,64,128]{2,1,0:T(8,128)(2,1)S(1)} %get-tuple-element.43), channel_id=1, source_target_pairs={{0,508},{2,510},{4,8},{5,9},{6,10},{7,11},{8,4},{9,5},{10,6},{11,7... | collective-permute-start | bytes 1572872 | tf_op jit(solution)/shard_map/ppermute | solution.py:205
  86.4 19.9 %collective-permute-start.17 = (bf16[32,64,128]{2,1,0:T(8,128)(2,1)S(1)}, bf16[32,64,128]{2,1,0:T(8,128)(2,1)S(1)}, u32[]{:S(2)}, u32[]{:S(2)}) collective-permute-start(bf16[32,64,128]{2,1,0:T(8,128)(2,1)S(1)} %collective-permute-done.16), channel_id=1, source_target_pairs={{97,509},{31,511},{29,129},{99,131},{225,125},{159,127},{157,257},... | collective-permute-start | bytes 1572872 | tf_op jit(solution)/shard_map/ppermute | solution.py:217
  87.7 8.2 %collective-permute-start.12 = (bf16[16,64,128]{2,1,0:T(8,128)(2,1)S(1)}, bf16[16,64,128]{2,1,0:T(8,128)(2,1)S(1)}, u32[]{:S(2)}, u32[]{:S(2)}) collective-permute-start(bf16[16,64,128]{2,1,0:T(8,128)(2,1)S(1)} %get-tuple-element.40), channel_id=1, source_target_pairs={{0,1},{1,0},{2,3},{3,2},{4,5},{5,4},{6,7},{7,6},{8,9},{9,8},{10,11... | collective-permute-start | bytes 786440 | tf_op jit(solution)/shard_map/ppermute | solution.py:208
  89.6 15.8 %collective-permute-start.13 = (bf16[16,64,128]{2,1,0:T(8,128)(2,1)S(1)}, bf16[16,64,128]{2,1,0:T(8,128)(2,1)S(1)}, u32[]{:S(2)}, u32[]{:S(2)}) collective-permute-start(bf16[16,64,128]{2,1,0:T(8,128)(2,1)S(1)} %get-tuple-element.41), channel_id=1, source_target_pairs={{0,3},{1,2},{2,1},{3,0},{4,7},{5,6},{6,5},{7,4},{8,11},{9,10},{10,... | collective-permute-start | bytes 786440 | tf_op jit(solution)/shard_map/ppermute | solution.py:207
  95.9 10.4 %copy-start.4 = (bf16[1,2,4,4,64,64]{5,4,3,2,1,0:T(8,128)(2,1)S(1)}, bf16[1,2,4,4,64,64]{5,4,3,2,1,0:T(8,128)(2,1)}, u32[]{:S(2)}) copy-start(bf16[1,2,4,4,64,64]{5,4,3,2,1,0:T(8,128)(2,1)} %param.11) | copy-start | bytes 786436
  105.3 0.9 copy-start.5
  108.4 3.2 %collective-permute-start.18 = (bf16[8,64,128]{2,1,0:T(8,128)(2,1)S(1)}, bf16[8,64,128]{2,1,0:T(8,128)(2,1)S(1)}, u32[]{:S(2)}, u32[]{:S(2)}) collective-permute-start(bf16[8,64,128]{2,1,0:T(8,128)(2,1)S(1)} %get-tuple-element.47), channel_id=1, source_target_pairs={{0,1},{1,0},{2,3},{3,2},{4,5},{5,4},{6,7},{7,6},{8,9},{9,8},{10,11... | collective-permute-start | bytes 393224 | tf_op jit(solution)/shard_map/ppermute | solution.py:248
  112.2 5.4 %collective-permute-start.19 = (bf16[4,64,128]{2,1,0:T(8,128)(2,1)S(1)}, bf16[4,64,128]{2,1,0:T(8,128)(2,1)S(1)}, u32[]{:S(2)}, u32[]{:S(2)}) collective-permute-start(bf16[4,64,128]{2,1,0:T(8,128)(2,1)S(1)} %get-tuple-element.49), channel_id=1, source_target_pairs={{0,2},{1,3},{2,0},{3,1},{4,6},{5,7},{6,4},{7,5},{8,10},{9,11},{10,... | collective-permute-start | bytes 196616 | tf_op jit(solution)/shard_map/ppermute | solution.py:256

commit v5 on v4

--- a/solution.py
+++ b/solution.py
@@ -14,6 +14,7 @@
 BF16 = jnp.bfloat16
 VMEM = pl.BlockSpec(memory_space=pltpu.VMEM)
 SMEM = pl.BlockSpec(memory_space=pltpu.SMEM)
+LONG = pl.CostEstimate(flops=10_000_000_000, bytes_accessed=0, transcendentals=0)
 PARAMS = pltpu.CompilerParams(vmem_limit_bytes=12 * 1024 * 1024)
 
 GROUP = 32
@@ -121,7 +122,7 @@
                 done[s] = partial[s] - OMEGA * scales[5 * s + 3] * term
 
 
-def new_estimates(role, scales, partial, inner, outer, relayed, hops, store):
+def new_estimates(role, scales, relayed, outer, inner, partial, hops, store):
     sites, d = partial.shape[:2]
     for when, t_next, t_back in either(role[2], inner, outer):
 
@@ -133,16 +134,16 @@
                 store(s, partial[s] - OMEGA * total)
 
 
-def sweep_end(role, scales, partial, inner, outer, relayed, hops, estimate, vector, *messages):
+def sweep_end(role, scales, relayed, outer, inner, partial, hops, estimate, vector, *messages):
     def store(s, e):
         estimate[s] = e
         vector[s] = e.astype(BF16)
 
-    new_estimates(role, scales, partial, inner, outer, relayed, hops, store)
+    new_estimates(role, scales, relayed, outer, inner, partial, hops, store)
     hop_terms(role, scales, vector, hops, *messages)
 
 
-def last_end(role, scales, labels, partial, inner, outer, relayed, hops, restrictor, vector, own, away, sums):
+def last_end(role, scales, labels, relayed, outer, inner, partial, hops, restrictor, vector, own, away, sums):
     half = own.shape[0] // 2
     xs, ys = labels.shape[2:]
     sums[...] = jnp.zeros_like(sums)
@@ -150,7 +151,7 @@
     def store(s, e):
         vector[s] = e.astype(BF16)
 
-    new_estimates(role, scales, partial, inner, outer, relayed, hops, store)
+    new_estimates(role, scales, relayed, outer, inner, partial, hops, store)
     for s in range(vector.shape[0]):
         label = labels[0, s // (xs * ys), s // ys % xs, s % ys]
         sums[label] += dot(restrictor[s], vector[s])
@@ -212,6 +213,7 @@
             in_specs=[SMEM] + [VMEM] * 5,
             out_specs=VMEM,
             input_output_aliases={1: 0} if sweep else {},
+            cost_estimate=LONG,
             compiler_params=PARAMS,
         )(scales, estimate, b, vector, selfs, hops)
         relayed = lax.ppermute(at_relay, both, back)
@@ -223,14 +225,14 @@
             input_output_aliases={2: 0},
             compiler_params=PARAMS,
         )(role, scales, partial, from_z_inner, from_z_outer, hops)
-        came = (partial, t_inner, t_outer, relayed, hops)
+        came = (relayed, t_outer, t_inner, partial, hops)
         if sweep + 1 < ITERS:
             estimate, vector, *sent = pl.pallas_call(
                 sweep_end,
                 out_shape=(wide, field) + messages,
                 in_specs=[SMEM] * 2 + [VMEM] * 5,
                 out_specs=(VMEM,) * 7,
-                input_output_aliases={2: 0},
+                input_output_aliases={5: 0},
                 compiler_params=PARAMS,
             )(role, scales, *came)
     keep = AGG // members

time: 119 us -> 121 us (1.017)
  starting transfers between devices: 51.1 us -> 62.7 us
  waiting for transfers between devices: 40.8 us -> 30.9 us
    ppermute x3, waiting for transfers between devices: 25.7 us -> 8.56 us  [shards(): from_z_outer = lax.ppermute(sent[2], 'gz', z_outer)]
    ppermute x3, waiting for transfers between devices: 0.01 us -> 15.7 us  [shards(): relayed = lax.ppermute(at_relay, both, back)]
    ppermute x3, waiting for transfers between devices: 10.3 us -> 0.01 us  [shards(): at_relay = lax.ppermute(sent[4], both, out)]
    ppermute x3, starting transfers between devices: 11.9 us -> 16.3 us  [shards(): at_relay = lax.ppermute(sent[4], both, out)]
    ppermute x1, starting transfers between devices: 1.91 us -> 5.82 us  [shards(): from_core = lax.ppermute(away, 'gz', [(i, i ^ 1) for i in range(members)])]
    ppermute x3, waiting for transfers between devices: 0.01 us -> 3.57 us  [shards(): t_inner = lax.ppermute(sent[1], both, inner)]
    ppermute x3, starting transfers between devices: 15.4 us -> 11.9 us  [shards(): from_z_inner = lax.ppermute(sent[3], 'gz', z_inner)]
    ppermute x3, starting transfers between devices: 8.34 us -> 11.8 us  [shards(): from_z_outer = lax.ppermute(sent[2], 'gz', z_outer)]
  transfers between devices with their start and end apart: 20 -> 20, of which waited for: 8 -> 9; matrix products, arithmetic and copies ran while one was open for 0% -> 0% of each run, Pallas kernels for 10% -> 10%
where the time goes in v5:
time: 121 us; the launch traced here: 120 us
  starting transfers between devices  62.7 us (52%)
  waiting for transfers between devices  30.9 us (26%)
  Pallas kernels  21.5 us (18%)
  local copies, waits for them, and re-layouts  3.07 us (3%)
    ppermute x3, starting transfers between devices, shards(): at_relay = lax.ppermute(sent[4], both, out)  16.3 us
    ppermute x3, waiting for transfers between devices, shards(): relayed = lax.ppermute(at_relay, both, back)  15.7 us
    ppermute x3, starting transfers between devices, shards(): from_z_inner = lax.ppermute(sent[3], 'gz', z_inner)  11.9 us
    ppermute x3, starting transfers between devices, shards(): from_z_outer = lax.ppermute(sent[2], 'gz', z_outer)  11.8 us
    pallas_call x3, Pallas kernels, shards(): pl.pallas_call(functools.partial(local_terms, (zs, xs, ys, d)), out_shape...  8.83 us
    ppermute x3, waiting for transfers between devices, shards(): from_z_outer = lax.ppermute(sent[2], 'gz', z_outer)  8.56 us
    ppermute x1, starting transfers between devices, shards(): from_core = lax.ppermute(away, 'gz', [(i, i ^ 1) for i in range(members)])  5.82 us
    ppermute x3, starting transfers between devices, shards(): t_inner = lax.ppermute(sent[1], both, inner)  5.76 us
  transfers between devices with their start and end apart: 20, of which 9 were waited for; matrix products, arithmetic and copies ran while one was open for 0% of the time, Pallas kernels for 10%

profile of v5, /device:TPU:1, one launch (start us, length us, event | category | flops | bytes accessed | tf_op | source)
XLA Modules:
  0.0 120.0 jit_solution(146102818208637251)
XLA Ops:
  0.7 0.0 copy-start.6
  0.7 0.7 copy-done.6
  1.3 0.1 reshape.37.scales
  1.5 0.1 pad_add_fusion.role
  1.5 0.0 copy-start
  1.5 1.2 %copy-done = bf16[1,2,4,4,64,256]{5,4,3,2,1,0:T(8,128)(2,1)S(1)} copy-done((bf16[1,2,4,4,64,256]{5,4,3,2,1,0:T(8,128)(2,1)S(1)}, bf16[1,2,4,4,64,256]{5,4,3,2,1,0:T(8,128)(2,1)}, u32[]{:S(2)}) %copy-start) | copy-done | bytes 1048600
  2.8 1.0 copy-done.2
  3.8 1.9 %shard_map.77 = (bf16[32,64,128]{2,1,0:T(8,128)(2,1)S(1)}, bf16[32,64,128]{2,1,0:T(8,128)(2,1)S(1)}, bf16[16,64,128]{2,1,0:T(8,128)(2,1)S(1)}, bf16[16,64,128]{2,1,0:T(8,128)(2,1)S(1)}, bf16[32,64,128]{2,1,0:T(8,128)(2,1)S(1)}) custom-call(s32[4]{0:T(128)S(1)} %pad_add_fusion.role, f32[160]{0:T(256)S(1)} %reshape.37.scales, ...), custom_call_target="tpu_custom_call" | custom-call | tf_op jit(solution)/shard_map/pallas_call | solution.py:196
  5.7 5.2 %collective-permute-start = (bf16[32,64,128]{2,1,0:T(8,128)(2,1)S(1)}, bf16[32,64,128]{2,1,0:T(8,128)(2,1)S(1)}, u32[]{:S(2)}, u32[]{:S(2)}) collective-permute-start(bf16[32,64,128]{2,1,0:T(8,128)(2,1)S(1)} %get-tuple-element.26), channel_id=1, source_target_pairs={{1,97},{3,31},{125,29},{127,99},{129,225},{131,159},{253,157},{255... | collective-permute-start | bytes 1572872 | tf_op jit(solution)/shard_map/ppermute | solution.py:205
  10.9 4.2 %collective-permute-start.4 = (bf16[16,64,128]{2,1,0:T(8,128)(2,1)S(1)}, bf16[16,64,128]{2,1,0:T(8,128)(2,1)S(1)}, u32[]{:S(2)}, u32[]{:S(2)}) collective-permute-start(bf16[16,64,128]{2,1,0:T(8,128)(2,1)S(1)} %get-tuple-element.29), channel_id=1, source_target_pairs={{0,1},{1,0},{2,3},{3,2},{4,5},{5,4},{6,7},{7,6},{8,9},{9,8},{10,11... | collective-permute-start | bytes 786440 | tf_op jit(solution)/shard_map/ppermute | solution.py:209
  15.2 7.6 %collective-permute-start.5 = (bf16[16,64,128]{2,1,0:T(8,128)(2,1)S(1)}, bf16[16,64,128]{2,1,0:T(8,128)(2,1)S(1)}, u32[]{:S(2)}, u32[]{:S(2)}) collective-permute-start(bf16[16,64,128]{2,1,0:T(8,128)(2,1)S(1)} %get-tuple-element.30), channel_id=1, source_target_pairs={{0,3},{1,2},{2,1},{3,0},{4,7},{5,6},{6,5},{7,4},{8,11},{9,10},{10,... | collective-permute-start | bytes 786440 | tf_op jit(solution)/shard_map/ppermute | solution.py:208
  22.7 0.7 collective-permute-start.2
  23.4 1.9 %collective-permute-start.3 = (bf16[32,64,128]{2,1,0:T(8,128)(2,1)S(1)}, bf16[32,64,128]{2,1,0:T(8,128)(2,1)S(1)}, u32[]{:S(2)}, u32[]{:S(2)}) collective-permute-start(bf16[32,64,128]{2,1,0:T(8,128)(2,1)S(1)} %get-tuple-element.28), channel_id=1, source_target_pairs={{0,4},{1,5},{2,6},{3,7},{4,0},{5,1},{6,2},{7,3},{8,12},{9,13},{10,... | collective-permute-start | bytes 1572872 | tf_op jit(solution)/shard_map/ppermute | solution.py:207
  25.4 0.0 collective-permute-done
  25.4 1.3 %collective-permute-start.1 = (bf16[32,64,128]{2,1,0:T(8,128)(2,1)S(1)}, bf16[32,64,128]{2,1,0:T(8,128)(2,1)S(1)}, u32[]{:S(2)}, u32[]{:S(2)}) collective-permute-start(bf16[32,64,128]{2,1,0:T(8,128)(2,1)S(1)} %collective-permute-done), channel_id=1, source_target_pairs={{97,509},{31,511},{29,129},{99,131},{225,125},{159,127},{157,257},... | collective-permute-start | bytes 1572872 | tf_op jit(solution)/shard_map/ppermute | solution.py:219
  26.7 0.0 copy-done.1
  26.7 0.0 copy-done.5
  26.7 3.0 %shard_map.78.partial = f32[32,64,128]{2,1,0:T(8,128)S(1)} custom-call(f32[160]{0:T(256)S(1)} %reshape.37.scales, bf16[32,64,128]{2,1,0:T(8,128)(2,1)S(1)} %bitcast.22, bf16[32,64,128]{2,1,0:T(8,128)(2,1)S(1)} %bitcast.23, bf16[32,64,128]{2,1,0:T(8,128)(2,1)S(1)} %bitcast.24, bf16[32,64,64]{2,1,0:T(8,128)(2,1)S(1)} %bitcast.28, bf16[32,64,256]{2,1,0:T(8,128)(2,1)S(1)} %bitcast.12), custom_call_target="tpu_custom_call" | custom-call | flops 10000000000 | tf_op jit(solution)/shard_map/pallas_call | solution.py:210
  29.6 0.0 collective-permute-done.4.z_inner
  29.7 0.0 collective-permute-done.5.z_outer
  29.7 0.9 shard_map.79.partial
  30.6 0.0 collective-permute-done.2.outer
  30.6 2.8 %collective-permute-done.3.inner = bf16[32,64,128]{2,1,0:T(8,128)(2,1)S(1)} collective-permute-done((bf16[32,64,128]{2,1,0:T(8,128)(2,1)S(1)}, bf16[32,64,128]{2,1,0:T(8,128)(2,1)S(1)}, u32[]{:S(2)}, u32[]{:S(2)}) %collective-permute-start.3) | collective-permute-done | bytes 524320 | tf_op jit(solution)/shard_map/ppermute | solution.py:207
  33.4 6.5 %collective-permute-done.1.relayed = bf16[32,64,128]{2,1,0:T(8,128)(2,1)S(1)} collective-permute-done((bf16[32,64,128]{2,1,0:T(8,128)(2,1)S(1)}, bf16[32,64,128]{2,1,0:T(8,128)(2,1)S(1)}, u32[]{:S(2)}, u32[]{:S(2)}) %collective-permute-start.1) | collective-permute-done | bytes 524320 | tf_op jit(solution)/shard_map/ppermute | solution.py:219
  39.8 2.6 %shard_map.80 = (f32[32,64,128]{2,1,0:T(8,128)S(1)}, bf16[32,64,128]{2,1,0:T(8,128)(2,1)S(1)}, bf16[32,64,128]{2,1,0:T(8,128)(2,1)S(1)}, bf16[32,64,128]{2,1,0:T...) custom-call(s32[4]{0:T(128)S(1)} %pad_add_fusion.role, ...), custom_call_target="tpu_custom_call", output_to_operand_aliasing={{0}: (5, {})} | custom-call | tf_op jit(solution)/shard_map/pallas_call | solution.py:230
  42.5 4.8 %collective-permute-start.6 = (bf16[32,64,128]{2,1,0:T(8,128)(2,1)S(1)}, bf16[32,64,128]{2,1,0:T(8,128)(2,1)S(1)}, u32[]{:S(2)}, u32[]{:S(2)}) collective-permute-start(bf16[32,64,128]{2,1,0:T(8,128)(2,1)S(1)} %get-tuple-element.31), channel_id=1, source_target_pairs={{1,97},{3,31},{125,29},{127,99},{129,225},{131,159},{253,157},{255... | collective-permute-start | bytes 1572872 | tf_op jit(solution)/shard_map/ppermute | solution.py:205
  47.3 3.7 %collective-permute-start.10 = (bf16[16,64,128]{2,1,0:T(8,128)(2,1)S(1)}, bf16[16,64,128]{2,1,0:T(8,128)(2,1)S(1)}, u32[]{:S(2)}, u32[]{:S(2)}) collective-permute-start(bf16[16,64,128]{2,1,0:T(8,128)(2,1)S(1)} %get-tuple-element.36), channel_id=1, source_target_pairs={{0,1},{1,0},{2,3},{3,2},{4,5},{5,4},{6,7},{7,6},{8,9},{9,8},{10,11... | collective-permute-start | bytes 786440 | tf_op jit(solution)/shard_map/ppermute | solution.py:209
  51.0 1.9 %collective-permute-start.11 = (bf16[16,64,128]{2,1,0:T(8,128)(2,1)S(1)}, bf16[16,64,128]{2,1,0:T(8,128)(2,1)S(1)}, u32[]{:S(2)}, u32[]{:S(2)}) collective-permute-start(bf16[16,64,128]{2,1,0:T(8,128)(2,1)S(1)} %get-tuple-element.37), channel_id=1, source_target_pairs={{0,3},{1,2},{2,1},{3,0},{4,7},{5,6},{6,5},{7,4},{8,11},{9,10},{10,... | collective-permute-start | bytes 786440 | tf_op jit(solution)/shard_map/ppermute | solution.py:208
  52.9 0.7 collective-permute-start.8
  53.6 1.9 %collective-permute-start.9 = (bf16[32,64,128]{2,1,0:T(8,128)(2,1)S(1)}, bf16[32,64,128]{2,1,0:T(8,128)(2,1)S(1)}, u32[]{:S(2)}, u32[]{:S(2)}) collective-permute-start(bf16[32,64,128]{2,1,0:T(8,128)(2,1)S(1)} %get-tuple-element.33), channel_id=1, source_target_pairs={{0,4},{1,5},{2,6},{3,7},{4,0},{5,1},{6,2},{7,3},{8,12},{9,13},{10,... | collective-permute-start | bytes 1572872 | tf_op jit(solution)/shard_map/ppermute | solution.py:207
  55.6 0.0 collective-permute-done.6
  55.6 1.3 %collective-permute-start.7 = (bf16[32,64,128]{2,1,0:T(8,128)(2,1)S(1)}, bf16[32,64,128]{2,1,0:T(8,128)(2,1)S(1)}, u32[]{:S(2)}, u32[]{:S(2)}) collective-permute-start(bf16[32,64,128]{2,1,0:T(8,128)(2,1)S(1)} %collective-permute-done.6), channel_id=1, source_target_pairs={{97,509},{31,511},{29,129},{99,131},{225,125},{159,127},{157,257},... | collective-permute-start | bytes 1572872 | tf_op jit(solution)/shard_map/ppermute | solution.py:219
  56.9 2.9 %shard_map.81.partial = f32[32,64,128]{2,1,0:T(8,128)S(1)} custom-call(f32[160]{0:T(256)S(1)} %reshape.37.scales, f32[32,64,128]{2,1,0:T(8,128)S(1)} %get-tuple-element.34.estimate, bf16[32,64,128]{2,1,0:T(8,128)(2,1)S(1)} %bitcast.25, bf16[32,64,128]{2,1,0:T(8,128)(2,1)S(1)} %get-tuple-element.35.vector, ...), custom_call_target="tpu_custom_call", output_to_operand_aliasing={{}: (1, {})} | custom-call | flops 10000000000 | tf_op jit(solution)/shard_map/pallas_call | solution.py:210
  59.8 0.0 collective-permute-done.10.z_inner
  59.8 2.1 %collective-permute-done.11.z_outer = bf16[16,64,128]{2,1,0:T(8,128)(2,1)S(1)} collective-permute-done((bf16[16,64,128]{2,1,0:T(8,128)(2,1)S(1)}, bf16[16,64,128]{2,1,0:T(8,128)(2,1)S(1)}, u32[]{:S(2)}, u32[]{:S(2)}) %collective-permute-start.11) | collective-permute-done | bytes 262176 | tf_op jit(solution)/shard_map/ppermute | solution.py:208
  61.9 0.9 shard_map.82.partial
  62.8 0.0 collective-permute-done.8.outer
  62.8 0.8 collective-permute-done.9.inner
  63.6 6.5 %collective-permute-done.7.relayed = bf16[32,64,128]{2,1,0:T(8,128)(2,1)S(1)} collective-permute-done((bf16[32,64,128]{2,1,0:T(8,128)(2,1)S(1)}, bf16[32,64,128]{2,1,0:T(8,128)(2,1)S(1)}, u32[]{:S(2)}, u32[]{:S(2)}) %collective-permute-start.7) | collective-permute-done | bytes 524320 | tf_op jit(solution)/shard_map/ppermute | solution.py:219
  70.0 2.8 %shard_map.83 = (f32[32,64,128]{2,1,0:T(8,128)S(1)}, bf16[32,64,128]{2,1,0:T(8,128)(2,1)S(1)}, bf16[32,64,128]{2,1,0:T(8,128)(2,1)S(1)}, bf16[32,64,128]{2,1,0:T...) custom-call(s32[4]{0:T(128)S(1)} %pad_add_fusion.role, ...), custom_call_target="tpu_custom_call", output_to_operand_aliasing={{0}: (5, {})} | custom-call | tf_op jit(solution)/shard_map/pallas_call | solution.py:230
  72.9 6.3 %collective-permute-start.12 = (bf16[32,64,128]{2,1,0:T(8,128)(2,1)S(1)}, bf16[32,64,128]{2,1,0:T(8,128)(2,1)S(1)}, u32[]{:S(2)}, u32[]{:S(2)}) collective-permute-start(bf16[32,64,128]{2,1,0:T(8,128)(2,1)S(1)} %get-tuple-element.38), channel_id=1, source_target_pairs={{1,97},{3,31},{125,29},{127,99},{129,225},{131,159},{253,157},{255... | collective-permute-start | bytes 1572872 | tf_op jit(solution)/shard_map/ppermute | solution.py:205
  79.1 3.9 %collective-permute-start.16 = (bf16[16,64,128]{2,1,0:T(8,128)(2,1)S(1)}, bf16[16,64,128]{2,1,0:T(8,128)(2,1)S(1)}, u32[]{:S(2)}, u32[]{:S(2)}) collective-permute-start(bf16[16,64,128]{2,1,0:T(8,128)(2,1)S(1)} %get-tuple-element.43), channel_id=1, source_target_pairs={{0,1},{1,0},{2,3},{3,2},{4,5},{5,4},{6,7},{7,6},{8,9},{9,8},{10,11... | collective-permute-start | bytes 786440 | tf_op jit(solution)/shard_map/ppermute | solution.py:209
  83.1 2.3 %collective-permute-start.17 = (bf16[16,64,128]{2,1,0:T(8,128)(2,1)S(1)}, bf16[16,64,128]{2,1,0:T(8,128)(2,1)S(1)}, u32[]{:S(2)}, u32[]{:S(2)}) collective-permute-start(bf16[16,64,128]{2,1,0:T(8,128)(2,1)S(1)} %get-tuple-element.44), channel_id=1, source_target_pairs={{0,3},{1,2},{2,1},{3,0},{4,7},{5,6},{6,5},{7,4},{8,11},{9,10},{10,... | collective-permute-start | bytes 786440 | tf_op jit(solution)/shard_map/ppermute | solution.py:208
  85.4 0.7 collective-permute-start.14
  86.1 1.9 %collective-permute-start.15 = (bf16[32,64,128]{2,1,0:T(8,128)(2,1)S(1)}, bf16[32,64,128]{2,1,0:T(8,128)(2,1)S(1)}, u32[]{:S(2)}, u32[]{:S(2)}) collective-permute-start(bf16[32,64,128]{2,1,0:T(8,128)(2,1)S(1)} %get-tuple-element.40), channel_id=1, source_target_pairs={{0,4},{1,5},{2,6},{3,7},{4,0},{5,1},{6,2},{7,3},{8,12},{9,13},{10,... | collective-permute-start | bytes 1572872 | tf_op jit(solution)/shard_map/ppermute | solution.py:207
  88.0 0.0 collective-permute-done.12
  88.0 1.3 %collective-permute-start.13 = (bf16[32,64,128]{2,1,0:T(8,128)(2,1)S(1)}, bf16[32,64,128]{2,1,0:T(8,128)(2,1)S(1)}, u32[]{:S(2)}, u32[]{:S(2)}) collective-permute-start(bf16[32,64,128]{2,1,0:T(8,128)(2,1)S(1)} %collective-permute-done.12), channel_id=1, source_target_pairs={{97,509},{31,511},{29,129},{99,131},{225,125},{159,127},{157,257},... | collective-permute-start | bytes 1572872 | tf_op jit(solution)/shard_map/ppermute | solution.py:219
  89.3 3.0 %shard_map.84.partial = f32[32,64,128]{2,1,0:T(8,128)S(1)} custom-call(f32[160]{0:T(256)S(1)} %reshape.37.scales, f32[32,64,128]{2,1,0:T(8,128)S(1)} %get-tuple-element.41.estimate, bf16[32,64,128]{2,1,0:T(8,128)(2,1)S(1)} %bitcast.26, bf16[32,64,128]{2,1,0:T(8,128)(2,1)S(1)} %get-tuple-element.42.vector, ...), custom_call_target="tpu_custom_call", output_to_operand_aliasing={{}: (1, {})} | custom-call | flops 10000000000 | tf_op jit(solution)/shard_map/pallas_call | solution.py:210
  92.3 0.0 copy-start.3
  92.3 0.0 collective-permute-done.16.z_inner
  92.3 6.5 %collective-permute-done.17.z_outer = bf16[16,64,128]{2,1,0:T(8,128)(2,1)S(1)} collective-permute-done((bf16[16,64,128]{2,1,0:T(8,128)(2,1)S(1)}, bf16[16,64,128]{2,1,0:T(8,128)(2,1)S(1)}, u32[]{:S(2)}, u32[]{:S(2)}) %collective-permute-start.17) | collective-permute-done | bytes 262176 | tf_op jit(solution)/shard_map/ppermute | solution.py:208
  98.8 0.9 shard_map.85.partial
  99.7 0.0 collective-permute-done.14.outer
  99.7 0.0 collective-permute-done.15.inner
  99.7 2.8 %collective-permute-done.13.relayed = bf16[32,64,128]{2,1,0:T(8,128)(2,1)S(1)} collective-permute-done((bf16[32,64,128]{2,1,0:T(8,128)(2,1)S(1)}, bf16[32,64,128]{2,1,0:T(8,128)(2,1)S(1)}, u32[]{:S(2)}, u32[]{:S(2)}) %collective-permute-start.13) | collective-permute-done | bytes 524320 | tf_op jit(solution)/shard_map/ppermute | solution.py:219
  102.5 0.0 copy-done.3
  102.5 0.0 copy-done.4
  102.5 2.1 %shard_map.86 = (bf16[32,64,128]{2,1,0:T(8,128)(2,1)}, f32[8,64,128]{2,1,0:T(8,128)S(1)}, bf16[8,64,128]{2,1,0:T(8,128)(2,1)S(1)}) custom-call(s32[4]{0:T(128)S(1)} %pad_add_fusion.role, f32[160]{0:T(256)S(1)} %reshape.37.scales, s32[1,2,4,4]{3,2,1,0:T(4,128)S(1)} %copy-done.4, bf16[32,64,128]{2,1,0:T(8,128)(2,1)S(1)} %collective-permute-done.13.relayed, ...), custom_call_target="tpu_custom_call" | custom-call | tf_op jit(solution)/shard_map/pallas_call | solution.py:242
  104.6 5.8 %collective-permute-start.18 = (bf16[8,64,128]{2,1,0:T(8,128)(2,1)S(1)}, bf16[8,64,128]{2,1,0:T(8,128)(2,1)S(1)}, u32[]{:S(2)}, u32[]{:S(2)}) collective-permute-start(bf16[8,64,128]{2,1,0:T(8,128)(2,1)S(1)} %get-tuple-element.47), channel_id=1, source_target_pairs={{0,1},{1,0},{2,3},{3,2},{4,5},{5,4},{6,7},{7,6},{8,9},{9,8},{10,11... | collective-permute-start | bytes 393224 | tf_op jit(solution)/shard_map/ppermute | solution.py:250
  110.4 1.0 collective-permute-done.18.came
  111.4 0.6 shard_map.87
  112.0 5.2 %collective-permute-start.19 = (bf16[4,64,128]{2,1,0:T(8,128)(2,1)S(1)}, bf16[4,64,128]{2,1,0:T(8,128)(2,1)S(1)}, u32[]{:S(2)}, u32[]{:S(2)}) collective-permute-start(bf16[4,64,128]{2,1,0:T(8,128)(2,1)S(1)} %get-tuple-element.49), channel_id=1, source_target_pairs={{0,2},{1,3},{2,0},{3,1},{4,6},{5,7},{6,4},{7,5},{8,10},{9,11},{10,... | collective-permute-start | bytes 196616 | tf_op jit(solution)/shard_map/ppermute | solution.py:258
  117.2 2.2 %collective-permute-done.19 = bf16[4,64,128]{2,1,0:T(8,128)(2,1)S(1)} collective-permute-done((bf16[4,64,128]{2,1,0:T(8,128)(2,1)S(1)}, bf16[4,64,128]{2,1,0:T(8,128)(2,1)S(1)}, u32[]{:S(2)}, u32[]{:S(2)}) %collective-permute-start.19) | collective-permute-done | bytes 65568 | tf_op jit(solution)/shard_map/ppermute | solution.py:258
  119.3 0.7 add_bitcast_fusion
  (4 shorter events, 0.0 us)
Async XLA Ops:
  0.7 0.7 copy-start.6
  1.5 1.2 %copy-start = (bf16[1,2,4,4,64,256]{5,4,3,2,1,0:T(8,128)(2,1)S(1)}, bf16[1,2,4,4,64,256]{5,4,3,2,1,0:T(8,128)(2,1)}, u32[]{:S(2)}) copy-start(bf16[1,2,4,4,64,256]{5,4,3,2,1,0:T(8,128)(2,1)} %param.8) | copy-start | bytes 3145732
  2.8 1.0 copy-start.2
  3.8 22.9 %copy-start.1 = (bf16[1,2,4,4,64,256]{5,4,3,2,1,0:T(8,128)(2,1)S(1)}, bf16[1,2,4,4,64,256]{5,4,3,2,1,0:T(8,128)(2,1)}, u32[]{:S(2)}) copy-start(bf16[1,2,4,4,64,256]{5,4,3,2,1,0:T(8,128)(2,1)} %param.8) | copy-start | bytes 3145732
  3.8 22.9 %copy-start.5 = (bf16[1,2,4,4,64,64]{5,4,3,2,1,0:T(8,128)(2,1)S(1)}, bf16[1,2,4,4,64,64]{5,4,3,2,1,0:T(8,128)(2,1)}, u32[]{:S(2)}) copy-start(bf16[1,2,4,4,64,64]{5,4,3,2,1,0:T(8,128)(2,1)} %param.7) | copy-start | bytes 786436
  5.7 19.7 %collective-permute-start = (bf16[32,64,128]{2,1,0:T(8,128)(2,1)S(1)}, bf16[32,64,128]{2,1,0:T(8,128)(2,1)S(1)}, u32[]{:S(2)}, u32[]{:S(2)}) collective-permute-start(bf16[32,64,128]{2,1,0:T(8,128)(2,1)S(1)} %get-tuple-element.26), channel_id=1, source_target_pairs={{1,97},{3,31},{125,29},{127,99},{129,225},{131,159},{253,157},{255... | collective-permute-start | bytes 1572872 | tf_op jit(solution)/shard_map/ppermute | solution.py:205
  10.9 18.7 %collective-permute-start.4 = (bf16[16,64,128]{2,1,0:T(8,128)(2,1)S(1)}, bf16[16,64,128]{2,1,0:T(8,128)(2,1)S(1)}, u32[]{:S(2)}, u32[]{:S(2)}) collective-permute-start(bf16[16,64,128]{2,1,0:T(8,128)(2,1)S(1)} %get-tuple-element.29), channel_id=1, source_target_pairs={{0,1},{1,0},{2,3},{3,2},{4,5},{5,4},{6,7},{7,6},{8,9},{9,8},{10,11... | collective-permute-start | bytes 786440 | tf_op jit(solution)/shard_map/ppermute | solution.py:209
  15.2 14.5 %collective-permute-start.5 = (bf16[16,64,128]{2,1,0:T(8,128)(2,1)S(1)}, bf16[16,64,128]{2,1,0:T(8,128)(2,1)S(1)}, u32[]{:S(2)}, u32[]{:S(2)}) collective-permute-start(bf16[16,64,128]{2,1,0:T(8,128)(2,1)S(1)} %get-tuple-element.30), channel_id=1, source_target_pairs={{0,3},{1,2},{2,1},{3,0},{4,7},{5,6},{6,5},{7,4},{8,11},{9,10},{10,... | collective-permute-start | bytes 786440 | tf_op jit(solution)/shard_map/ppermute | solution.py:208
  22.7 7.8 %collective-permute-start.2 = (bf16[32,64,128]{2,1,0:T(8,128)(2,1)S(1)}, bf16[32,64,128]{2,1,0:T(8,128)(2,1)S(1)}, u32[]{:S(2)}, u32[]{:S(2)}) collective-permute-start(bf16[32,64,128]{2,1,0:T(8,128)(2,1)S(1)} %get-tuple-element.27), channel_id=1, source_target_pairs={{0,508},{2,510},{4,8},{5,9},{6,10},{7,11},{8,4},{9,5},{10,6},{11,7... | collective-permute-start | bytes 1572872 | tf_op jit(solution)/shard_map/ppermute | solution.py:206
  23.4 9.9 %collective-permute-start.3 = (bf16[32,64,128]{2,1,0:T(8,128)(2,1)S(1)}, bf16[32,64,128]{2,1,0:T(8,128)(2,1)S(1)}, u32[]{:S(2)}, u32[]{:S(2)}) collective-permute-start(bf16[32,64,128]{2,1,0:T(8,128)(2,1)S(1)} %get-tuple-element.28), channel_id=1, source_target_pairs={{0,4},{1,5},{2,6},{3,7},{4,0},{5,1},{6,2},{7,3},{8,12},{9,13},{10,... | collective-permute-start | bytes 1572872 | tf_op jit(solution)/shard_map/ppermute | solution.py:207
  25.4 14.4 %collective-permute-start.1 = (bf16[32,64,128]{2,1,0:T(8,128)(2,1)S(1)}, bf16[32,64,128]{2,1,0:T(8,128)(2,1)S(1)}, u32[]{:S(2)}, u32[]{:S(2)}) collective-permute-start(bf16[32,64,128]{2,1,0:T(8,128)(2,1)S(1)} %collective-permute-done), channel_id=1, source_target_pairs={{97,509},{31,511},{29,129},{99,131},{225,125},{159,127},{157,257},... | collective-permute-start | bytes 1572872 | tf_op jit(solution)/shard_map/ppermute | solution.py:219
  42.5 13.1 %collective-permute-start.6 = (bf16[32,64,128]{2,1,0:T(8,128)(2,1)S(1)}, bf16[32,64,128]{2,1,0:T(8,128)(2,1)S(1)}, u32[]{:S(2)}, u32[]{:S(2)}) collective-permute-start(bf16[32,64,128]{2,1,0:T(8,128)(2,1)S(1)} %get-tuple-element.31), channel_id=1, source_target_pairs={{1,97},{3,31},{125,29},{127,99},{129,225},{131,159},{253,157},{255... | collective-permute-start | bytes 1572872 | tf_op jit(solution)/shard_map/ppermute | solution.py:205
  47.3 12.5 %collective-permute-start.10 = (bf16[16,64,128]{2,1,0:T(8,128)(2,1)S(1)}, bf16[16,64,128]{2,1,0:T(8,128)(2,1)S(1)}, u32[]{:S(2)}, u32[]{:S(2)}) collective-permute-start(bf16[16,64,128]{2,1,0:T(8,128)(2,1)S(1)} %get-tuple-element.36), channel_id=1, source_target_pairs={{0,1},{1,0},{2,3},{3,2},{4,5},{5,4},{6,7},{7,6},{8,9},{9,8},{10,11... | collective-permute-start | bytes 786440 | tf_op jit(solution)/shard_map/ppermute | solution.py:209
  51.0 10.9 %collective-permute-start.11 = (bf16[16,64,128]{2,1,0:T(8,128)(2,1)S(1)}, bf16[16,64,128]{2,1,0:T(8,128)(2,1)S(1)}, u32[]{:S(2)}, u32[]{:S(2)}) collective-permute-start(bf16[16,64,128]{2,1,0:T(8,128)(2,1)S(1)} %get-tuple-element.37), channel_id=1, source_target_pairs={{0,3},{1,2},{2,1},{3,0},{4,7},{5,6},{6,5},{7,4},{8,11},{9,10},{10,... | collective-permute-start | bytes 786440 | tf_op jit(solution)/shard_map/ppermute | solution.py:208
  52.9 9.8 %collective-permute-start.8 = (bf16[32,64,128]{2,1,0:T(8,128)(2,1)S(1)}, bf16[32,64,128]{2,1,0:T(8,128)(2,1)S(1)}, u32[]{:S(2)}, u32[]{:S(2)}) collective-permute-start(bf16[32,64,128]{2,1,0:T(8,128)(2,1)S(1)} %get-tuple-element.32), channel_id=1, source_target_pairs={{0,508},{2,510},{4,8},{5,9},{6,10},{7,11},{8,4},{9,5},{10,6},{11,7... | collective-permute-start | bytes 1572872 | tf_op jit(solution)/shard_map/ppermute | solution.py:206
  53.6 9.9 %collective-permute-start.9 = (bf16[32,64,128]{2,1,0:T(8,128)(2,1)S(1)}, bf16[32,64,128]{2,1,0:T(8,128)(2,1)S(1)}, u32[]{:S(2)}, u32[]{:S(2)}) collective-permute-start(bf16[32,64,128]{2,1,0:T(8,128)(2,1)S(1)} %get-tuple-element.33), channel_id=1, source_target_pairs={{0,4},{1,5},{2,6},{3,7},{4,0},{5,1},{6,2},{7,3},{8,12},{9,13},{10,... | collective-permute-start | bytes 1572872 | tf_op jit(solution)/shard_map/ppermute | solution.py:207
  55.6 14.4 %collective-permute-start.7 = (bf16[32,64,128]{2,1,0:T(8,128)(2,1)S(1)}, bf16[32,64,128]{2,1,0:T(8,128)(2,1)S(1)}, u32[]{:S(2)}, u32[]{:S(2)}) collective-permute-start(bf16[32,64,128]{2,1,0:T(8,128)(2,1)S(1)} %collective-permute-done.6), channel_id=1, source_target_pairs={{97,509},{31,511},{29,129},{99,131},{225,125},{159,127},{157,257},... | collective-permute-start | bytes 1572872 | tf_op jit(solution)/shard_map/ppermute | solution.py:219
  72.9 15.2 %collective-permute-start.12 = (bf16[32,64,128]{2,1,0:T(8,128)(2,1)S(1)}, bf16[32,64,128]{2,1,0:T(8,128)(2,1)S(1)}, u32[]{:S(2)}, u32[]{:S(2)}) collective-permute-start(bf16[32,64,128]{2,1,0:T(8,128)(2,1)S(1)} %get-tuple-element.38), channel_id=1, source_target_pairs={{1,97},{3,31},{125,29},{127,99},{129,225},{131,159},{253,157},{255... | collective-permute-start | bytes 1572872 | tf_op jit(solution)/shard_map/ppermute | solution.py:205
  79.1 13.2 %collective-permute-start.16 = (bf16[16,64,128]{2,1,0:T(8,128)(2,1)S(1)}, bf16[16,64,128]{2,1,0:T(8,128)(2,1)S(1)}, u32[]{:S(2)}, u32[]{:S(2)}) collective-permute-start(bf16[16,64,128]{2,1,0:T(8,128)(2,1)S(1)} %get-tuple-element.43), channel_id=1, source_target_pairs={{0,1},{1,0},{2,3},{3,2},{4,5},{5,4},{6,7},{7,6},{8,9},{9,8},{10,11... | collective-permute-start | bytes 786440 | tf_op jit(solution)/shard_map/ppermute | solution.py:209
  83.1 15.7 %collective-permute-start.17 = (bf16[16,64,128]{2,1,0:T(8,128)(2,1)S(1)}, bf16[16,64,128]{2,1,0:T(8,128)(2,1)S(1)}, u32[]{:S(2)}, u32[]{:S(2)}) collective-permute-start(bf16[16,64,128]{2,1,0:T(8,128)(2,1)S(1)} %get-tuple-element.44), channel_id=1, source_target_pairs={{0,3},{1,2},{2,1},{3,0},{4,7},{5,6},{6,5},{7,4},{8,11},{9,10},{10,... | collective-permute-start | bytes 786440 | tf_op jit(solution)/shard_map/ppermute | solution.py:208
  85.4 14.3 %collective-permute-start.14 = (bf16[32,64,128]{2,1,0:T(8,128)(2,1)S(1)}, bf16[32,64,128]{2,1,0:T(8,128)(2,1)S(1)}, u32[]{:S(2)}, u32[]{:S(2)}) collective-permute-start(bf16[32,64,128]{2,1,0:T(8,128)(2,1)S(1)} %get-tuple-element.39), channel_id=1, source_target_pairs={{0,508},{2,510},{4,8},{5,9},{6,10},{7,11},{8,4},{9,5},{10,6},{11,7... | collective-permute-start | bytes 1572872 | tf_op jit(solution)/shard_map/ppermute | solution.py:206
  86.1 13.6 %collective-permute-start.15 = (bf16[32,64,128]{2,1,0:T(8,128)(2,1)S(1)}, bf16[32,64,128]{2,1,0:T(8,128)(2,1)S(1)}, u32[]{:S(2)}, u32[]{:S(2)}) collective-permute-start(bf16[32,64,128]{2,1,0:T(8,128)(2,1)S(1)} %get-tuple-element.40), channel_id=1, source_target_pairs={{0,4},{1,5},{2,6},{3,7},{4,0},{5,1},{6,2},{7,3},{8,12},{9,13},{10,... | collective-permute-start | bytes 1572872 | tf_op jit(solution)/shard_map/ppermute | solution.py:207
  88.0 14.4 %collective-permute-start.13 = (bf16[32,64,128]{2,1,0:T(8,128)(2,1)S(1)}, bf16[32,64,128]{2,1,0:T(8,128)(2,1)S(1)}, u32[]{:S(2)}, u32[]{:S(2)}) collective-permute-start(bf16[32,64,128]{2,1,0:T(8,128)(2,1)S(1)} %collective-permute-done.12), channel_id=1, source_target_pairs={{97,509},{31,511},{29,129},{99,131},{225,125},{159,127},{157,257},... | collective-permute-start | bytes 1572872 | tf_op jit(solution)/shard_map/ppermute | solution.py:219
  92.3 10.2 %copy-start.3 = (bf16[1,2,4,4,64,64]{5,4,3,2,1,0:T(8,128)(2,1)S(1)}, bf16[1,2,4,4,64,64]{5,4,3,2,1,0:T(8,128)(2,1)}, u32[]{:S(2)}) copy-start(bf16[1,2,4,4,64,64]{5,4,3,2,1,0:T(8,128)(2,1)} %param.11) | copy-start | bytes 786436
  98.8 3.7 %copy-start.4 = (s32[1,2,4,4]{3,2,1,0:T(4,128)S(1)}, s32[1,2,4,4]{3,2,1,0:T(4,128)}, u32[]{:S(2)}) copy-start(s32[1,2,4,4]{3,2,1,0:T(4,128)} %labels.1) | copy-start | bytes 388
  104.6 6.8 %collective-permute-start.18 = (bf16[8,64,128]{2,1,0:T(8,128)(2,1)S(1)}, bf16[8,64,128]{2,1,0:T(8,128)(2,1)S(1)}, u32[]{:S(2)}, u32[]{:S(2)}) collective-permute-start(bf16[8,64,128]{2,1,0:T(8,128)(2,1)S(1)} %get-tuple-element.47), channel_id=1, source_target_pairs={{0,1},{1,0},{2,3},{3,2},{4,5},{5,4},{6,7},{7,6},{8,9},{9,8},{10,11... | collective-permute-start | bytes 393224 | tf_op jit(solution)/shard_map/ppermute | solution.py:250
  112.0 7.3 %collective-permute-start.19 = (bf16[4,64,128]{2,1,0:T(8,128)(2,1)S(1)}, bf16[4,64,128]{2,1,0:T(8,128)(2,1)S(1)}, u32[]{:S(2)}, u32[]{:S(2)}) collective-permute-start(bf16[4,64,128]{2,1,0:T(8,128)(2,1)S(1)} %get-tuple-element.49), channel_id=1, source_target_pairs={{0,2},{1,3},{2,0},{3,1},{4,6},{5,7},{6,4},{7,5},{8,10},{9,11},{10,... | collective-permute-start | bytes 196616 | tf_op jit(solution)/shard_map/ppermute | solution.py:258

commit v6 on v5

--- a/solution.py
+++ b/solution.py
@@ -14,7 +14,6 @@
 BF16 = jnp.bfloat16
 VMEM = pl.BlockSpec(memory_space=pltpu.VMEM)
 SMEM = pl.BlockSpec(memory_space=pltpu.SMEM)
-LONG = pl.CostEstimate(flops=10_000_000_000, bytes_accessed=0, transcendentals=0)
 PARAMS = pltpu.CompilerParams(vmem_limit_bytes=12 * 1024 * 1024)
 
 GROUP = 32
@@ -213,7 +212,6 @@
             in_specs=[SMEM] + [VMEM] * 5,
             out_specs=VMEM,
             input_output_aliases={1: 0} if sweep else {},
-            cost_estimate=LONG,
             compiler_params=PARAMS,
         )(scales, estimate, b, vector, selfs, hops)
         relayed = lax.ppermute(at_relay, both, back)

time: 121 us -> 128 us (1.058)
  the two profiles are of different devices: /device:TPU:1 before, /device:TPU:14 now
where the time goes in v6:
time: 128 us; the launch traced here: 127 us
  starting transfers between devices  74.8 us (58%)
  waiting for transfers between devices  26.3 us (21%)
  Pallas kernels  21.3 us (17%)
  local copies, waits for them, and re-layouts  3.07 us (2%)
    ppermute x3, starting transfers between devices, shards(): from_z_inner = lax.ppermute(sent[3], 'gz', z_inner)  38.4 us
    ppermute x3, waiting for transfers between devices, shards(): from_z_outer = lax.ppermute(sent[2], 'gz', z_outer)  20.9 us
    ppermute x3, starting transfers between devices, shards(): t_outer = lax.ppermute(sent[0], both, outer)  15.1 us
    pallas_call x3, Pallas kernels, shards(): pl.pallas_call(functools.partial(local_terms, (zs, xs, ys, d)), out_shape...  8.79 us
    ppermute x3, starting transfers between devices, shards(): from_z_outer = lax.ppermute(sent[2], 'gz', z_outer)  7.48 us
    ppermute x3, starting transfers between devices, shards(): t_inner = lax.ppermute(sent[1], both, inner)  5.76 us
    pallas_call x2, Pallas kernels, shards(): pl.pallas_call(sweep_end, out_shape=(wide, field) + messages, in_specs=[S...  5.39 us
    ppermute x1, waiting for transfers between devices, shards(): from_chip = lax.ppermute(away, 'gz', [(i, i ^ 2) for i in range(members)])  4.23 us
  transfers between devices with their start and end apart: 20, of which 5 were waited for; matrix products, arithmetic and copies ran while one was open for 0% of the time, Pallas kernels for 9%

profile of v6, /device:TPU:14, one launch (start us, length us, event | category | flops | bytes accessed | tf_op | source)
XLA Modules:
  0.0 127.4 jit_solution(10960996026973805709)
XLA Ops:
  0.7 0.0 copy-start.6
  0.7 0.7 copy-done.6
  1.3 0.1 reshape.37.scales
  1.5 0.1 pad_add_fusion.role
  1.5 0.0 copy-start
  1.5 1.2 copy-done
  2.8 1.0 copy-done.2
  3.8 1.8 %shard_map.77 = (bf16[32,64,128]{2,1,0:T(8,128)(2,1)S(1)}, bf16[32,64,128]{2,1,0:T(8,128)(2,1)S(1)}, bf16[16,64,128]{2,1,0:T(8,128)(2,1)S(1)}, bf16[16,64,128]{2,1,0:T(8,128)(2,1)S(1)}, bf16[32,64,128]{2,1,0:T(8,128)(2,1)S(1)}) custom-call(s32[4]{0:T(128)S(1)} %pad_add_fusion.role, f32[160]{0:T(256)S(1)} %reshape.37.scales, ...), custom_call_target="tpu_custom_call" | custom-call | tf_op jit(solution)/shard_map/pallas_call | solution.py:195
  5.7 0.7 collective-permute-start
  6.4 11.2 %collective-permute-start.2 = (bf16[32,64,128]{2,1,0:T(8,128)(2,1)S(1)}, bf16[32,64,128]{2,1,0:T(8,128)(2,1)S(1)}, u32[]{:S(2)}, u32[]{:S(2)}) collective-permute-start(bf16[32,64,128]{2,1,0:T(8,128)(2,1)S(1)} %get-tuple-element.27), channel_id=1, source_target_pairs={{0,508},{2,510},{4,8},{5,9},{6,10},{7,11},{8,4},{9,5},{10,6},{11,7... | collective-permute-start | bytes 1572872 | tf_op jit(solution)/shard_map/ppermute | solution.py:205
  17.6 1.9 %collective-permute-start.3 = (bf16[32,64,128]{2,1,0:T(8,128)(2,1)S(1)}, bf16[32,64,128]{2,1,0:T(8,128)(2,1)S(1)}, u32[]{:S(2)}, u32[]{:S(2)}) collective-permute-start(bf16[32,64,128]{2,1,0:T(8,128)(2,1)S(1)} %get-tuple-element.28), channel_id=1, source_target_pairs={{0,4},{1,5},{2,6},{3,7},{4,0},{5,1},{6,2},{7,3},{8,12},{9,13},{10,... | collective-permute-start | bytes 1572872 | tf_op jit(solution)/shard_map/ppermute | solution.py:206
  19.5 0.0 collective-permute-done
  19.5 0.7 collective-permute-start.1
  20.2 8.1 %collective-permute-start.4 = (bf16[16,64,128]{2,1,0:T(8,128)(2,1)S(1)}, bf16[16,64,128]{2,1,0:T(8,128)(2,1)S(1)}, u32[]{:S(2)}, u32[]{:S(2)}) collective-permute-start(bf16[16,64,128]{2,1,0:T(8,128)(2,1)S(1)} %get-tuple-element.29), channel_id=1, source_target_pairs={{0,1},{1,0},{2,3},{3,2},{4,5},{5,4},{6,7},{7,6},{8,9},{9,8},{10,11... | collective-permute-start | bytes 786440 | tf_op jit(solution)/shard_map/ppermute | solution.py:208
  28.4 3.6 %collective-permute-start.5 = (bf16[16,64,128]{2,1,0:T(8,128)(2,1)S(1)}, bf16[16,64,128]{2,1,0:T(8,128)(2,1)S(1)}, u32[]{:S(2)}, u32[]{:S(2)}) collective-permute-start(bf16[16,64,128]{2,1,0:T(8,128)(2,1)S(1)} %get-tuple-element.30), channel_id=1, source_target_pairs={{0,3},{1,2},{2,1},{3,0},{4,7},{5,6},{6,5},{7,4},{8,11},{9,10},{10,... | collective-permute-start | bytes 786440 | tf_op jit(solution)/shard_map/ppermute | solution.py:207
  32.0 0.0 copy-done.1
  32.0 0.0 copy-done.3
  32.0 2.9 %shard_map.78.partial = f32[32,64,128]{2,1,0:T(8,128)S(1)} custom-call(f32[160]{0:T(256)S(1)} %reshape.37.scales, bf16[32,64,128]{2,1,0:T(8,128)(2,1)S(1)} %bitcast.22, bf16[32,64,128]{2,1,0:T(8,128)(2,1)S(1)} %bitcast.23, bf16[32,64,128]{2,1,0:T(8,128)(2,1)S(1)} %bitcast.24, bf16[32,64,64]{2,1,0:T(8,128)(2,1)S(1)} %bitcast.27, bf16[32,64,256]{2,1,0:T(8,128)(2,1)S(1)} %bitcast.12), custom_call_target="tpu_custom_call" | custom-call | tf_op jit(solution)/shard_map/pallas_call | solution.py:209
  35.0 0.0 collective-permute-done.4.z_inner
  35.0 6.0 %collective-permute-done.5.z_outer = bf16[16,64,128]{2,1,0:T(8,128)(2,1)S(1)} collective-permute-done((bf16[16,64,128]{2,1,0:T(8,128)(2,1)S(1)}, bf16[16,64,128]{2,1,0:T(8,128)(2,1)S(1)}, u32[]{:S(2)}, u32[]{:S(2)}) %collective-permute-start.5) | collective-permute-done | bytes 262176 | tf_op jit(solution)/shard_map/ppermute | solution.py:207
  41.0 0.9 shard_map.79.partial
  41.8 0.0 collective-permute-done.2.outer
  41.8 0.0 collective-permute-done.3.inner
  41.8 0.0 collective-permute-done.1.relayed
  41.9 2.6 %shard_map.80 = (f32[32,64,128]{2,1,0:T(8,128)S(1)}, bf16[32,64,128]{2,1,0:T(8,128)(2,1)S(1)}, bf16[32,64,128]{2,1,0:T(8,128)(2,1)S(1)}, bf16[32,64,128]{2,1,0:T...) custom-call(s32[4]{0:T(128)S(1)} %pad_add_fusion.role, ...), custom_call_target="tpu_custom_call", output_to_operand_aliasing={{0}: (5, {})} | custom-call | tf_op jit(solution)/shard_map/pallas_call | solution.py:228
  44.5 0.7 collective-permute-start.6
  45.2 1.9 %collective-permute-start.8 = (bf16[32,64,128]{2,1,0:T(8,128)(2,1)S(1)}, bf16[32,64,128]{2,1,0:T(8,128)(2,1)S(1)}, u32[]{:S(2)}, u32[]{:S(2)}) collective-permute-start(bf16[32,64,128]{2,1,0:T(8,128)(2,1)S(1)} %get-tuple-element.32), channel_id=1, source_target_pairs={{0,508},{2,510},{4,8},{5,9},{6,10},{7,11},{8,4},{9,5},{10,6},{11,7... | collective-permute-start | bytes 1572872 | tf_op jit(solution)/shard_map/ppermute | solution.py:205
  47.1 1.9 %collective-permute-start.9 = (bf16[32,64,128]{2,1,0:T(8,128)(2,1)S(1)}, bf16[32,64,128]{2,1,0:T(8,128)(2,1)S(1)}, u32[]{:S(2)}, u32[]{:S(2)}) collective-permute-start(bf16[32,64,128]{2,1,0:T(8,128)(2,1)S(1)} %get-tuple-element.33), channel_id=1, source_target_pairs={{0,4},{1,5},{2,6},{3,7},{4,0},{5,1},{6,2},{7,3},{8,12},{9,13},{10,... | collective-permute-start | bytes 1572872 | tf_op jit(solution)/shard_map/ppermute | solution.py:206
  49.0 0.0 collective-permute-done.6
  49.0 0.7 collective-permute-start.7
  49.7 15.2 %collective-permute-start.10 = (bf16[16,64,128]{2,1,0:T(8,128)(2,1)S(1)}, bf16[16,64,128]{2,1,0:T(8,128)(2,1)S(1)}, u32[]{:S(2)}, u32[]{:S(2)}) collective-permute-start(bf16[16,64,128]{2,1,0:T(8,128)(2,1)S(1)} %get-tuple-element.36), channel_id=1, source_target_pairs={{0,1},{1,0},{2,3},{3,2},{4,5},{5,4},{6,7},{7,6},{8,9},{9,8},{10,11... | collective-permute-start | bytes 786440 | tf_op jit(solution)/shard_map/ppermute | solution.py:208
  64.9 1.9 %collective-permute-start.11 = (bf16[16,64,128]{2,1,0:T(8,128)(2,1)S(1)}, bf16[16,64,128]{2,1,0:T(8,128)(2,1)S(1)}, u32[]{:S(2)}, u32[]{:S(2)}) collective-permute-start(bf16[16,64,128]{2,1,0:T(8,128)(2,1)S(1)} %get-tuple-element.37), channel_id=1, source_target_pairs={{0,3},{1,2},{2,1},{3,0},{4,7},{5,6},{6,5},{7,4},{8,11},{9,10},{10,... | collective-permute-start | bytes 786440 | tf_op jit(solution)/shard_map/ppermute | solution.py:207
  66.9 2.9 %shard_map.81.partial = f32[32,64,128]{2,1,0:T(8,128)S(1)} custom-call(f32[160]{0:T(256)S(1)} %reshape.37.scales, f32[32,64,128]{2,1,0:T(8,128)S(1)} %get-tuple-element.34.estimate, bf16[32,64,128]{2,1,0:T(8,128)(2,1)S(1)} %bitcast.25, bf16[32,64,128]{2,1,0:T(8,128)(2,1)S(1)} %get-tuple-element.35.vector, ...), custom_call_target="tpu_custom_call", output_to_operand_aliasing={{}: (1, {})} | custom-call | tf_op jit(solution)/shard_map/pallas_call | solution.py:209
  69.8 0.0 collective-permute-done.10.z_inner
  69.8 7.5 %collective-permute-done.11.z_outer = bf16[16,64,128]{2,1,0:T(8,128)(2,1)S(1)} collective-permute-done((bf16[16,64,128]{2,1,0:T(8,128)(2,1)S(1)}, bf16[16,64,128]{2,1,0:T(8,128)(2,1)S(1)}, u32[]{:S(2)}, u32[]{:S(2)}) %collective-permute-start.11) | collective-permute-done | bytes 262176 | tf_op jit(solution)/shard_map/ppermute | solution.py:207
  77.3 0.9 shard_map.82.partial
  78.2 0.0 collective-permute-done.8.outer
  78.2 0.0 collective-permute-done.9.inner
  78.2 0.0 collective-permute-done.7.relayed
  78.2 2.8 %shard_map.83 = (f32[32,64,128]{2,1,0:T(8,128)S(1)}, bf16[32,64,128]{2,1,0:T(8,128)(2,1)S(1)}, bf16[32,64,128]{2,1,0:T(8,128)(2,1)S(1)}, bf16[32,64,128]{2,1,0:T...) custom-call(s32[4]{0:T(128)S(1)} %pad_add_fusion.role, ...), custom_call_target="tpu_custom_call", output_to_operand_aliasing={{0}: (5, {})} | custom-call | tf_op jit(solution)/shard_map/pallas_call | solution.py:228
  81.0 0.7 collective-permute-start.12
  81.7 1.9 %collective-permute-start.14 = (bf16[32,64,128]{2,1,0:T(8,128)(2,1)S(1)}, bf16[32,64,128]{2,1,0:T(8,128)(2,1)S(1)}, u32[]{:S(2)}, u32[]{:S(2)}) collective-permute-start(bf16[32,64,128]{2,1,0:T(8,128)(2,1)S(1)} %get-tuple-element.39), channel_id=1, source_target_pairs={{0,508},{2,510},{4,8},{5,9},{6,10},{7,11},{8,4},{9,5},{10,6},{11,7... | collective-permute-start | bytes 1572872 | tf_op jit(solution)/shard_map/ppermute | solution.py:205
  83.6 1.9 %collective-permute-start.15 = (bf16[32,64,128]{2,1,0:T(8,128)(2,1)S(1)}, bf16[32,64,128]{2,1,0:T(8,128)(2,1)S(1)}, u32[]{:S(2)}, u32[]{:S(2)}) collective-permute-start(bf16[32,64,128]{2,1,0:T(8,128)(2,1)S(1)} %get-tuple-element.40), channel_id=1, source_target_pairs={{0,4},{1,5},{2,6},{3,7},{4,0},{5,1},{6,2},{7,3},{8,12},{9,13},{10,... | collective-permute-start | bytes 1572872 | tf_op jit(solution)/shard_map/ppermute | solution.py:206
  85.5 0.0 collective-permute-done.12
  85.6 0.7 collective-permute-start.13
  86.3 15.1 %collective-permute-start.16 = (bf16[16,64,128]{2,1,0:T(8,128)(2,1)S(1)}, bf16[16,64,128]{2,1,0:T(8,128)(2,1)S(1)}, u32[]{:S(2)}, u32[]{:S(2)}) collective-permute-start(bf16[16,64,128]{2,1,0:T(8,128)(2,1)S(1)} %get-tuple-element.43), channel_id=1, source_target_pairs={{0,1},{1,0},{2,3},{3,2},{4,5},{5,4},{6,7},{7,6},{8,9},{9,8},{10,11... | collective-permute-start | bytes 786440 | tf_op jit(solution)/shard_map/ppermute | solution.py:208
  101.4 1.9 %collective-permute-start.17 = (bf16[16,64,128]{2,1,0:T(8,128)(2,1)S(1)}, bf16[16,64,128]{2,1,0:T(8,128)(2,1)S(1)}, u32[]{:S(2)}, u32[]{:S(2)}) collective-permute-start(bf16[16,64,128]{2,1,0:T(8,128)(2,1)S(1)} %get-tuple-element.44), channel_id=1, source_target_pairs={{0,3},{1,2},{2,1},{3,0},{4,7},{5,6},{6,5},{7,4},{8,11},{9,10},{10,... | collective-permute-start | bytes 786440 | tf_op jit(solution)/shard_map/ppermute | solution.py:207
  103.3 2.9 %shard_map.84.partial = f32[32,64,128]{2,1,0:T(8,128)S(1)} custom-call(f32[160]{0:T(256)S(1)} %reshape.37.scales, f32[32,64,128]{2,1,0:T(8,128)S(1)} %get-tuple-element.41.estimate, bf16[32,64,128]{2,1,0:T(8,128)(2,1)S(1)} %bitcast.26, bf16[32,64,128]{2,1,0:T(8,128)(2,1)S(1)} %get-tuple-element.42.vector, ...), custom_call_target="tpu_custom_call", output_to_operand_aliasing={{}: (1, {})} | custom-call | tf_op jit(solution)/shard_map/pallas_call | solution.py:209
  106.3 0.0 copy-start.4
  106.3 0.0 collective-permute-done.16.z_inner
  106.3 7.4 %collective-permute-done.17.z_outer = bf16[16,64,128]{2,1,0:T(8,128)(2,1)S(1)} collective-permute-done((bf16[16,64,128]{2,1,0:T(8,128)(2,1)S(1)}, bf16[16,64,128]{2,1,0:T(8,128)(2,1)S(1)}, u32[]{:S(2)}, u32[]{:S(2)}) %collective-permute-start.17) | collective-permute-done | bytes 262176 | tf_op jit(solution)/shard_map/ppermute | solution.py:207
  113.7 0.9 shard_map.85.partial
  114.6 0.0 collective-permute-done.14.outer
  114.6 0.0 collective-permute-done.15.inner
  114.6 0.0 collective-permute-done.13.relayed
  114.6 0.0 copy-done.4
  114.6 0.0 copy-done.5
  114.6 2.1 %shard_map.86 = (bf16[32,64,128]{2,1,0:T(8,128)(2,1)}, f32[8,64,128]{2,1,0:T(8,128)S(1)}, bf16[8,64,128]{2,1,0:T(8,128)(2,1)S(1)}) custom-call(s32[4]{0:T(128)S(1)} %pad_add_fusion.role, f32[160]{0:T(256)S(1)} %reshape.37.scales, s32[1,2,4,4]{3,2,1,0:T(4,128)S(1)} %copy-done.5, bf16[32,64,128]{2,1,0:T(8,128)(2,1)S(1)} %collective-permute-done.13.relayed, ...), custom_call_target="tpu_custom_call" | custom-call | tf_op jit(solution)/shard_map/pallas_call | solution.py:240
  116.7 2.0 %collective-permute-start.18 = (bf16[8,64,128]{2,1,0:T(8,128)(2,1)S(1)}, bf16[8,64,128]{2,1,0:T(8,128)(2,1)S(1)}, u32[]{:S(2)}, u32[]{:S(2)}) collective-permute-start(bf16[8,64,128]{2,1,0:T(8,128)(2,1)S(1)} %get-tuple-element.47), channel_id=1, source_target_pairs={{0,1},{1,0},{2,3},{3,2},{4,5},{5,4},{6,7},{7,6},{8,9},{9,8},{10,11... | collective-permute-start | bytes 393224 | tf_op jit(solution)/shard_map/ppermute | solution.py:248
  118.8 1.2 collective-permute-done.18.came
  120.0 0.6 shard_map.87
  120.6 1.9 %collective-permute-start.19 = (bf16[4,64,128]{2,1,0:T(8,128)(2,1)S(1)}, bf16[4,64,128]{2,1,0:T(8,128)(2,1)S(1)}, u32[]{:S(2)}, u32[]{:S(2)}) collective-permute-start(bf16[4,64,128]{2,1,0:T(8,128)(2,1)S(1)} %get-tuple-element.49), channel_id=1, source_target_pairs={{0,2},{1,3},{2,0},{3,1},{4,6},{5,7},{6,4},{7,5},{8,10},{9,11},{10,... | collective-permute-start | bytes 196616 | tf_op jit(solution)/shard_map/ppermute | solution.py:256
  122.5 4.2 %collective-permute-done.19 = bf16[4,64,128]{2,1,0:T(8,128)(2,1)S(1)} collective-permute-done((bf16[4,64,128]{2,1,0:T(8,128)(2,1)S(1)}, bf16[4,64,128]{2,1,0:T(8,128)(2,1)S(1)}, u32[]{:S(2)}, u32[]{:S(2)}) %collective-permute-start.19) | collective-permute-done | bytes 65568 | tf_op jit(solution)/shard_map/ppermute | solution.py:256
  126.7 0.7 add_bitcast_fusion
  (4 shorter events, 0.0 us)
Async XLA Ops:
  0.7 0.7 copy-start.6
  1.5 1.2 copy-start
  2.8 1.0 copy-start.2
  3.8 28.2 %copy-start.1 = (bf16[1,2,4,4,64,256]{5,4,3,2,1,0:T(8,128)(2,1)S(1)}, bf16[1,2,4,4,64,256]{5,4,3,2,1,0:T(8,128)(2,1)}, u32[]{:S(2)}) copy-start(bf16[1,2,4,4,64,256]{5,4,3,2,1,0:T(8,128)(2,1)} %param.8) | copy-start | bytes 3145732
  3.8 28.2 %copy-start.3 = (bf16[1,2,4,4,64,64]{5,4,3,2,1,0:T(8,128)(2,1)S(1)}, bf16[1,2,4,4,64,64]{5,4,3,2,1,0:T(8,128)(2,1)}, u32[]{:S(2)}) copy-start(bf16[1,2,4,4,64,64]{5,4,3,2,1,0:T(8,128)(2,1)} %param.7) | copy-start | bytes 786436
  5.7 13.9 %collective-permute-start = (bf16[32,64,128]{2,1,0:T(8,128)(2,1)S(1)}, bf16[32,64,128]{2,1,0:T(8,128)(2,1)S(1)}, u32[]{:S(2)}, u32[]{:S(2)}) collective-permute-start(bf16[32,64,128]{2,1,0:T(8,128)(2,1)S(1)} %get-tuple-element.26), channel_id=1, source_target_pairs={{1,97},{3,31},{125,29},{127,99},{129,225},{131,159},{253,157},{255... | collective-permute-start | bytes 1572872 | tf_op jit(solution)/shard_map/ppermute | solution.py:204
  6.4 35.5 %collective-permute-start.2 = (bf16[32,64,128]{2,1,0:T(8,128)(2,1)S(1)}, bf16[32,64,128]{2,1,0:T(8,128)(2,1)S(1)}, u32[]{:S(2)}, u32[]{:S(2)}) collective-permute-start(bf16[32,64,128]{2,1,0:T(8,128)(2,1)S(1)} %get-tuple-element.27), channel_id=1, source_target_pairs={{0,508},{2,510},{4,8},{5,9},{6,10},{7,11},{8,4},{9,5},{10,6},{11,7... | collective-permute-start | bytes 1572872 | tf_op jit(solution)/shard_map/ppermute | solution.py:205
  17.6 24.3 %collective-permute-start.3 = (bf16[32,64,128]{2,1,0:T(8,128)(2,1)S(1)}, bf16[32,64,128]{2,1,0:T(8,128)(2,1)S(1)}, u32[]{:S(2)}, u32[]{:S(2)}) collective-permute-start(bf16[32,64,128]{2,1,0:T(8,128)(2,1)S(1)} %get-tuple-element.28), channel_id=1, source_target_pairs={{0,4},{1,5},{2,6},{3,7},{4,0},{5,1},{6,2},{7,3},{8,12},{9,13},{10,... | collective-permute-start | bytes 1572872 | tf_op jit(solution)/shard_map/ppermute | solution.py:206
  19.5 22.3 %collective-permute-start.1 = (bf16[32,64,128]{2,1,0:T(8,128)(2,1)S(1)}, bf16[32,64,128]{2,1,0:T(8,128)(2,1)S(1)}, u32[]{:S(2)}, u32[]{:S(2)}) collective-permute-start(bf16[32,64,128]{2,1,0:T(8,128)(2,1)S(1)} %collective-permute-done), channel_id=1, source_target_pairs={{97,509},{31,511},{29,129},{99,131},{225,125},{159,127},{157,257},... | collective-permute-start | bytes 1572872 | tf_op jit(solution)/shard_map/ppermute | solution.py:217
  20.2 14.7 %collective-permute-start.4 = (bf16[16,64,128]{2,1,0:T(8,128)(2,1)S(1)}, bf16[16,64,128]{2,1,0:T(8,128)(2,1)S(1)}, u32[]{:S(2)}, u32[]{:S(2)}) collective-permute-start(bf16[16,64,128]{2,1,0:T(8,128)(2,1)S(1)} %get-tuple-element.29), channel_id=1, source_target_pairs={{0,1},{1,0},{2,3},{3,2},{4,5},{5,4},{6,7},{7,6},{8,9},{9,8},{10,11... | collective-permute-start | bytes 786440 | tf_op jit(solution)/shard_map/ppermute | solution.py:208
  28.4 12.6 %collective-permute-start.5 = (bf16[16,64,128]{2,1,0:T(8,128)(2,1)S(1)}, bf16[16,64,128]{2,1,0:T(8,128)(2,1)S(1)}, u32[]{:S(2)}, u32[]{:S(2)}) collective-permute-start(bf16[16,64,128]{2,1,0:T(8,128)(2,1)S(1)} %get-tuple-element.30), channel_id=1, source_target_pairs={{0,3},{1,2},{2,1},{3,0},{4,7},{5,6},{6,5},{7,4},{8,11},{9,10},{10,... | collective-permute-start | bytes 786440 | tf_op jit(solution)/shard_map/ppermute | solution.py:207
  44.5 4.6 %collective-permute-start.6 = (bf16[32,64,128]{2,1,0:T(8,128)(2,1)S(1)}, bf16[32,64,128]{2,1,0:T(8,128)(2,1)S(1)}, u32[]{:S(2)}, u32[]{:S(2)}) collective-permute-start(bf16[32,64,128]{2,1,0:T(8,128)(2,1)S(1)} %get-tuple-element.31), channel_id=1, source_target_pairs={{1,97},{3,31},{125,29},{127,99},{129,225},{131,159},{253,157},{255... | collective-permute-start | bytes 1572872 | tf_op jit(solution)/shard_map/ppermute | solution.py:204
  45.2 33.0 %collective-permute-start.8 = (bf16[32,64,128]{2,1,0:T(8,128)(2,1)S(1)}, bf16[32,64,128]{2,1,0:T(8,128)(2,1)S(1)}, u32[]{:S(2)}, u32[]{:S(2)}) collective-permute-start(bf16[32,64,128]{2,1,0:T(8,128)(2,1)S(1)} %get-tuple-element.32), channel_id=1, source_target_pairs={{0,508},{2,510},{4,8},{5,9},{6,10},{7,11},{8,4},{9,5},{10,6},{11,7... | collective-permute-start | bytes 1572872 | tf_op jit(solution)/shard_map/ppermute | solution.py:205
  47.1 31.1 %collective-permute-start.9 = (bf16[32,64,128]{2,1,0:T(8,128)(2,1)S(1)}, bf16[32,64,128]{2,1,0:T(8,128)(2,1)S(1)}, u32[]{:S(2)}, u32[]{:S(2)}) collective-permute-start(bf16[32,64,128]{2,1,0:T(8,128)(2,1)S(1)} %get-tuple-element.33), channel_id=1, source_target_pairs={{0,4},{1,5},{2,6},{3,7},{4,0},{5,1},{6,2},{7,3},{8,12},{9,13},{10,... | collective-permute-start | bytes 1572872 | tf_op jit(solution)/shard_map/ppermute | solution.py:206
  49.0 29.2 %collective-permute-start.7 = (bf16[32,64,128]{2,1,0:T(8,128)(2,1)S(1)}, bf16[32,64,128]{2,1,0:T(8,128)(2,1)S(1)}, u32[]{:S(2)}, u32[]{:S(2)}) collective-permute-start(bf16[32,64,128]{2,1,0:T(8,128)(2,1)S(1)} %collective-permute-done.6), channel_id=1, source_target_pairs={{97,509},{31,511},{29,129},{99,131},{225,125},{159,127},{157,257},... | collective-permute-start | bytes 1572872 | tf_op jit(solution)/shard_map/ppermute | solution.py:217
  49.7 20.0 %collective-permute-start.10 = (bf16[16,64,128]{2,1,0:T(8,128)(2,1)S(1)}, bf16[16,64,128]{2,1,0:T(8,128)(2,1)S(1)}, u32[]{:S(2)}, u32[]{:S(2)}) collective-permute-start(bf16[16,64,128]{2,1,0:T(8,128)(2,1)S(1)} %get-tuple-element.36), channel_id=1, source_target_pairs={{0,1},{1,0},{2,3},{3,2},{4,5},{5,4},{6,7},{7,6},{8,9},{9,8},{10,11... | collective-permute-start | bytes 786440 | tf_op jit(solution)/shard_map/ppermute | solution.py:208
  64.9 12.4 %collective-permute-start.11 = (bf16[16,64,128]{2,1,0:T(8,128)(2,1)S(1)}, bf16[16,64,128]{2,1,0:T(8,128)(2,1)S(1)}, u32[]{:S(2)}, u32[]{:S(2)}) collective-permute-start(bf16[16,64,128]{2,1,0:T(8,128)(2,1)S(1)} %get-tuple-element.37), channel_id=1, source_target_pairs={{0,3},{1,2},{2,1},{3,0},{4,7},{5,6},{6,5},{7,4},{8,11},{9,10},{10,... | collective-permute-start | bytes 786440 | tf_op jit(solution)/shard_map/ppermute | solution.py:207
  81.0 4.6 %collective-permute-start.12 = (bf16[32,64,128]{2,1,0:T(8,128)(2,1)S(1)}, bf16[32,64,128]{2,1,0:T(8,128)(2,1)S(1)}, u32[]{:S(2)}, u32[]{:S(2)}) collective-permute-start(bf16[32,64,128]{2,1,0:T(8,128)(2,1)S(1)} %get-tuple-element.38), channel_id=1, source_target_pairs={{1,97},{3,31},{125,29},{127,99},{129,225},{131,159},{253,157},{255... | collective-permute-start | bytes 1572872 | tf_op jit(solution)/shard_map/ppermute | solution.py:204
  81.7 32.9 %collective-permute-start.14 = (bf16[32,64,128]{2,1,0:T(8,128)(2,1)S(1)}, bf16[32,64,128]{2,1,0:T(8,128)(2,1)S(1)}, u32[]{:S(2)}, u32[]{:S(2)}) collective-permute-start(bf16[32,64,128]{2,1,0:T(8,128)(2,1)S(1)} %get-tuple-element.39), channel_id=1, source_target_pairs={{0,508},{2,510},{4,8},{5,9},{6,10},{7,11},{8,4},{9,5},{10,6},{11,7... | collective-permute-start | bytes 1572872 | tf_op jit(solution)/shard_map/ppermute | solution.py:205
  83.6 30.9 %collective-permute-start.15 = (bf16[32,64,128]{2,1,0:T(8,128)(2,1)S(1)}, bf16[32,64,128]{2,1,0:T(8,128)(2,1)S(1)}, u32[]{:S(2)}, u32[]{:S(2)}) collective-permute-start(bf16[32,64,128]{2,1,0:T(8,128)(2,1)S(1)} %get-tuple-element.40), channel_id=1, source_target_pairs={{0,4},{1,5},{2,6},{3,7},{4,0},{5,1},{6,2},{7,3},{8,12},{9,13},{10,... | collective-permute-start | bytes 1572872 | tf_op jit(solution)/shard_map/ppermute | solution.py:206
  85.6 29.0 %collective-permute-start.13 = (bf16[32,64,128]{2,1,0:T(8,128)(2,1)S(1)}, bf16[32,64,128]{2,1,0:T(8,128)(2,1)S(1)}, u32[]{:S(2)}, u32[]{:S(2)}) collective-permute-start(bf16[32,64,128]{2,1,0:T(8,128)(2,1)S(1)} %collective-permute-done.12), channel_id=1, source_target_pairs={{97,509},{31,511},{29,129},{99,131},{225,125},{159,127},{157,257},... | collective-permute-start | bytes 1572872 | tf_op jit(solution)/shard_map/ppermute | solution.py:217
  86.3 20.0 %collective-permute-start.16 = (bf16[16,64,128]{2,1,0:T(8,128)(2,1)S(1)}, bf16[16,64,128]{2,1,0:T(8,128)(2,1)S(1)}, u32[]{:S(2)}, u32[]{:S(2)}) collective-permute-start(bf16[16,64,128]{2,1,0:T(8,128)(2,1)S(1)} %get-tuple-element.43), channel_id=1, source_target_pairs={{0,1},{1,0},{2,3},{3,2},{4,5},{5,4},{6,7},{7,6},{8,9},{9,8},{10,11... | collective-permute-start | bytes 786440 | tf_op jit(solution)/shard_map/ppermute | solution.py:208
  101.4 12.3 %collective-permute-start.17 = (bf16[16,64,128]{2,1,0:T(8,128)(2,1)S(1)}, bf16[16,64,128]{2,1,0:T(8,128)(2,1)S(1)}, u32[]{:S(2)}, u32[]{:S(2)}) collective-permute-start(bf16[16,64,128]{2,1,0:T(8,128)(2,1)S(1)} %get-tuple-element.44), channel_id=1, source_target_pairs={{0,3},{1,2},{2,1},{3,0},{4,7},{5,6},{6,5},{7,4},{8,11},{9,10},{10,... | collective-permute-start | bytes 786440 | tf_op jit(solution)/shard_map/ppermute | solution.py:207
  106.3 8.3 %copy-start.4 = (bf16[1,2,4,4,64,64]{5,4,3,2,1,0:T(8,128)(2,1)S(1)}, bf16[1,2,4,4,64,64]{5,4,3,2,1,0:T(8,128)(2,1)}, u32[]{:S(2)}) copy-start(bf16[1,2,4,4,64,64]{5,4,3,2,1,0:T(8,128)(2,1)} %param.11) | copy-start | bytes 786436
  113.7 0.9 copy-start.5
  116.7 3.2 %collective-permute-start.18 = (bf16[8,64,128]{2,1,0:T(8,128)(2,1)S(1)}, bf16[8,64,128]{2,1,0:T(8,128)(2,1)S(1)}, u32[]{:S(2)}, u32[]{:S(2)}) collective-permute-start(bf16[8,64,128]{2,1,0:T(8,128)(2,1)S(1)} %get-tuple-element.47), channel_id=1, source_target_pairs={{0,1},{1,0},{2,3},{3,2},{4,5},{5,4},{6,7},{7,6},{8,9},{9,8},{10,11... | collective-permute-start | bytes 393224 | tf_op jit(solution)/shard_map/ppermute | solution.py:248
  120.6 6.2 %collective-permute-start.19 = (bf16[4,64,128]{2,1,0:T(8,128)(2,1)S(1)}, bf16[4,64,128]{2,1,0:T(8,128)(2,1)S(1)}, u32[]{:S(2)}, u32[]{:S(2)}) collective-permute-start(bf16[4,64,128]{2,1,0:T(8,128)(2,1)S(1)} %get-tuple-element.49), channel_id=1, source_target_pairs={{0,2},{1,3},{2,0},{3,1},{4,6},{5,7},{6,4},{7,5},{8,10},{9,11},{10,... | collective-permute-start | bytes 196616 | tf_op jit(solution)/shard_map/ppermute | solution.py:256

commit v7 on v4

--- a/solution.py
+++ b/solution.py
@@ -14,6 +14,7 @@
 BF16 = jnp.bfloat16
 VMEM = pl.BlockSpec(memory_space=pltpu.VMEM)
 SMEM = pl.BlockSpec(memory_space=pltpu.SMEM)
+LONG = pl.CostEstimate(flops=10_000_000_000, bytes_accessed=0, transcendentals=0)
 PARAMS = pltpu.CompilerParams(vmem_limit_bytes=12 * 1024 * 1024)
 
 GROUP = 32
@@ -212,6 +213,7 @@
             in_specs=[SMEM] + [VMEM] * 5,
             out_specs=VMEM,
             input_output_aliases={1: 0} if sweep else {},
+            cost_estimate=LONG,
             compiler_params=PARAMS,
         )(scales, estimate, b, vector, selfs, hops)
         relayed = lax.ppermute(at_relay, both, back)

time: 119 us -> 125 us (1.050)
  starting transfers between devices: 51.1 us -> 66.9 us
  waiting for transfers between devices: 40.8 us -> 31 us
    ppermute x3, waiting for transfers between devices: 25.7 us -> 4.64 us  [shards(): from_z_outer = lax.ppermute(sent[2], 'gz', z_outer)]
    ppermute x3, waiting for transfers between devices: 0.01 us -> 17.8 us  [shards(): t_inner = lax.ppermute(sent[1], both, inner)]
    ppermute x3, waiting for transfers between devices: 10.3 us -> 0.01 us  [shards(): at_relay = lax.ppermute(sent[4], both, out)]
    ppermute x3, starting transfers between devices: 11.9 us -> 20.3 us  [shards(): at_relay = lax.ppermute(sent[4], both, out)]
    ppermute x3, waiting for transfers between devices: 0.01 us -> 5.46 us  [shards(): relayed = lax.ppermute(at_relay, both, back)]
    ppermute x3, starting transfers between devices: 15.4 us -> 9.93 us  [shards(): from_z_inner = lax.ppermute(sent[3], 'gz', z_inner)]
    ppermute x1, starting transfers between devices: 1.92 us -> 6.41 us  [shards(): from_chip = lax.ppermute(away, 'gz', [(i, i ^ 2) for i in range(members)])]
    ppermute x3, starting transfers between devices: 8.34 us -> 12.5 us  [shards(): from_z_outer = lax.ppermute(sent[2], 'gz', z_outer)]
  transfers between devices with their start and end apart: 20 -> 20, of which waited for: 8 -> 10; matrix products, arithmetic and copies ran while one was open for 0% -> 0% of each run, Pallas kernels for 10% -> 9%
where the time goes in v7:
time: 125 us; the launch traced here: 124 us
  starting transfers between devices  66.9 us (54%)
  waiting for transfers between devices  31 us (25%)
  Pallas kernels  21.5 us (17%)
  local copies, waits for them, and re-layouts  3.07 us (2%)
    ppermute x3, starting transfers between devices, shards(): at_relay = lax.ppermute(sent[4], both, out)  20.3 us
    ppermute x3, waiting for transfers between devices, shards(): t_inner = lax.ppermute(sent[1], both, inner)  17.8 us
    ppermute x3, starting transfers between devices, shards(): from_z_outer = lax.ppermute(sent[2], 'gz', z_outer)  12.5 us
    ppermute x3, starting transfers between devices, shards(): from_z_inner = lax.ppermute(sent[3], 'gz', z_inner)  9.93 us
    pallas_call x3, Pallas kernels, shards(): pl.pallas_call(functools.partial(local_terms, (zs, xs, ys, d)), out_shape...  8.82 us
    ppermute x1, starting transfers between devices, shards(): from_chip = lax.ppermute(away, 'gz', [(i, i ^ 2) for i in range(members)])  6.41 us
    ppermute x1, starting transfers between devices, shards(): from_core = lax.ppermute(away, 'gz', [(i, i ^ 1) for i in range(members)])  6 us
    ppermute x3, starting transfers between devices, shards(): t_inner = lax.ppermute(sent[1], both, inner)  5.76 us
  transfers between devices with their start and end apart: 20, of which 10 were waited for; matrix products, arithmetic and copies ran while one was open for 0% of the time, Pallas kernels for 9%

profile of v7, /device:TPU:1, one launch (start us, length us, event | category | flops | bytes accessed | tf_op | source)
XLA Modules:
  0.0 124.3 jit_solution(5378101166087001239)
XLA Ops:
  0.7 0.0 copy-start.6
  0.7 0.7 copy-done.6
  1.3 0.1 reshape.37.scales
  1.5 0.1 pad_add_fusion.role
  1.5 0.0 copy-start
  1.5 1.2 copy-done
  2.8 1.0 copy-done.2
  3.8 1.9 %shard_map.78 = (bf16[32,64,128]{2,1,0:T(8,128)(2,1)S(1)}, bf16[32,64,128]{2,1,0:T(8,128)(2,1)S(1)}, bf16[16,64,128]{2,1,0:T(8,128)(2,1)S(1)}, bf16[16,64,128]{2,1,0:T(8,128)(2,1)S(1)}, bf16[32,64,128]{2,1,0:T(8,128)(2,1)S(1)}) custom-call(s32[4]{0:T(128)S(1)} %pad_add_fusion.role, f32[160]{0:T(256)S(1)} %reshape.37.scales, ...), custom_call_target="tpu_custom_call" | custom-call | tf_op jit(solution)/shard_map/pallas_call | solution.py:196
  5.7 5.2 %collective-permute-start.4 = (bf16[32,64,128]{2,1,0:T(8,128)(2,1)S(1)}, bf16[32,64,128]{2,1,0:T(8,128)(2,1)S(1)}, u32[]{:S(2)}, u32[]{:S(2)}) collective-permute-start(bf16[32,64,128]{2,1,0:T(8,128)(2,1)S(1)} %get-tuple-element.30), channel_id=1, source_target_pairs={{1,97},{3,31},{125,29},{127,99},{129,225},{131,159},{253,157},{255... | collective-permute-start | bytes 1572872 | tf_op jit(solution)/shard_map/ppermute | solution.py:205
  10.9 4.2 %collective-permute-start = (bf16[16,64,128]{2,1,0:T(8,128)(2,1)S(1)}, bf16[16,64,128]{2,1,0:T(8,128)(2,1)S(1)}, u32[]{:S(2)}, u32[]{:S(2)}) collective-permute-start(bf16[16,64,128]{2,1,0:T(8,128)(2,1)S(1)} %get-tuple-element.26), channel_id=1, source_target_pairs={{0,1},{1,0},{2,3},{3,2},{4,5},{5,4},{6,7},{7,6},{8,9},{9,8},{10,11... | collective-permute-start | bytes 786440 | tf_op jit(solution)/shard_map/ppermute | solution.py:209
  15.2 7.6 %collective-permute-start.1 = (bf16[16,64,128]{2,1,0:T(8,128)(2,1)S(1)}, bf16[16,64,128]{2,1,0:T(8,128)(2,1)S(1)}, u32[]{:S(2)}, u32[]{:S(2)}) collective-permute-start(bf16[16,64,128]{2,1,0:T(8,128)(2,1)S(1)} %get-tuple-element.27), channel_id=1, source_target_pairs={{0,3},{1,2},{2,1},{3,0},{4,7},{5,6},{6,5},{7,4},{8,11},{9,10},{10,... | collective-permute-start | bytes 786440 | tf_op jit(solution)/shard_map/ppermute | solution.py:208
  22.7 1.9 %collective-permute-start.2 = (bf16[32,64,128]{2,1,0:T(8,128)(2,1)S(1)}, bf16[32,64,128]{2,1,0:T(8,128)(2,1)S(1)}, u32[]{:S(2)}, u32[]{:S(2)}) collective-permute-start(bf16[32,64,128]{2,1,0:T(8,128)(2,1)S(1)} %get-tuple-element.28), channel_id=1, source_target_pairs={{0,4},{1,5},{2,6},{3,7},{4,0},{5,1},{6,2},{7,3},{8,12},{9,13},{10,... | collective-permute-start | bytes 1572872 | tf_op jit(solution)/shard_map/ppermute | solution.py:207
  24.7 0.7 collective-permute-start.3
  25.4 0.0 collective-permute-done.4
  25.4 1.3 %collective-permute-start.5 = (bf16[32,64,128]{2,1,0:T(8,128)(2,1)S(1)}, bf16[32,64,128]{2,1,0:T(8,128)(2,1)S(1)}, u32[]{:S(2)}, u32[]{:S(2)}) collective-permute-start(bf16[32,64,128]{2,1,0:T(8,128)(2,1)S(1)} %collective-permute-done.4), channel_id=1, source_target_pairs={{97,509},{31,511},{29,129},{99,131},{225,125},{159,127},{157,257},... | collective-permute-start | bytes 1572872 | tf_op jit(solution)/shard_map/ppermute | solution.py:219
  26.7 0.0 copy-done.1
  26.7 0.0 copy-done.5
  26.7 3.0 %shard_map.77.partial = f32[32,64,128]{2,1,0:T(8,128)S(1)} custom-call(f32[160]{0:T(256)S(1)} %reshape.37.scales, bf16[32,64,128]{2,1,0:T(8,128)(2,1)S(1)} %bitcast.22, bf16[32,64,128]{2,1,0:T(8,128)(2,1)S(1)} %bitcast.23, bf16[32,64,128]{2,1,0:T(8,128)(2,1)S(1)} %bitcast.24, bf16[32,64,64]{2,1,0:T(8,128)(2,1)S(1)} %bitcast.28, bf16[32,64,256]{2,1,0:T(8,128)(2,1)S(1)} %bitcast.12), custom_call_target="tpu_custom_call" | custom-call | flops 10000000000 | tf_op jit(solution)/shard_map/pallas_call | solution.py:210
  29.6 0.0 collective-permute-done.z_inner
  29.7 0.0 collective-permute-done.1.z_outer
  29.7 0.9 shard_map.79.partial
  30.5 7.6 %collective-permute-done.2.inner = bf16[32,64,128]{2,1,0:T(8,128)(2,1)S(1)} collective-permute-done((bf16[32,64,128]{2,1,0:T(8,128)(2,1)S(1)}, bf16[32,64,128]{2,1,0:T(8,128)(2,1)S(1)}, u32[]{:S(2)}, u32[]{:S(2)}) %collective-permute-start.2) | collective-permute-done | bytes 524320 | tf_op jit(solution)/shard_map/ppermute | solution.py:207
  38.2 0.0 collective-permute-done.3.outer
  38.2 1.6 %collective-permute-done.5.relayed = bf16[32,64,128]{2,1,0:T(8,128)(2,1)S(1)} collective-permute-done((bf16[32,64,128]{2,1,0:T(8,128)(2,1)S(1)}, bf16[32,64,128]{2,1,0:T(8,128)(2,1)S(1)}, u32[]{:S(2)}, u32[]{:S(2)}) %collective-permute-start.5) | collective-permute-done | bytes 524320 | tf_op jit(solution)/shard_map/ppermute | solution.py:219
  39.8 2.7 %shard_map.80 = (f32[32,64,128]{2,1,0:T(8,128)S(1)}, bf16[32,64,128]{2,1,0:T(8,128)(2,1)S(1)}, bf16[32,64,128]{2,1,0:T(8,128)(2,1)S(1)}, bf16[32,64,128]{2,1,0:T...) custom-call(s32[4]{0:T(128)S(1)} %pad_add_fusion.role, ...), custom_call_target="tpu_custom_call", output_to_operand_aliasing={{0}: (2, {})} | custom-call | tf_op jit(solution)/shard_map/pallas_call | solution.py:230
  42.5 6.7 %collective-permute-start.10 = (bf16[32,64,128]{2,1,0:T(8,128)(2,1)S(1)}, bf16[32,64,128]{2,1,0:T(8,128)(2,1)S(1)}, u32[]{:S(2)}, u32[]{:S(2)}) collective-permute-start(bf16[32,64,128]{2,1,0:T(8,128)(2,1)S(1)} %get-tuple-element.37), channel_id=1, source_target_pairs={{1,97},{3,31},{125,29},{127,99},{129,225},{131,159},{253,157},{255... | collective-permute-start | bytes 1572872 | tf_op jit(solution)/shard_map/ppermute | solution.py:205
  49.1 3.8 %collective-permute-start.6 = (bf16[16,64,128]{2,1,0:T(8,128)(2,1)S(1)}, bf16[16,64,128]{2,1,0:T(8,128)(2,1)S(1)}, u32[]{:S(2)}, u32[]{:S(2)}) collective-permute-start(bf16[16,64,128]{2,1,0:T(8,128)(2,1)S(1)} %get-tuple-element.33), channel_id=1, source_target_pairs={{0,1},{1,0},{2,3},{3,2},{4,5},{5,4},{6,7},{7,6},{8,9},{9,8},{10,11... | collective-permute-start | bytes 786440 | tf_op jit(solution)/shard_map/ppermute | solution.py:209
  52.9 1.9 %collective-permute-start.7 = (bf16[16,64,128]{2,1,0:T(8,128)(2,1)S(1)}, bf16[16,64,128]{2,1,0:T(8,128)(2,1)S(1)}, u32[]{:S(2)}, u32[]{:S(2)}) collective-permute-start(bf16[16,64,128]{2,1,0:T(8,128)(2,1)S(1)} %get-tuple-element.34), channel_id=1, source_target_pairs={{0,3},{1,2},{2,1},{3,0},{4,7},{5,6},{6,5},{7,4},{8,11},{9,10},{10,... | collective-permute-start | bytes 786440 | tf_op jit(solution)/shard_map/ppermute | solution.py:208
  54.9 1.9 %collective-permute-start.8 = (bf16[32,64,128]{2,1,0:T(8,128)(2,1)S(1)}, bf16[32,64,128]{2,1,0:T(8,128)(2,1)S(1)}, u32[]{:S(2)}, u32[]{:S(2)}) collective-permute-start(bf16[32,64,128]{2,1,0:T(8,128)(2,1)S(1)} %get-tuple-element.35), channel_id=1, source_target_pairs={{0,4},{1,5},{2,6},{3,7},{4,0},{5,1},{6,2},{7,3},{8,12},{9,13},{10,... | collective-permute-start | bytes 1572872 | tf_op jit(solution)/shard_map/ppermute | solution.py:207
  56.8 0.7 collective-permute-start.9
  57.5 0.0 collective-permute-done.10
  57.5 1.3 %collective-permute-start.11 = (bf16[32,64,128]{2,1,0:T(8,128)(2,1)S(1)}, bf16[32,64,128]{2,1,0:T(8,128)(2,1)S(1)}, u32[]{:S(2)}, u32[]{:S(2)}) collective-permute-start(bf16[32,64,128]{2,1,0:T(8,128)(2,1)S(1)} %collective-permute-done.10), channel_id=1, source_target_pairs={{97,509},{31,511},{29,129},{99,131},{225,125},{159,127},{157,257},... | collective-permute-start | bytes 1572872 | tf_op jit(solution)/shard_map/ppermute | solution.py:219
  58.8 2.9 %shard_map.81.partial = f32[32,64,128]{2,1,0:T(8,128)S(1)} custom-call(f32[160]{0:T(256)S(1)} %reshape.37.scales, f32[32,64,128]{2,1,0:T(8,128)S(1)} %get-tuple-element.31.estimate, bf16[32,64,128]{2,1,0:T(8,128)(2,1)S(1)} %bitcast.25, bf16[32,64,128]{2,1,0:T(8,128)(2,1)S(1)} %get-tuple-element.32.vector, ...), custom_call_target="tpu_custom_call", output_to_operand_aliasing={{}: (1, {})} | custom-call | flops 10000000000 | tf_op jit(solution)/shard_map/pallas_call | solution.py:210
  61.7 0.0 collective-permute-done.6.z_inner
  61.8 1.3 %collective-permute-done.7.z_outer = bf16[16,64,128]{2,1,0:T(8,128)(2,1)S(1)} collective-permute-done((bf16[16,64,128]{2,1,0:T(8,128)(2,1)S(1)}, bf16[16,64,128]{2,1,0:T(8,128)(2,1)S(1)}, u32[]{:S(2)}, u32[]{:S(2)}) %collective-permute-start.7) | collective-permute-done | bytes 262176 | tf_op jit(solution)/shard_map/ppermute | solution.py:208
  63.1 0.9 shard_map.82.partial
  63.9 6.4 %collective-permute-done.8.inner = bf16[32,64,128]{2,1,0:T(8,128)(2,1)S(1)} collective-permute-done((bf16[32,64,128]{2,1,0:T(8,128)(2,1)S(1)}, bf16[32,64,128]{2,1,0:T(8,128)(2,1)S(1)}, u32[]{:S(2)}, u32[]{:S(2)}) %collective-permute-start.8) | collective-permute-done | bytes 524320 | tf_op jit(solution)/shard_map/ppermute | solution.py:207
  70.3 0.0 collective-permute-done.9.outer
  70.3 1.6 %collective-permute-done.11.relayed = bf16[32,64,128]{2,1,0:T(8,128)(2,1)S(1)} collective-permute-done((bf16[32,64,128]{2,1,0:T(8,128)(2,1)S(1)}, bf16[32,64,128]{2,1,0:T(8,128)(2,1)S(1)}, u32[]{:S(2)}, u32[]{:S(2)}) %collective-permute-start.11) | collective-permute-done | bytes 524320 | tf_op jit(solution)/shard_map/ppermute | solution.py:219
  71.9 2.8 %shard_map.83 = (f32[32,64,128]{2,1,0:T(8,128)S(1)}, bf16[32,64,128]{2,1,0:T(8,128)(2,1)S(1)}, bf16[32,64,128]{2,1,0:T(8,128)(2,1)S(1)}, bf16[32,64,128]{2,1,0:T...) custom-call(s32[4]{0:T(128)S(1)} %pad_add_fusion.role, ...), custom_call_target="tpu_custom_call", output_to_operand_aliasing={{0}: (2, {})} | custom-call | tf_op jit(solution)/shard_map/pallas_call | solution.py:230
  74.8 8.5 %collective-permute-start.16 = (bf16[32,64,128]{2,1,0:T(8,128)(2,1)S(1)}, bf16[32,64,128]{2,1,0:T(8,128)(2,1)S(1)}, u32[]{:S(2)}, u32[]{:S(2)}) collective-permute-start(bf16[32,64,128]{2,1,0:T(8,128)(2,1)S(1)} %get-tuple-element.44), channel_id=1, source_target_pairs={{1,97},{3,31},{125,29},{127,99},{129,225},{131,159},{253,157},{255... | collective-permute-start | bytes 1572872 | tf_op jit(solution)/shard_map/ppermute | solution.py:205
  83.3 1.9 %collective-permute-start.12 = (bf16[16,64,128]{2,1,0:T(8,128)(2,1)S(1)}, bf16[16,64,128]{2,1,0:T(8,128)(2,1)S(1)}, u32[]{:S(2)}, u32[]{:S(2)}) collective-permute-start(bf16[16,64,128]{2,1,0:T(8,128)(2,1)S(1)} %get-tuple-element.40), channel_id=1, source_target_pairs={{0,1},{1,0},{2,3},{3,2},{4,5},{5,4},{6,7},{7,6},{8,9},{9,8},{10,11... | collective-permute-start | bytes 786440 | tf_op jit(solution)/shard_map/ppermute | solution.py:209
  85.2 3.0 %collective-permute-start.13 = (bf16[16,64,128]{2,1,0:T(8,128)(2,1)S(1)}, bf16[16,64,128]{2,1,0:T(8,128)(2,1)S(1)}, u32[]{:S(2)}, u32[]{:S(2)}) collective-permute-start(bf16[16,64,128]{2,1,0:T(8,128)(2,1)S(1)} %get-tuple-element.41), channel_id=1, source_target_pairs={{0,3},{1,2},{2,1},{3,0},{4,7},{5,6},{6,5},{7,4},{8,11},{9,10},{10,... | collective-permute-start | bytes 786440 | tf_op jit(solution)/shard_map/ppermute | solution.py:208
  88.3 1.9 %collective-permute-start.14 = (bf16[32,64,128]{2,1,0:T(8,128)(2,1)S(1)}, bf16[32,64,128]{2,1,0:T(8,128)(2,1)S(1)}, u32[]{:S(2)}, u32[]{:S(2)}) collective-permute-start(bf16[32,64,128]{2,1,0:T(8,128)(2,1)S(1)} %get-tuple-element.42), channel_id=1, source_target_pairs={{0,4},{1,5},{2,6},{3,7},{4,0},{5,1},{6,2},{7,3},{8,12},{9,13},{10,... | collective-permute-start | bytes 1572872 | tf_op jit(solution)/shard_map/ppermute | solution.py:207
  90.2 0.7 collective-permute-start.15
  90.9 0.0 collective-permute-done.16
  90.9 1.3 %collective-permute-start.17 = (bf16[32,64,128]{2,1,0:T(8,128)(2,1)S(1)}, bf16[32,64,128]{2,1,0:T(8,128)(2,1)S(1)}, u32[]{:S(2)}, u32[]{:S(2)}) collective-permute-start(bf16[32,64,128]{2,1,0:T(8,128)(2,1)S(1)} %collective-permute-done.16), channel_id=1, source_target_pairs={{97,509},{31,511},{29,129},{99,131},{225,125},{159,127},{157,257},... | collective-permute-start | bytes 1572872 | tf_op jit(solution)/shard_map/ppermute | solution.py:219
  92.2 2.9 %shard_map.84.partial = f32[32,64,128]{2,1,0:T(8,128)S(1)} custom-call(f32[160]{0:T(256)S(1)} %reshape.37.scales, f32[32,64,128]{2,1,0:T(8,128)S(1)} %get-tuple-element.38.estimate, bf16[32,64,128]{2,1,0:T(8,128)(2,1)S(1)} %bitcast.26, bf16[32,64,128]{2,1,0:T(8,128)(2,1)S(1)} %get-tuple-element.39.vector, ...), custom_call_target="tpu_custom_call", output_to_operand_aliasing={{}: (1, {})} | custom-call | flops 10000000000 | tf_op jit(solution)/shard_map/pallas_call | solution.py:210
  95.1 0.0 copy-start.3
  95.1 0.0 collective-permute-done.12.z_inner
  95.2 3.3 %collective-permute-done.13.z_outer = bf16[16,64,128]{2,1,0:T(8,128)(2,1)S(1)} collective-permute-done((bf16[16,64,128]{2,1,0:T(8,128)(2,1)S(1)}, bf16[16,64,128]{2,1,0:T(8,128)(2,1)S(1)}, u32[]{:S(2)}, u32[]{:S(2)}) %collective-permute-start.13) | collective-permute-done | bytes 262176 | tf_op jit(solution)/shard_map/ppermute | solution.py:208
  98.5 0.9 shard_map.85.partial
  99.4 3.8 %collective-permute-done.14.inner = bf16[32,64,128]{2,1,0:T(8,128)(2,1)S(1)} collective-permute-done((bf16[32,64,128]{2,1,0:T(8,128)(2,1)S(1)}, bf16[32,64,128]{2,1,0:T(8,128)(2,1)S(1)}, u32[]{:S(2)}, u32[]{:S(2)}) %collective-permute-start.14) | collective-permute-done | bytes 524320 | tf_op jit(solution)/shard_map/ppermute | solution.py:207
  103.1 0.0 collective-permute-done.15.outer
  103.1 2.2 %collective-permute-done.17.relayed = bf16[32,64,128]{2,1,0:T(8,128)(2,1)S(1)} collective-permute-done((bf16[32,64,128]{2,1,0:T(8,128)(2,1)S(1)}, bf16[32,64,128]{2,1,0:T(8,128)(2,1)S(1)}, u32[]{:S(2)}, u32[]{:S(2)}) %collective-permute-start.17) | collective-permute-done | bytes 524320 | tf_op jit(solution)/shard_map/ppermute | solution.py:219
  105.3 0.0 copy-done.3
  105.3 0.0 copy-done.4
  105.3 2.1 %shard_map.86 = (bf16[32,64,128]{2,1,0:T(8,128)(2,1)}, f32[8,64,128]{2,1,0:T(8,128)S(1)}, bf16[8,64,128]{2,1,0:T(8,128)(2,1)S(1)}) custom-call(s32[4]{0:T(128)S(1)} %pad_add_fusion.role, f32[160]{0:T(256)S(1)} %reshape.37.scales, s32[1,2,4,4]{3,2,1,0:T(4,128)S(1)} %copy-done.4, f32[32,64,128]{2,1,0:T(8,128)S(1)} %shard_map.85.partial, ...), custom_call_target="tpu_custom_call" | custom-call | tf_op jit(solution)/shard_map/pallas_call | solution.py:242
  107.5 6.0 %collective-permute-start.18 = (bf16[8,64,128]{2,1,0:T(8,128)(2,1)S(1)}, bf16[8,64,128]{2,1,0:T(8,128)(2,1)S(1)}, u32[]{:S(2)}, u32[]{:S(2)}) collective-permute-start(bf16[8,64,128]{2,1,0:T(8,128)(2,1)S(1)} %get-tuple-element.47), channel_id=1, source_target_pairs={{0,1},{1,0},{2,3},{3,2},{4,5},{5,4},{6,7},{7,6},{8,9},{9,8},{10,11... | collective-permute-start | bytes 393224 | tf_op jit(solution)/shard_map/ppermute | solution.py:250
  113.5 1.0 collective-permute-done.18.came
  114.5 0.6 shard_map.87
  115.0 6.4 %collective-permute-start.19 = (bf16[4,64,128]{2,1,0:T(8,128)(2,1)S(1)}, bf16[4,64,128]{2,1,0:T(8,128)(2,1)S(1)}, u32[]{:S(2)}, u32[]{:S(2)}) collective-permute-start(bf16[4,64,128]{2,1,0:T(8,128)(2,1)S(1)} %get-tuple-element.49), channel_id=1, source_target_pairs={{0,2},{1,3},{2,0},{3,1},{4,6},{5,7},{6,4},{7,5},{8,10},{9,11},{10,... | collective-permute-start | bytes 196616 | tf_op jit(solution)/shard_map/ppermute | solution.py:258
  121.5 2.2 %collective-permute-done.19 = bf16[4,64,128]{2,1,0:T(8,128)(2,1)S(1)} collective-permute-done((bf16[4,64,128]{2,1,0:T(8,128)(2,1)S(1)}, bf16[4,64,128]{2,1,0:T(8,128)(2,1)S(1)}, u32[]{:S(2)}, u32[]{:S(2)}) %collective-permute-start.19) | collective-permute-done | bytes 65568 | tf_op jit(solution)/shard_map/ppermute | solution.py:258
  123.6 0.7 add_bitcast_fusion
  (4 shorter events, 0.0 us)
Async XLA Ops:
  0.7 0.7 copy-start.6
  1.5 1.2 copy-start
  2.8 1.0 copy-start.2
  3.8 22.9 %copy-start.1 = (bf16[1,2,4,4,64,256]{5,4,3,2,1,0:T(8,128)(2,1)S(1)}, bf16[1,2,4,4,64,256]{5,4,3,2,1,0:T(8,128)(2,1)}, u32[]{:S(2)}) copy-start(bf16[1,2,4,4,64,256]{5,4,3,2,1,0:T(8,128)(2,1)} %param.8) | copy-start | bytes 3145732
  3.8 22.9 %copy-start.5 = (bf16[1,2,4,4,64,64]{5,4,3,2,1,0:T(8,128)(2,1)S(1)}, bf16[1,2,4,4,64,64]{5,4,3,2,1,0:T(8,128)(2,1)}, u32[]{:S(2)}) copy-start(bf16[1,2,4,4,64,64]{5,4,3,2,1,0:T(8,128)(2,1)} %param.7) | copy-start | bytes 786436
  5.7 19.7 %collective-permute-start.4 = (bf16[32,64,128]{2,1,0:T(8,128)(2,1)S(1)}, bf16[32,64,128]{2,1,0:T(8,128)(2,1)S(1)}, u32[]{:S(2)}, u32[]{:S(2)}) collective-permute-start(bf16[32,64,128]{2,1,0:T(8,128)(2,1)S(1)} %get-tuple-element.30), channel_id=1, source_target_pairs={{1,97},{3,31},{125,29},{127,99},{129,225},{131,159},{253,157},{255... | collective-permute-start | bytes 1572872 | tf_op jit(solution)/shard_map/ppermute | solution.py:205
  10.9 18.7 %collective-permute-start = (bf16[16,64,128]{2,1,0:T(8,128)(2,1)S(1)}, bf16[16,64,128]{2,1,0:T(8,128)(2,1)S(1)}, u32[]{:S(2)}, u32[]{:S(2)}) collective-permute-start(bf16[16,64,128]{2,1,0:T(8,128)(2,1)S(1)} %get-tuple-element.26), channel_id=1, source_target_pairs={{0,1},{1,0},{2,3},{3,2},{4,5},{5,4},{6,7},{7,6},{8,9},{9,8},{10,11... | collective-permute-start | bytes 786440 | tf_op jit(solution)/shard_map/ppermute | solution.py:209
  15.2 14.5 %collective-permute-start.1 = (bf16[16,64,128]{2,1,0:T(8,128)(2,1)S(1)}, bf16[16,64,128]{2,1,0:T(8,128)(2,1)S(1)}, u32[]{:S(2)}, u32[]{:S(2)}) collective-permute-start(bf16[16,64,128]{2,1,0:T(8,128)(2,1)S(1)} %get-tuple-element.27), channel_id=1, source_target_pairs={{0,3},{1,2},{2,1},{3,0},{4,7},{5,6},{6,5},{7,4},{8,11},{9,10},{10,... | collective-permute-start | bytes 786440 | tf_op jit(solution)/shard_map/ppermute | solution.py:208
  22.7 15.4 %collective-permute-start.2 = (bf16[32,64,128]{2,1,0:T(8,128)(2,1)S(1)}, bf16[32,64,128]{2,1,0:T(8,128)(2,1)S(1)}, u32[]{:S(2)}, u32[]{:S(2)}) collective-permute-start(bf16[32,64,128]{2,1,0:T(8,128)(2,1)S(1)} %get-tuple-element.28), channel_id=1, source_target_pairs={{0,4},{1,5},{2,6},{3,7},{4,0},{5,1},{6,2},{7,3},{8,12},{9,13},{10,... | collective-permute-start | bytes 1572872 | tf_op jit(solution)/shard_map/ppermute | solution.py:207
  24.7 13.5 %collective-permute-start.3 = (bf16[32,64,128]{2,1,0:T(8,128)(2,1)S(1)}, bf16[32,64,128]{2,1,0:T(8,128)(2,1)S(1)}, u32[]{:S(2)}, u32[]{:S(2)}) collective-permute-start(bf16[32,64,128]{2,1,0:T(8,128)(2,1)S(1)} %get-tuple-element.29), channel_id=1, source_target_pairs={{0,508},{2,510},{4,8},{5,9},{6,10},{7,11},{8,4},{9,5},{10,6},{11,7... | collective-permute-start | bytes 1572872 | tf_op jit(solution)/shard_map/ppermute | solution.py:206
  25.4 14.4 %collective-permute-start.5 = (bf16[32,64,128]{2,1,0:T(8,128)(2,1)S(1)}, bf16[32,64,128]{2,1,0:T(8,128)(2,1)S(1)}, u32[]{:S(2)}, u32[]{:S(2)}) collective-permute-start(bf16[32,64,128]{2,1,0:T(8,128)(2,1)S(1)} %collective-permute-done.4), channel_id=1, source_target_pairs={{97,509},{31,511},{29,129},{99,131},{225,125},{159,127},{157,257},... | collective-permute-start | bytes 1572872 | tf_op jit(solution)/shard_map/ppermute | solution.py:219
  42.5 15.0 %collective-permute-start.10 = (bf16[32,64,128]{2,1,0:T(8,128)(2,1)S(1)}, bf16[32,64,128]{2,1,0:T(8,128)(2,1)S(1)}, u32[]{:S(2)}, u32[]{:S(2)}) collective-permute-start(bf16[32,64,128]{2,1,0:T(8,128)(2,1)S(1)} %get-tuple-element.37), channel_id=1, source_target_pairs={{1,97},{3,31},{125,29},{127,99},{129,225},{131,159},{253,157},{255... | collective-permute-start | bytes 1572872 | tf_op jit(solution)/shard_map/ppermute | solution.py:205
  49.1 12.6 %collective-permute-start.6 = (bf16[16,64,128]{2,1,0:T(8,128)(2,1)S(1)}, bf16[16,64,128]{2,1,0:T(8,128)(2,1)S(1)}, u32[]{:S(2)}, u32[]{:S(2)}) collective-permute-start(bf16[16,64,128]{2,1,0:T(8,128)(2,1)S(1)} %get-tuple-element.33), channel_id=1, source_target_pairs={{0,1},{1,0},{2,3},{3,2},{4,5},{5,4},{6,7},{7,6},{8,9},{9,8},{10,11... | collective-permute-start | bytes 786440 | tf_op jit(solution)/shard_map/ppermute | solution.py:209
  52.9 10.1 %collective-permute-start.7 = (bf16[16,64,128]{2,1,0:T(8,128)(2,1)S(1)}, bf16[16,64,128]{2,1,0:T(8,128)(2,1)S(1)}, u32[]{:S(2)}, u32[]{:S(2)}) collective-permute-start(bf16[16,64,128]{2,1,0:T(8,128)(2,1)S(1)} %get-tuple-element.34), channel_id=1, source_target_pairs={{0,3},{1,2},{2,1},{3,0},{4,7},{5,6},{6,5},{7,4},{8,11},{9,10},{10,... | collective-permute-start | bytes 786440 | tf_op jit(solution)/shard_map/ppermute | solution.py:208
  54.9 15.4 %collective-permute-start.8 = (bf16[32,64,128]{2,1,0:T(8,128)(2,1)S(1)}, bf16[32,64,128]{2,1,0:T(8,128)(2,1)S(1)}, u32[]{:S(2)}, u32[]{:S(2)}) collective-permute-start(bf16[32,64,128]{2,1,0:T(8,128)(2,1)S(1)} %get-tuple-element.35), channel_id=1, source_target_pairs={{0,4},{1,5},{2,6},{3,7},{4,0},{5,1},{6,2},{7,3},{8,12},{9,13},{10,... | collective-permute-start | bytes 1572872 | tf_op jit(solution)/shard_map/ppermute | solution.py:207
  56.8 13.5 %collective-permute-start.9 = (bf16[32,64,128]{2,1,0:T(8,128)(2,1)S(1)}, bf16[32,64,128]{2,1,0:T(8,128)(2,1)S(1)}, u32[]{:S(2)}, u32[]{:S(2)}) collective-permute-start(bf16[32,64,128]{2,1,0:T(8,128)(2,1)S(1)} %get-tuple-element.36), channel_id=1, source_target_pairs={{0,508},{2,510},{4,8},{5,9},{6,10},{7,11},{8,4},{9,5},{10,6},{11,7... | collective-permute-start | bytes 1572872 | tf_op jit(solution)/shard_map/ppermute | solution.py:206
  57.5 14.4 %collective-permute-start.11 = (bf16[32,64,128]{2,1,0:T(8,128)(2,1)S(1)}, bf16[32,64,128]{2,1,0:T(8,128)(2,1)S(1)}, u32[]{:S(2)}, u32[]{:S(2)}) collective-permute-start(bf16[32,64,128]{2,1,0:T(8,128)(2,1)S(1)} %collective-permute-done.10), channel_id=1, source_target_pairs={{97,509},{31,511},{29,129},{99,131},{225,125},{159,127},{157,257},... | collective-permute-start | bytes 1572872 | tf_op jit(solution)/shard_map/ppermute | solution.py:219
  74.8 16.1 %collective-permute-start.16 = (bf16[32,64,128]{2,1,0:T(8,128)(2,1)S(1)}, bf16[32,64,128]{2,1,0:T(8,128)(2,1)S(1)}, u32[]{:S(2)}, u32[]{:S(2)}) collective-permute-start(bf16[32,64,128]{2,1,0:T(8,128)(2,1)S(1)} %get-tuple-element.44), channel_id=1, source_target_pairs={{1,97},{3,31},{125,29},{127,99},{129,225},{131,159},{253,157},{255... | collective-permute-start | bytes 1572872 | tf_op jit(solution)/shard_map/ppermute | solution.py:205
  83.3 11.9 %collective-permute-start.12 = (bf16[16,64,128]{2,1,0:T(8,128)(2,1)S(1)}, bf16[16,64,128]{2,1,0:T(8,128)(2,1)S(1)}, u32[]{:S(2)}, u32[]{:S(2)}) collective-permute-start(bf16[16,64,128]{2,1,0:T(8,128)(2,1)S(1)} %get-tuple-element.40), channel_id=1, source_target_pairs={{0,1},{1,0},{2,3},{3,2},{4,5},{5,4},{6,7},{7,6},{8,9},{9,8},{10,11... | collective-permute-start | bytes 786440 | tf_op jit(solution)/shard_map/ppermute | solution.py:209
  85.2 13.3 %collective-permute-start.13 = (bf16[16,64,128]{2,1,0:T(8,128)(2,1)S(1)}, bf16[16,64,128]{2,1,0:T(8,128)(2,1)S(1)}, u32[]{:S(2)}, u32[]{:S(2)}) collective-permute-start(bf16[16,64,128]{2,1,0:T(8,128)(2,1)S(1)} %get-tuple-element.41), channel_id=1, source_target_pairs={{0,3},{1,2},{2,1},{3,0},{4,7},{5,6},{6,5},{7,4},{8,11},{9,10},{10,... | collective-permute-start | bytes 786440 | tf_op jit(solution)/shard_map/ppermute | solution.py:208
  88.3 14.9 %collective-permute-start.14 = (bf16[32,64,128]{2,1,0:T(8,128)(2,1)S(1)}, bf16[32,64,128]{2,1,0:T(8,128)(2,1)S(1)}, u32[]{:S(2)}, u32[]{:S(2)}) collective-permute-start(bf16[32,64,128]{2,1,0:T(8,128)(2,1)S(1)} %get-tuple-element.42), channel_id=1, source_target_pairs={{0,4},{1,5},{2,6},{3,7},{4,0},{5,1},{6,2},{7,3},{8,12},{9,13},{10,... | collective-permute-start | bytes 1572872 | tf_op jit(solution)/shard_map/ppermute | solution.py:207
  90.2 13.0 %collective-permute-start.15 = (bf16[32,64,128]{2,1,0:T(8,128)(2,1)S(1)}, bf16[32,64,128]{2,1,0:T(8,128)(2,1)S(1)}, u32[]{:S(2)}, u32[]{:S(2)}) collective-permute-start(bf16[32,64,128]{2,1,0:T(8,128)(2,1)S(1)} %get-tuple-element.43), channel_id=1, source_target_pairs={{0,508},{2,510},{4,8},{5,9},{6,10},{7,11},{8,4},{9,5},{10,6},{11,7... | collective-permute-start | bytes 1572872 | tf_op jit(solution)/shard_map/ppermute | solution.py:206
  90.9 14.4 %collective-permute-start.17 = (bf16[32,64,128]{2,1,0:T(8,128)(2,1)S(1)}, bf16[32,64,128]{2,1,0:T(8,128)(2,1)S(1)}, u32[]{:S(2)}, u32[]{:S(2)}) collective-permute-start(bf16[32,64,128]{2,1,0:T(8,128)(2,1)S(1)} %collective-permute-done.16), channel_id=1, source_target_pairs={{97,509},{31,511},{29,129},{99,131},{225,125},{159,127},{157,257},... | collective-permute-start | bytes 1572872 | tf_op jit(solution)/shard_map/ppermute | solution.py:219
  95.1 10.2 %copy-start.3 = (bf16[1,2,4,4,64,64]{5,4,3,2,1,0:T(8,128)(2,1)S(1)}, bf16[1,2,4,4,64,64]{5,4,3,2,1,0:T(8,128)(2,1)}, u32[]{:S(2)}) copy-start(bf16[1,2,4,4,64,64]{5,4,3,2,1,0:T(8,128)(2,1)} %param.11) | copy-start | bytes 786436
  98.5 6.8 %copy-start.4 = (s32[1,2,4,4]{3,2,1,0:T(4,128)S(1)}, s32[1,2,4,4]{3,2,1,0:T(4,128)}, u32[]{:S(2)}) copy-start(s32[1,2,4,4]{3,2,1,0:T(4,128)} %labels.1) | copy-start | bytes 388
  107.5 7.0 %collective-permute-start.18 = (bf16[8,64,128]{2,1,0:T(8,128)(2,1)S(1)}, bf16[8,64,128]{2,1,0:T(8,128)(2,1)S(1)}, u32[]{:S(2)}, u32[]{:S(2)}) collective-permute-start(bf16[8,64,128]{2,1,0:T(8,128)(2,1)S(1)} %get-tuple-element.47), channel_id=1, source_target_pairs={{0,1},{1,0},{2,3},{3,2},{4,5},{5,4},{6,7},{7,6},{8,9},{9,8},{10,11... | collective-permute-start | bytes 393224 | tf_op jit(solution)/shard_map/ppermute | solution.py:250
  115.0 8.6 %collective-permute-start.19 = (bf16[4,64,128]{2,1,0:T(8,128)(2,1)S(1)}, bf16[4,64,128]{2,1,0:T(8,128)(2,1)S(1)}, u32[]{:S(2)}, u32[]{:S(2)}) collective-permute-start(bf16[4,64,128]{2,1,0:T(8,128)(2,1)S(1)} %get-tuple-element.49), channel_id=1, source_target_pairs={{0,2},{1,3},{2,0},{3,1},{4,6},{5,7},{6,4},{7,5},{8,10},{9,11},{10,... | collective-permute-start | bytes 196616 | tf_op jit(solution)/shard_map/ppermute | solution.py:258

commit v8 on v4

--- a/solution.py
+++ b/solution.py
@@ -52,7 +52,7 @@
         yield pl.when(parity == value), *pair
 
 
-def hop_terms(role, scales, vector, hops, outer, inner, z_outer, z_inner, detour):
+def hop_terms(role, scales, vector, hops, outer, inner, z_outer, z_inner):
     sites, d = vector.shape[:2]
     edge = z_inner.shape[0]
     last = sites - edge
@@ -71,10 +71,6 @@
             for s in range(last, sites):
                 ahead[s - last] = (scales[5 * s + 3] * dot_t(hops[s, :, 2 * d : 3 * d], vector[s])).astype(BF16)
             behind[...] = vector[:edge]
-
-    @pl.when(role[0] != 0)
-    def _():
-        detour[...] = outer[...]
 
 
 def local_terms(shape, scales, estimate, source, vector, selfs, hops, partial):
@@ -191,17 +187,17 @@
     both = ("ta", "gz")
 
     scales = link_scales.astype(F32).reshape(sites * 5)
-    messages = (field, field, slab, slab, field)
+    messages = (field, field, slab, slab)
     sent = pl.pallas_call(
         hop_terms,
         out_shape=messages,
         in_specs=[SMEM] * 2 + [VMEM] * 2,
-        out_specs=(VMEM,) * 5,
+        out_specs=(VMEM,) * 4,
         compiler_params=PARAMS,
     )(role, scales, b, hops)
     vector, estimate = b, b
     for sweep in range(ITERS):
-        at_relay = lax.ppermute(sent[4], both, out)
+        at_relay = lax.ppermute(sent[0], both, out)
         t_outer = lax.ppermute(sent[0], both, outer)
         t_inner = lax.ppermute(sent[1], both, inner)
         from_z_outer = lax.ppermute(sent[2], "gz", z_outer)
@@ -229,7 +225,7 @@
                 sweep_end,
                 out_shape=(wide, field) + messages,
                 in_specs=[SMEM] * 2 + [VMEM] * 5,
-                out_specs=(VMEM,) * 7,
+                out_specs=(VMEM,) * 6,
                 input_output_aliases={2: 0},
                 compiler_params=PARAMS,
             )(role, scales, *came)

time: 119 us -> 128 us (1.076)
  the two profiles are of different devices: /device:TPU:1 before, /device:TPU:14 now
where the time goes in v8:
time: 128 us; the launch traced here: 127 us
  starting transfers between devices  74.8 us (58%)
  waiting for transfers between devices  26.4 us (21%)
  Pallas kernels  21.4 us (17%)
  local copies, waits for them, and re-layouts  3.07 us (2%)
    ppermute x3, starting transfers between devices, shards(): from_z_inner = lax.ppermute(sent[3], 'gz', z_inner)  38.4 us
    ppermute x3, waiting for transfers between devices, shards(): from_z_outer = lax.ppermute(sent[2], 'gz', z_outer)  20.9 us
    ppermute x3, starting transfers between devices, shards(): t_outer = lax.ppermute(sent[0], both, outer)  15.1 us
    pallas_call x3, Pallas kernels, shards(): pl.pallas_call(functools.partial(local_terms, (zs, xs, ys, d)), out_shape...  8.8 us
    ppermute x3, starting transfers between devices, shards(): from_z_outer = lax.ppermute(sent[2], 'gz', z_outer)  7.48 us
    ppermute x3, starting transfers between devices, shards(): t_inner = lax.ppermute(sent[1], both, inner)  5.76 us
    pallas_call x2, Pallas kernels, shards(): pl.pallas_call(sweep_end, out_shape=(wide, field) + messages, in_specs=[S...  5.4 us
    ppermute x1, waiting for transfers between devices, shards(): from_chip = lax.ppermute(away, 'gz', [(i, i ^ 2) for i in range(members)])  4.23 us
  transfers between devices with their start and end apart: 20, of which 5 were waited for; matrix products, arithmetic and copies ran while one was open for 0% of the time, Pallas kernels for 9%

profile of v8, /device:TPU:14, one launch (start us, length us, event | category | flops | bytes accessed | tf_op | source)
XLA Modules:
  0.0 127.4 jit_solution(11097791351713846014)
XLA Ops:
  0.7 0.0 copy-start.6
  0.7 0.7 copy-done.6
  1.3 0.1 reshape.37.scales
  1.5 0.1 pad_add_fusion.role
  1.5 0.0 copy-start
  1.5 1.2 copy-done
  2.8 1.0 copy-done.2
  3.8 1.8 %shard_map.78 = (bf16[32,64,128]{2,1,0:T(8,128)(2,1)S(1)}, bf16[32,64,128]{2,1,0:T(8,128)(2,1)S(1)}, bf16[16,64,128]{2,1,0:T(8,128)(2,1)S(1)}, bf16[16,64,128]{2,1,0:T(8,128)(2,1)S(1)}) custom-call(s32[4]{0:T(128)S(1)} %pad_add_fusion.role, f32[160]{0:T(256)S(1)} %reshape.37.scales, bf16[32,64,128]{2,1,0:T(8,128)(2,1)S(1)} %bitcast.21, ...), custom_call_target="tpu_custom_call" | custom-call | tf_op jit(solution)/shard_map/pallas_call | solution.py:191
  5.7 0.7 collective-permute-start.4
  6.4 11.2 %collective-permute-start.3 = (bf16[32,64,128]{2,1,0:T(8,128)(2,1)S(1)}, bf16[32,64,128]{2,1,0:T(8,128)(2,1)S(1)}, u32[]{:S(2)}, u32[]{:S(2)}) collective-permute-start(bf16[32,64,128]{2,1,0:T(8,128)(2,1)S(1)} %get-tuple-element.26), channel_id=1, source_target_pairs={{0,508},{2,510},{4,8},{5,9},{6,10},{7,11},{8,4},{9,5},{10,6},{11,7... | collective-permute-start | bytes 1572872 | tf_op jit(solution)/shard_map/ppermute | solution.py:201
  17.6 1.9 %collective-permute-start.2 = (bf16[32,64,128]{2,1,0:T(8,128)(2,1)S(1)}, bf16[32,64,128]{2,1,0:T(8,128)(2,1)S(1)}, u32[]{:S(2)}, u32[]{:S(2)}) collective-permute-start(bf16[32,64,128]{2,1,0:T(8,128)(2,1)S(1)} %get-tuple-element.25), channel_id=1, source_target_pairs={{0,4},{1,5},{2,6},{3,7},{4,0},{5,1},{6,2},{7,3},{8,12},{9,13},{10,... | collective-permute-start | bytes 1572872 | tf_op jit(solution)/shard_map/ppermute | solution.py:202
  19.5 0.0 collective-permute-done.4
  19.5 0.7 collective-permute-start.5
  20.2 8.1 %collective-permute-start = (bf16[16,64,128]{2,1,0:T(8,128)(2,1)S(1)}, bf16[16,64,128]{2,1,0:T(8,128)(2,1)S(1)}, u32[]{:S(2)}, u32[]{:S(2)}) collective-permute-start(bf16[16,64,128]{2,1,0:T(8,128)(2,1)S(1)} %get-tuple-element.23), channel_id=1, source_target_pairs={{0,1},{1,0},{2,3},{3,2},{4,5},{5,4},{6,7},{7,6},{8,9},{9,8},{10,11... | collective-permute-start | bytes 786440 | tf_op jit(solution)/shard_map/ppermute | solution.py:204
  28.3 3.6 %collective-permute-start.1 = (bf16[16,64,128]{2,1,0:T(8,128)(2,1)S(1)}, bf16[16,64,128]{2,1,0:T(8,128)(2,1)S(1)}, u32[]{:S(2)}, u32[]{:S(2)}) collective-permute-start(bf16[16,64,128]{2,1,0:T(8,128)(2,1)S(1)} %get-tuple-element.24), channel_id=1, source_target_pairs={{0,3},{1,2},{2,1},{3,0},{4,7},{5,6},{6,5},{7,4},{8,11},{9,10},{10,... | collective-permute-start | bytes 786440 | tf_op jit(solution)/shard_map/ppermute | solution.py:203
  32.0 0.0 copy-done.1
  32.0 0.0 copy-done.3
  32.0 2.9 %shard_map.77.partial = f32[32,64,128]{2,1,0:T(8,128)S(1)} custom-call(f32[160]{0:T(256)S(1)} %reshape.37.scales, bf16[32,64,128]{2,1,0:T(8,128)(2,1)S(1)} %bitcast.22, bf16[32,64,128]{2,1,0:T(8,128)(2,1)S(1)} %bitcast.23, bf16[32,64,128]{2,1,0:T(8,128)(2,1)S(1)} %bitcast.24, bf16[32,64,64]{2,1,0:T(8,128)(2,1)S(1)} %bitcast.27, bf16[32,64,256]{2,1,0:T(8,128)(2,1)S(1)} %bitcast.12), custom_call_target="tpu_custom_call" | custom-call | tf_op jit(solution)/shard_map/pallas_call | solution.py:205
  35.0 0.0 collective-permute-done.z_inner
  35.0 6.0 %collective-permute-done.1.z_outer = bf16[16,64,128]{2,1,0:T(8,128)(2,1)S(1)} collective-permute-done((bf16[16,64,128]{2,1,0:T(8,128)(2,1)S(1)}, bf16[16,64,128]{2,1,0:T(8,128)(2,1)S(1)}, u32[]{:S(2)}, u32[]{:S(2)}) %collective-permute-start.1) | collective-permute-done | bytes 262176 | tf_op jit(solution)/shard_map/ppermute | solution.py:203
  40.9 0.9 shard_map.79.partial
  41.8 0.0 collective-permute-done.2.inner
  41.8 0.0 collective-permute-done.3.outer
  41.8 0.0 collective-permute-done.5.relayed
  41.8 2.6 %shard_map.80 = (f32[32,64,128]{2,1,0:T(8,128)S(1)}, bf16[32,64,128]{2,1,0:T(8,128)(2,1)S(1)}, bf16[32,64,128]{2,1,0:T(8,128)(2,1)S(1)}, bf16[32,64,128]{2,1,0:T...) custom-call(s32[4]{0:T(128)S(1)} %pad_add_fusion.role, ...), custom_call_target="tpu_custom_call", output_to_operand_aliasing={{0}: (2, {})} | custom-call | tf_op jit(solution)/shard_map/pallas_call | solution.py:224
  44.5 0.7 collective-permute-start.10
  45.2 1.9 %collective-permute-start.9 = (bf16[32,64,128]{2,1,0:T(8,128)(2,1)S(1)}, bf16[32,64,128]{2,1,0:T(8,128)(2,1)S(1)}, u32[]{:S(2)}, u32[]{:S(2)}) collective-permute-start(bf16[32,64,128]{2,1,0:T(8,128)(2,1)S(1)} %get-tuple-element.32), channel_id=1, source_target_pairs={{0,508},{2,510},{4,8},{5,9},{6,10},{7,11},{8,4},{9,5},{10,6},{11,7... | collective-permute-start | bytes 1572872 | tf_op jit(solution)/shard_map/ppermute | solution.py:201
  47.1 1.9 %collective-permute-start.8 = (bf16[32,64,128]{2,1,0:T(8,128)(2,1)S(1)}, bf16[32,64,128]{2,1,0:T(8,128)(2,1)S(1)}, u32[]{:S(2)}, u32[]{:S(2)}) collective-permute-start(bf16[32,64,128]{2,1,0:T(8,128)(2,1)S(1)} %get-tuple-element.31), channel_id=1, source_target_pairs={{0,4},{1,5},{2,6},{3,7},{4,0},{5,1},{6,2},{7,3},{8,12},{9,13},{10,... | collective-permute-start | bytes 1572872 | tf_op jit(solution)/shard_map/ppermute | solution.py:202
  49.0 0.0 collective-permute-done.10
  49.0 0.7 collective-permute-start.11
  49.7 15.2 %collective-permute-start.6 = (bf16[16,64,128]{2,1,0:T(8,128)(2,1)S(1)}, bf16[16,64,128]{2,1,0:T(8,128)(2,1)S(1)}, u32[]{:S(2)}, u32[]{:S(2)}) collective-permute-start(bf16[16,64,128]{2,1,0:T(8,128)(2,1)S(1)} %get-tuple-element.29), channel_id=1, source_target_pairs={{0,1},{1,0},{2,3},{3,2},{4,5},{5,4},{6,7},{7,6},{8,9},{9,8},{10,11... | collective-permute-start | bytes 786440 | tf_op jit(solution)/shard_map/ppermute | solution.py:204
  64.9 1.9 %collective-permute-start.7 = (bf16[16,64,128]{2,1,0:T(8,128)(2,1)S(1)}, bf16[16,64,128]{2,1,0:T(8,128)(2,1)S(1)}, u32[]{:S(2)}, u32[]{:S(2)}) collective-permute-start(bf16[16,64,128]{2,1,0:T(8,128)(2,1)S(1)} %get-tuple-element.30), channel_id=1, source_target_pairs={{0,3},{1,2},{2,1},{3,0},{4,7},{5,6},{6,5},{7,4},{8,11},{9,10},{10,... | collective-permute-start | bytes 786440 | tf_op jit(solution)/shard_map/ppermute | solution.py:203
  66.8 2.9 %shard_map.81.partial = f32[32,64,128]{2,1,0:T(8,128)S(1)} custom-call(f32[160]{0:T(256)S(1)} %reshape.37.scales, f32[32,64,128]{2,1,0:T(8,128)S(1)} %get-tuple-element.27.estimate, bf16[32,64,128]{2,1,0:T(8,128)(2,1)S(1)} %bitcast.25, bf16[32,64,128]{2,1,0:T(8,128)(2,1)S(1)} %get-tuple-element.28.vector, ...), custom_call_target="tpu_custom_call", output_to_operand_aliasing={{}: (1, {})} | custom-call | tf_op jit(solution)/shard_map/pallas_call | solution.py:205
  69.8 0.0 collective-permute-done.6.z_inner
  69.8 7.5 %collective-permute-done.7.z_outer = bf16[16,64,128]{2,1,0:T(8,128)(2,1)S(1)} collective-permute-done((bf16[16,64,128]{2,1,0:T(8,128)(2,1)S(1)}, bf16[16,64,128]{2,1,0:T(8,128)(2,1)S(1)}, u32[]{:S(2)}, u32[]{:S(2)}) %collective-permute-start.7) | collective-permute-done | bytes 262176 | tf_op jit(solution)/shard_map/ppermute | solution.py:203
  77.3 0.9 shard_map.82.partial
  78.2 0.0 collective-permute-done.8.inner
  78.2 0.0 collective-permute-done.9.outer
  78.2 0.0 collective-permute-done.11.relayed
  78.2 2.8 %shard_map.83 = (f32[32,64,128]{2,1,0:T(8,128)S(1)}, bf16[32,64,128]{2,1,0:T(8,128)(2,1)S(1)}, bf16[32,64,128]{2,1,0:T(8,128)(2,1)S(1)}, bf16[32,64,128]{2,1,0:T...) custom-call(s32[4]{0:T(128)S(1)} %pad_add_fusion.role, ...), custom_call_target="tpu_custom_call", output_to_operand_aliasing={{0}: (2, {})} | custom-call | tf_op jit(solution)/shard_map/pallas_call | solution.py:224
  81.0 0.7 collective-permute-start.16
  81.7 1.9 %collective-permute-start.15 = (bf16[32,64,128]{2,1,0:T(8,128)(2,1)S(1)}, bf16[32,64,128]{2,1,0:T(8,128)(2,1)S(1)}, u32[]{:S(2)}, u32[]{:S(2)}) collective-permute-start(bf16[32,64,128]{2,1,0:T(8,128)(2,1)S(1)} %get-tuple-element.38), channel_id=1, source_target_pairs={{0,508},{2,510},{4,8},{5,9},{6,10},{7,11},{8,4},{9,5},{10,6},{11,7... | collective-permute-start | bytes 1572872 | tf_op jit(solution)/shard_map/ppermute | solution.py:201
  83.6 1.9 %collective-permute-start.14 = (bf16[32,64,128]{2,1,0:T(8,128)(2,1)S(1)}, bf16[32,64,128]{2,1,0:T(8,128)(2,1)S(1)}, u32[]{:S(2)}, u32[]{:S(2)}) collective-permute-start(bf16[32,64,128]{2,1,0:T(8,128)(2,1)S(1)} %get-tuple-element.37), channel_id=1, source_target_pairs={{0,4},{1,5},{2,6},{3,7},{4,0},{5,1},{6,2},{7,3},{8,12},{9,13},{10,... | collective-permute-start | bytes 1572872 | tf_op jit(solution)/shard_map/ppermute | solution.py:202
  85.6 0.0 collective-permute-done.16
  85.6 0.7 collective-permute-start.17
  86.3 15.1 %collective-permute-start.12 = (bf16[16,64,128]{2,1,0:T(8,128)(2,1)S(1)}, bf16[16,64,128]{2,1,0:T(8,128)(2,1)S(1)}, u32[]{:S(2)}, u32[]{:S(2)}) collective-permute-start(bf16[16,64,128]{2,1,0:T(8,128)(2,1)S(1)} %get-tuple-element.35), channel_id=1, source_target_pairs={{0,1},{1,0},{2,3},{3,2},{4,5},{5,4},{6,7},{7,6},{8,9},{9,8},{10,11... | collective-permute-start | bytes 786440 | tf_op jit(solution)/shard_map/ppermute | solution.py:204
  101.4 1.9 %collective-permute-start.13 = (bf16[16,64,128]{2,1,0:T(8,128)(2,1)S(1)}, bf16[16,64,128]{2,1,0:T(8,128)(2,1)S(1)}, u32[]{:S(2)}, u32[]{:S(2)}) collective-permute-start(bf16[16,64,128]{2,1,0:T(8,128)(2,1)S(1)} %get-tuple-element.36), channel_id=1, source_target_pairs={{0,3},{1,2},{2,1},{3,0},{4,7},{5,6},{6,5},{7,4},{8,11},{9,10},{10,... | collective-permute-start | bytes 786440 | tf_op jit(solution)/shard_map/ppermute | solution.py:203
  103.3 2.9 %shard_map.84.partial = f32[32,64,128]{2,1,0:T(8,128)S(1)} custom-call(f32[160]{0:T(256)S(1)} %reshape.37.scales, f32[32,64,128]{2,1,0:T(8,128)S(1)} %get-tuple-element.33.estimate, bf16[32,64,128]{2,1,0:T(8,128)(2,1)S(1)} %bitcast.26, bf16[32,64,128]{2,1,0:T(8,128)(2,1)S(1)} %get-tuple-element.34.vector, ...), custom_call_target="tpu_custom_call", output_to_operand_aliasing={{}: (1, {})} | custom-call | tf_op jit(solution)/shard_map/pallas_call | solution.py:205
  106.3 0.0 copy-start.4
  106.3 0.0 collective-permute-done.12.z_inner
  106.3 7.4 %collective-permute-done.13.z_outer = bf16[16,64,128]{2,1,0:T(8,128)(2,1)S(1)} collective-permute-done((bf16[16,64,128]{2,1,0:T(8,128)(2,1)S(1)}, bf16[16,64,128]{2,1,0:T(8,128)(2,1)S(1)}, u32[]{:S(2)}, u32[]{:S(2)}) %collective-permute-start.13) | collective-permute-done | bytes 262176 | tf_op jit(solution)/shard_map/ppermute | solution.py:203
  113.7 0.9 shard_map.85.partial
  114.6 0.0 collective-permute-done.14.inner
  114.6 0.0 collective-permute-done.15.outer
  114.6 0.0 collective-permute-done.17.relayed
  114.6 0.0 copy-done.4
  114.6 0.0 copy-done.5
  114.6 2.2 %shard_map.86 = (bf16[32,64,128]{2,1,0:T(8,128)(2,1)}, f32[8,64,128]{2,1,0:T(8,128)S(1)}, bf16[8,64,128]{2,1,0:T(8,128)(2,1)S(1)}) custom-call(s32[4]{0:T(128)S(1)} %pad_add_fusion.role, f32[160]{0:T(256)S(1)} %reshape.37.scales, s32[1,2,4,4]{3,2,1,0:T(4,128)S(1)} %copy-done.5, f32[32,64,128]{2,1,0:T(8,128)S(1)} %shard_map.85.partial, ...), custom_call_target="tpu_custom_call" | custom-call | tf_op jit(solution)/shard_map/pallas_call | solution.py:236
  116.8 2.0 %collective-permute-start.18 = (bf16[8,64,128]{2,1,0:T(8,128)(2,1)S(1)}, bf16[8,64,128]{2,1,0:T(8,128)(2,1)S(1)}, u32[]{:S(2)}, u32[]{:S(2)}) collective-permute-start(bf16[8,64,128]{2,1,0:T(8,128)(2,1)S(1)} %get-tuple-element.41), channel_id=1, source_target_pairs={{0,1},{1,0},{2,3},{3,2},{4,5},{5,4},{6,7},{7,6},{8,9},{9,8},{10,11... | collective-permute-start | bytes 393224 | tf_op jit(solution)/shard_map/ppermute | solution.py:244
  118.8 1.2 collective-permute-done.18.came
  120.0 0.6 shard_map.87
  120.6 1.9 %collective-permute-start.19 = (bf16[4,64,128]{2,1,0:T(8,128)(2,1)S(1)}, bf16[4,64,128]{2,1,0:T(8,128)(2,1)S(1)}, u32[]{:S(2)}, u32[]{:S(2)}) collective-permute-start(bf16[4,64,128]{2,1,0:T(8,128)(2,1)S(1)} %get-tuple-element.43), channel_id=1, source_target_pairs={{0,2},{1,3},{2,0},{3,1},{4,6},{5,7},{6,4},{7,5},{8,10},{9,11},{10,... | collective-permute-start | bytes 196616 | tf_op jit(solution)/shard_map/ppermute | solution.py:252
  122.5 4.2 %collective-permute-done.19 = bf16[4,64,128]{2,1,0:T(8,128)(2,1)S(1)} collective-permute-done((bf16[4,64,128]{2,1,0:T(8,128)(2,1)S(1)}, bf16[4,64,128]{2,1,0:T(8,128)(2,1)S(1)}, u32[]{:S(2)}, u32[]{:S(2)}) %collective-permute-start.19) | collective-permute-done | bytes 65568 | tf_op jit(solution)/shard_map/ppermute | solution.py:252
  126.8 0.7 add_bitcast_fusion
  (4 shorter events, 0.0 us)
Async XLA Ops:
  0.7 0.7 copy-start.6
  1.5 1.2 copy-start
  2.8 1.0 copy-start.2
  3.8 28.2 %copy-start.1 = (bf16[1,2,4,4,64,256]{5,4,3,2,1,0:T(8,128)(2,1)S(1)}, bf16[1,2,4,4,64,256]{5,4,3,2,1,0:T(8,128)(2,1)}, u32[]{:S(2)}) copy-start(bf16[1,2,4,4,64,256]{5,4,3,2,1,0:T(8,128)(2,1)} %param.8) | copy-start | bytes 3145732
  3.8 28.2 %copy-start.3 = (bf16[1,2,4,4,64,64]{5,4,3,2,1,0:T(8,128)(2,1)S(1)}, bf16[1,2,4,4,64,64]{5,4,3,2,1,0:T(8,128)(2,1)}, u32[]{:S(2)}) copy-start(bf16[1,2,4,4,64,64]{5,4,3,2,1,0:T(8,128)(2,1)} %param.7) | copy-start | bytes 786436
  5.7 13.9 %collective-permute-start.4 = (bf16[32,64,128]{2,1,0:T(8,128)(2,1)S(1)}, bf16[32,64,128]{2,1,0:T(8,128)(2,1)S(1)}, u32[]{:S(2)}, u32[]{:S(2)}) collective-permute-start(bf16[32,64,128]{2,1,0:T(8,128)(2,1)S(1)} %get-tuple-element.26), channel_id=1, source_target_pairs={{1,97},{3,31},{125,29},{127,99},{129,225},{131,159},{253,157},{255... | collective-permute-start | bytes 1572872 | tf_op jit(solution)/shard_map/ppermute | solution.py:200
  6.4 35.5 %collective-permute-start.3 = (bf16[32,64,128]{2,1,0:T(8,128)(2,1)S(1)}, bf16[32,64,128]{2,1,0:T(8,128)(2,1)S(1)}, u32[]{:S(2)}, u32[]{:S(2)}) collective-permute-start(bf16[32,64,128]{2,1,0:T(8,128)(2,1)S(1)} %get-tuple-element.26), channel_id=1, source_target_pairs={{0,508},{2,510},{4,8},{5,9},{6,10},{7,11},{8,4},{9,5},{10,6},{11,7... | collective-permute-start | bytes 1572872 | tf_op jit(solution)/shard_map/ppermute | solution.py:201
  17.6 24.2 %collective-permute-start.2 = (bf16[32,64,128]{2,1,0:T(8,128)(2,1)S(1)}, bf16[32,64,128]{2,1,0:T(8,128)(2,1)S(1)}, u32[]{:S(2)}, u32[]{:S(2)}) collective-permute-start(bf16[32,64,128]{2,1,0:T(8,128)(2,1)S(1)} %get-tuple-element.25), channel_id=1, source_target_pairs={{0,4},{1,5},{2,6},{3,7},{4,0},{5,1},{6,2},{7,3},{8,12},{9,13},{10,... | collective-permute-start | bytes 1572872 | tf_op jit(solution)/shard_map/ppermute | solution.py:202
  19.5 22.3 %collective-permute-start.5 = (bf16[32,64,128]{2,1,0:T(8,128)(2,1)S(1)}, bf16[32,64,128]{2,1,0:T(8,128)(2,1)S(1)}, u32[]{:S(2)}, u32[]{:S(2)}) collective-permute-start(bf16[32,64,128]{2,1,0:T(8,128)(2,1)S(1)} %collective-permute-done.4), channel_id=1, source_target_pairs={{97,509},{31,511},{29,129},{99,131},{225,125},{159,127},{157,257},... | collective-permute-start | bytes 1572872 | tf_op jit(solution)/shard_map/ppermute | solution.py:213
  20.2 14.7 %collective-permute-start = (bf16[16,64,128]{2,1,0:T(8,128)(2,1)S(1)}, bf16[16,64,128]{2,1,0:T(8,128)(2,1)S(1)}, u32[]{:S(2)}, u32[]{:S(2)}) collective-permute-start(bf16[16,64,128]{2,1,0:T(8,128)(2,1)S(1)} %get-tuple-element.23), channel_id=1, source_target_pairs={{0,1},{1,0},{2,3},{3,2},{4,5},{5,4},{6,7},{7,6},{8,9},{9,8},{10,11... | collective-permute-start | bytes 786440 | tf_op jit(solution)/shard_map/ppermute | solution.py:204
  28.3 12.6 %collective-permute-start.1 = (bf16[16,64,128]{2,1,0:T(8,128)(2,1)S(1)}, bf16[16,64,128]{2,1,0:T(8,128)(2,1)S(1)}, u32[]{:S(2)}, u32[]{:S(2)}) collective-permute-start(bf16[16,64,128]{2,1,0:T(8,128)(2,1)S(1)} %get-tuple-element.24), channel_id=1, source_target_pairs={{0,3},{1,2},{2,1},{3,0},{4,7},{5,6},{6,5},{7,4},{8,11},{9,10},{10,... | collective-permute-start | bytes 786440 | tf_op jit(solution)/shard_map/ppermute | solution.py:203
  44.5 4.6 %collective-permute-start.10 = (bf16[32,64,128]{2,1,0:T(8,128)(2,1)S(1)}, bf16[32,64,128]{2,1,0:T(8,128)(2,1)S(1)}, u32[]{:S(2)}, u32[]{:S(2)}) collective-permute-start(bf16[32,64,128]{2,1,0:T(8,128)(2,1)S(1)} %get-tuple-element.32), channel_id=1, source_target_pairs={{1,97},{3,31},{125,29},{127,99},{129,225},{131,159},{253,157},{255... | collective-permute-start | bytes 1572872 | tf_op jit(solution)/shard_map/ppermute | solution.py:200
  45.2 33.0 %collective-permute-start.9 = (bf16[32,64,128]{2,1,0:T(8,128)(2,1)S(1)}, bf16[32,64,128]{2,1,0:T(8,128)(2,1)S(1)}, u32[]{:S(2)}, u32[]{:S(2)}) collective-permute-start(bf16[32,64,128]{2,1,0:T(8,128)(2,1)S(1)} %get-tuple-element.32), channel_id=1, source_target_pairs={{0,508},{2,510},{4,8},{5,9},{6,10},{7,11},{8,4},{9,5},{10,6},{11,7... | collective-permute-start | bytes 1572872 | tf_op jit(solution)/shard_map/ppermute | solution.py:201
  47.1 31.1 %collective-permute-start.8 = (bf16[32,64,128]{2,1,0:T(8,128)(2,1)S(1)}, bf16[32,64,128]{2,1,0:T(8,128)(2,1)S(1)}, u32[]{:S(2)}, u32[]{:S(2)}) collective-permute-start(bf16[32,64,128]{2,1,0:T(8,128)(2,1)S(1)} %get-tuple-element.31), channel_id=1, source_target_pairs={{0,4},{1,5},{2,6},{3,7},{4,0},{5,1},{6,2},{7,3},{8,12},{9,13},{10,... | collective-permute-start | bytes 1572872 | tf_op jit(solution)/shard_map/ppermute | solution.py:202
  49.0 29.2 %collective-permute-start.11 = (bf16[32,64,128]{2,1,0:T(8,128)(2,1)S(1)}, bf16[32,64,128]{2,1,0:T(8,128)(2,1)S(1)}, u32[]{:S(2)}, u32[]{:S(2)}) collective-permute-start(bf16[32,64,128]{2,1,0:T(8,128)(2,1)S(1)} %collective-permute-done.10), channel_id=1, source_target_pairs={{97,509},{31,511},{29,129},{99,131},{225,125},{159,127},{157,257},... | collective-permute-start | bytes 1572872 | tf_op jit(solution)/shard_map/ppermute | solution.py:213
  49.7 20.0 %collective-permute-start.6 = (bf16[16,64,128]{2,1,0:T(8,128)(2,1)S(1)}, bf16[16,64,128]{2,1,0:T(8,128)(2,1)S(1)}, u32[]{:S(2)}, u32[]{:S(2)}) collective-permute-start(bf16[16,64,128]{2,1,0:T(8,128)(2,1)S(1)} %get-tuple-element.29), channel_id=1, source_target_pairs={{0,1},{1,0},{2,3},{3,2},{4,5},{5,4},{6,7},{7,6},{8,9},{9,8},{10,11... | collective-permute-start | bytes 786440 | tf_op jit(solution)/shard_map/ppermute | solution.py:204
  64.9 12.4 %collective-permute-start.7 = (bf16[16,64,128]{2,1,0:T(8,128)(2,1)S(1)}, bf16[16,64,128]{2,1,0:T(8,128)(2,1)S(1)}, u32[]{:S(2)}, u32[]{:S(2)}) collective-permute-start(bf16[16,64,128]{2,1,0:T(8,128)(2,1)S(1)} %get-tuple-element.30), channel_id=1, source_target_pairs={{0,3},{1,2},{2,1},{3,0},{4,7},{5,6},{6,5},{7,4},{8,11},{9,10},{10,... | collective-permute-start | bytes 786440 | tf_op jit(solution)/shard_map/ppermute | solution.py:203
  81.0 4.6 %collective-permute-start.16 = (bf16[32,64,128]{2,1,0:T(8,128)(2,1)S(1)}, bf16[32,64,128]{2,1,0:T(8,128)(2,1)S(1)}, u32[]{:S(2)}, u32[]{:S(2)}) collective-permute-start(bf16[32,64,128]{2,1,0:T(8,128)(2,1)S(1)} %get-tuple-element.38), channel_id=1, source_target_pairs={{1,97},{3,31},{125,29},{127,99},{129,225},{131,159},{253,157},{255... | collective-permute-start | bytes 1572872 | tf_op jit(solution)/shard_map/ppermute | solution.py:200
  81.7 32.9 %collective-permute-start.15 = (bf16[32,64,128]{2,1,0:T(8,128)(2,1)S(1)}, bf16[32,64,128]{2,1,0:T(8,128)(2,1)S(1)}, u32[]{:S(2)}, u32[]{:S(2)}) collective-permute-start(bf16[32,64,128]{2,1,0:T(8,128)(2,1)S(1)} %get-tuple-element.38), channel_id=1, source_target_pairs={{0,508},{2,510},{4,8},{5,9},{6,10},{7,11},{8,4},{9,5},{10,6},{11,7... | collective-permute-start | bytes 1572872 | tf_op jit(solution)/shard_map/ppermute | solution.py:201
  83.6 30.9 %collective-permute-start.14 = (bf16[32,64,128]{2,1,0:T(8,128)(2,1)S(1)}, bf16[32,64,128]{2,1,0:T(8,128)(2,1)S(1)}, u32[]{:S(2)}, u32[]{:S(2)}) collective-permute-start(bf16[32,64,128]{2,1,0:T(8,128)(2,1)S(1)} %get-tuple-element.37), channel_id=1, source_target_pairs={{0,4},{1,5},{2,6},{3,7},{4,0},{5,1},{6,2},{7,3},{8,12},{9,13},{10,... | collective-permute-start | bytes 1572872 | tf_op jit(solution)/shard_map/ppermute | solution.py:202
  85.6 29.0 %collective-permute-start.17 = (bf16[32,64,128]{2,1,0:T(8,128)(2,1)S(1)}, bf16[32,64,128]{2,1,0:T(8,128)(2,1)S(1)}, u32[]{:S(2)}, u32[]{:S(2)}) collective-permute-start(bf16[32,64,128]{2,1,0:T(8,128)(2,1)S(1)} %collective-permute-done.16), channel_id=1, source_target_pairs={{97,509},{31,511},{29,129},{99,131},{225,125},{159,127},{157,257},... | collective-permute-start | bytes 1572872 | tf_op jit(solution)/shard_map/ppermute | solution.py:213
  86.3 20.0 %collective-permute-start.12 = (bf16[16,64,128]{2,1,0:T(8,128)(2,1)S(1)}, bf16[16,64,128]{2,1,0:T(8,128)(2,1)S(1)}, u32[]{:S(2)}, u32[]{:S(2)}) collective-permute-start(bf16[16,64,128]{2,1,0:T(8,128)(2,1)S(1)} %get-tuple-element.35), channel_id=1, source_target_pairs={{0,1},{1,0},{2,3},{3,2},{4,5},{5,4},{6,7},{7,6},{8,9},{9,8},{10,11... | collective-permute-start | bytes 786440 | tf_op jit(solution)/shard_map/ppermute | solution.py:204
  101.4 12.3 %collective-permute-start.13 = (bf16[16,64,128]{2,1,0:T(8,128)(2,1)S(1)}, bf16[16,64,128]{2,1,0:T(8,128)(2,1)S(1)}, u32[]{:S(2)}, u32[]{:S(2)}) collective-permute-start(bf16[16,64,128]{2,1,0:T(8,128)(2,1)S(1)} %get-tuple-element.36), channel_id=1, source_target_pairs={{0,3},{1,2},{2,1},{3,0},{4,7},{5,6},{6,5},{7,4},{8,11},{9,10},{10,... | collective-permute-start | bytes 786440 | tf_op jit(solution)/shard_map/ppermute | solution.py:203
  106.3 8.4 %copy-start.4 = (bf16[1,2,4,4,64,64]{5,4,3,2,1,0:T(8,128)(2,1)S(1)}, bf16[1,2,4,4,64,64]{5,4,3,2,1,0:T(8,128)(2,1)}, u32[]{:S(2)}) copy-start(bf16[1,2,4,4,64,64]{5,4,3,2,1,0:T(8,128)(2,1)} %param.11) | copy-start | bytes 786436
  113.7 0.9 copy-start.5
  116.8 3.2 %collective-permute-start.18 = (bf16[8,64,128]{2,1,0:T(8,128)(2,1)S(1)}, bf16[8,64,128]{2,1,0:T(8,128)(2,1)S(1)}, u32[]{:S(2)}, u32[]{:S(2)}) collective-permute-start(bf16[8,64,128]{2,1,0:T(8,128)(2,1)S(1)} %get-tuple-element.41), channel_id=1, source_target_pairs={{0,1},{1,0},{2,3},{3,2},{4,5},{5,4},{6,7},{7,6},{8,9},{9,8},{10,11... | collective-permute-start | bytes 393224 | tf_op jit(solution)/shard_map/ppermute | solution.py:244
  120.6 6.2 %collective-permute-start.19 = (bf16[4,64,128]{2,1,0:T(8,128)(2,1)S(1)}, bf16[4,64,128]{2,1,0:T(8,128)(2,1)S(1)}, u32[]{:S(2)}, u32[]{:S(2)}) collective-permute-start(bf16[4,64,128]{2,1,0:T(8,128)(2,1)S(1)} %get-tuple-element.43), channel_id=1, source_target_pairs={{0,2},{1,3},{2,0},{3,1},{4,6},{5,7},{6,4},{7,5},{8,10},{9,11},{10,... | collective-permute-start | bytes 196616 | tf_op jit(solution)/shard_map/ppermute | solution.py:252
